TPU v7x, 32 devices: a whole 2x2x4 slice. The times are simulated.
32 devices in a mesh: groups: 2 (over x), dp: 4 (over z), tensor: 4 (over y, core).
Axes of the slice: x: 2, y: 2, z: 4, core: 2. Of those that a mesh axis runs over, the one named last changes fastest.
Arguments:
- patches: float32 [16, 256, 6144], P(('groups', 'dp'), None, 'tensor'), parts along dimension 0, may hold values from -60 to 60
- counts: int32 [16], P(('groups', 'dp')), parts along dimension 0, may hold values from 1 to 63, as said below
- ranking: int32 [16, 256], P(('groups', 'dp')), parts along dimension 0, may hold values from 0 to 255, each once within a row
- norm_gain: float32 [6144], P('tensor'), may hold values from 0.1 to 1.9
- expand_weight: bfloat16 [24576, 6144], P(('dp', 'tensor')), may hold values from -0.078125 to 0.078125
- expand_bias: bfloat16 [24576], P(('dp', 'tensor')), may hold values from -4 to 4
- reduce_weight: bfloat16 [24576, 6144], P(('dp', 'tensor')), may hold values from -0.078125 to 0.078125
- reduce_bias: float32 [6144], P('tensor'), may hold values from -4 to 4
Outputs:
- updated: float32 [16, 256, 6144], P(('groups', 'dp'), None, 'tensor'), parts along dimension 0
There are 2 independent parts, one for each index of `groups`. A program takes and returns all parts, laid end to end along the dimension named above; an argument that names none is the same for every part. Nothing has to cross between parts.
Inputs may be any that keep to these rules, and one draw needn't show every extreme that they name: The counts of the 2 images of one index of dp (images b * 2 to (b + 1) * 2 - 1) sum to at most 64; in every draw one such group sums to exactly 64, and some image holds exactly 63.
All inputs are finite; a program needn't handle non-finite values.
Results may differ from a plain program's by a relative error of at most 0.00061.
Values may be sent and summed in bfloat16 or wider, within the bound.
No kernel may reach another device: no remote copies, remote signals or barrier semaphores. Data moves between devices by JAX's collectives and lax.ppermute only.
A program may use at most 128 MiB of HBM per device.

v0:
```python
import jax
import jax.numpy as jnp
from jax import lax
from jax.sharding import PartitionSpec as P

D = 6144
CAP = 64


def body(
    patches, counts, ranking, norm_gain, expand_weight, expand_bias, reduce_weight, reduce_bias
):
    images, patch_len, width_local = patches.shape
    starts = jnp.cumsum(counts) - counts
    column = jnp.arange(CAP, dtype=jnp.int32)
    valid = column[None, :] < counts[:, None]
    target = jnp.where(valid, starts[:, None] + column[None, :], CAP).reshape(-1)
    source = (jnp.arange(images, dtype=jnp.int32)[:, None] * patch_len + ranking[:, :CAP]).reshape(
        -1
    )
    slot_source = jnp.zeros((CAP,), jnp.int32).at[target].set(source, mode="drop")
    slot_live = jnp.zeros((CAP,), jnp.float32).at[target].set(1.0, mode="drop")
    flat = patches.reshape(images * patch_len, width_local)
    rows = flat[slot_source]
    first, second = lax.psum((jnp.sum(rows, axis=1), jnp.sum(rows * rows, axis=1)), "tensor")
    mean = first[:, None] / D
    var = second[:, None] / D - mean * mean
    normed = ((rows - mean) * lax.rsqrt(var + 1e-06) * norm_gain).astype(jnp.bfloat16)
    full_rows = lax.all_gather(normed, "tensor", axis=1, tiled=True)
    pre = lax.dot_general(
        lax.all_gather(full_rows, "dp", axis=0, tiled=True),
        expand_weight,
        (((1,), (1,)), ((), ())),
        preferred_element_type=jnp.float32,
    )
    hidden = jax.nn.gelu(pre + expand_bias.astype(jnp.float32), approximate=True).astype(
        jnp.bfloat16
    )
    partial_value = jnp.dot(hidden, reduce_weight, preferred_element_type=jnp.float32)
    by_feature = lax.psum_scatter(partial_value, "tensor", scatter_dimension=1, tiled=True)
    branch = lax.psum_scatter(by_feature, "dp", scatter_dimension=0, tiled=True)
    update = slot_live[:, None] * (branch + reduce_bias)
    result = flat.at[slot_source].add(update)
    return result.reshape(images, patch_len, width_local)


def solution(mesh):
    placed = (
        P(("groups", "dp"), None, "tensor"),
        P(("groups", "dp")),
        P(("groups", "dp"), None),
        P("tensor"),
        P(("dp", "tensor"), None),
        P(("dp", "tensor")),
        P(("dp", "tensor"), None),
        P("tensor"),
    )
    return jax.shard_map(
        body,
        mesh=mesh,
        in_specs=placed,
        out_specs=P(("groups", "dp"), None, "tensor"),
        check_vma=False,
    )
```

profile of v0, /device:TPU:0, one launch (start us, length us, event | category | flops | bytes accessed | tf_op | source)
XLA Modules:
  0.0 221.0 jit_solution(17634967251671957816)
XLA Ops:
  6.5 0.0 copy-start.6
  6.5 0.0 copy-start.5
  6.5 0.0 all-gather.2.cloned.1.call-start
  6.5 1.9 copy.11
  8.5 0.0 copy-start.1
  8.5 0.0 copy-done.6
  8.5 0.2 reduce-window.9
  8.6 0.1 compare_select_fusion.2
  8.7 0.1 select_n.31
  8.8 0.0 copy-done.5
  8.8 0.0 copy-start.7
  8.8 0.1 slice_add_fusion
  8.9 0.1 reshape.126
  9.0 1.0 scatter_custom_fusion
  10.0 0.0 copy-start.4
  10.0 0.0 copy-done.7
  10.0 0.5 copy-done.4
  10.5 0.0 copy-start.3
  10.5 0.7 gather_fusion
  11.2 0.7 fusion.18
  11.9 9.0 %all-reduce = (f32[64]{0:T(128)}, f32[64]{0:T(128)}) all-reduce(f32[64]{0:T(128)} %get-tuple-element.6, f32[64]{0:T(128)S(1)} %get-tuple-element.5), channel_id=1, replica_groups=mesh['groups'=2,'dp'=4,'tensor'=4] {'tensor'}, use_global_device_ids=true, to_apply=%region_6.7 | all-reduce | flops 128 | bytes 1024 | tf_op jit(solution)/shard_map/psum | solution.py:25
  20.9 0.6 broadcast_multiply_fusion
  21.6 0.0 copy-done.1
  21.6 0.1 multiply_convert_fusion
  21.7 7.9 %all_gather.6 = bf16[64,6144]{1,0:T(8,128)(2,1)} all-gather(bf16[64,1536]{1,0:T(8,128)(2,1)S(1)} %multiply_convert_fusion), channel_id=1, replica_groups=mesh['groups'=2,'dp'=4,'tensor'=4] {'tensor'}, dimensions={1}, use_global_device_ids=true | all-gather | bytes 983040 | tf_op jit(solution)/shard_map/all_gather | solution.py:29
  29.6 0.0 all-gather.2.cloned.1.call-update
  29.7 0.0 reduce-scatter.3.cloned.1.call-start
  29.7 0.0 copy-done.3
  29.7 65.0 %all-gather.2.cloned.1.call-done = bf16[256,6144]{1,0:T(8,128)(2,1)} async-done(((bf16[64,6144]{1,0:T(8,128)(2,1)}), bf16[256,6144]{1,0:T(8,128)(2,1)}) %all-gather.2.cloned.1.call-update) | async-done | bytes 3145744 | tf_op jit(solution)/shard_map/all_gather | solution.py:31
  94.7 20.2 %fusion.19 = f32[256,6144]{1,0:T(8,128)} fusion(bf16[1536,6144]{1,0:T(8,128)(2,1)} %param.14, bf16[256,6144]{1,0:T(8,128)(2,1)} %all-gather.2.cloned.1.call-done, bf16[1536,6144]{1,0:T(8,128)(2,1)} %param.12, f32[1536]{0:T(1024)S(1)} %convert_element_type.10), kind=kOutput, calls=%fused_computation.36 | convolution fusion | flops 9667608576 | bytes 47192064 | tf_op jit(solution)/shard_map/dot_general | solution.py:39
  114.9 0.0 copy-start.2
  114.9 0.0 reduce-scatter.3.cloned.1.call-update
  114.9 0.0 reduce-scatter.5.cloned.1.call-start
  115.0 57.1 %reduce-scatter.3.cloned.1.call-done = f32[256,1536]{1,0:T(8,128)} async-done(((f32[256,6144]{1,0:T(8,128)}), f32[256,1536]{1,0:T(8,128)}) %reduce-scatter.3.cloned.1.call-update) | async-done | bytes 1572880 | tf_op jit(solution)/shard_map/reduce_scatter | solution.py:40
  172.1 0.0 reduce-scatter.5.cloned.1.call-update
  172.1 1.1 scatter_custom_fusion.1
  173.2 36.6 %reduce-scatter.5.cloned.1.call-done = f32[64,1536]{1,0:T(8,128)} async-done(((f32[256,1536]{1,0:T(8,128)}), f32[64,1536]{1,0:T(8,128)}) %reduce-scatter.5.cloned.1.call-update) | async-done | bytes 393232 | tf_op jit(solution)/shard_map/reduce_scatter | solution.py:41
  209.9 0.0 copy-done.2
  209.9 2.9 %scatter_custom_fusion.2 = f32[512,1536]{1,0:T(8,128)S(1)} fusion(f32[512,1536]{1,0:T(8,128)S(1)} %bitcast.22, s32[64]{0:T(128)} %copy-done.4, f32[64,1536]{1,0:T(8,128)} %reduce-scatter.5.cloned.1.call-done, f32[1536]{0:T(1024)S(1)} %copy-done.2, f32[64]{0:T(128)S(1)} %scatter_custom_fusion.1), kind=kCustom, calls=%fused_computation.14 | custom fusion | flops 294912 | bytes 3547648 | tf_op jit(solution)/shard_map/scatter-add | solution.py:43
  212.8 0.0 copy-start
  212.8 1.7 copy-done
  (7 shorter events, 0.0 us)
Async XLA Ops:
  6.5 1.9 copy-start.6
  6.5 2.3 %copy-start.5 = (s32[2,256]{1,0:T(2,128)S(1)}, s32[2,256]{1,0:T(2,128)}, u32[]{:S(2)}) copy-start(s32[2,256]{1,0:T(2,128)} %param.10) | copy-start | bytes 6148
  6.5 88.2 %all-gather.2.cloned.1.call-start = ((), (), s32[]{:S(2)}) async-start(), calls=%async_computation.2 | async-start | bytes 3932160 | tf_op jit(solution)/shard_map/all_gather | solution.py:31
  8.5 13.1 %copy-start.1 = (f32[1536]{0:T(1024)S(1)}, f32[1536]{0:T(1024)}, u32[]{:S(2)}) copy-start(f32[1536]{0:T(1024)} %param.11) | copy-start | bytes 18436
  8.8 1.2 copy-start.7
  10.0 0.5 copy-start.4
  10.5 19.2 %copy-start.3 = (bf16[1536]{0:T(1024)(128)(2,1)S(1)}, bf16[1536]{0:T(1024)(128)(2,1)}, u32[]{:S(2)}) copy-start(bf16[1536]{0:T(1024)(128)(2,1)} %param.13) | copy-start | bytes 9220
  29.7 142.4 %reduce-scatter.3.cloned.1.call-start = ((), (), s32[]{:S(2)}) async-start(), calls=%async_computation.3 | async-start | bytes 7864320 | tf_op jit(solution)/shard_map/reduce_scatter | solution.py:40
  114.9 95.0 %copy-start.2 = (f32[1536]{0:T(1024)S(1)}, f32[1536]{0:T(1024)}, u32[]{:S(2)}) copy-start(f32[1536]{0:T(1024)} %param.15) | copy-start | bytes 18436
  114.9 94.9 %reduce-scatter.5.cloned.1.call-start = ((), (), s32[]{:S(2)}) async-start(), calls=%async_computation.4 | async-start | bytes 1966080 | tf_op jit(solution)/shard_map/reduce_scatter | solution.py:41
  212.8 1.7 copy-start
Sparse Core Ops, SparseCore 0:
  29.8 64.9 all-gather.1
  115.1 57.0 reduce-scatter.2
  174.5 35.2 reduce-scatter.4
where the time goes:
time: 221 us
  waiting for transfers between devices  159 us (72%)
  matrix products  20.2 us (9%)
  blocking collectives  16.9 us (8%)
  between operations  13.2 us (6%)
  local copies, waits for them, and re-layouts  7.03 us (3%)
  other arithmetic  4.73 us (2%)
    all_gather x1, waiting for transfers between devices, body(): lax.all_gather(full_rows, 'dp', axis=0, tiled=True)  65 us
    reduce_scatter x1, waiting for transfers between devices, body(): lax.psum_scatter(partial_value, 'tensor', scatter_dimension=1, tiled=True)  57.1 us
    reduce_scatter x1, waiting for transfers between devices, body(): branch = lax.psum_scatter(by_feature, 'dp', scatter_dimension=0, tiled=True)  36.6 us
    dot_general x1, matrix products, body(): jnp.dot(hidden, reduce_weight, preferred_element_type=jnp.float32)  20.2 us
    psum x1, blocking collectives, body(): lax.psum((jnp.sum(rows, axis=1), jnp.sum(rows * rows, axis=1)), 'tensor')  9 us
    all_gather x1, blocking collectives, body(): full_rows = lax.all_gather(normed, 'tensor', axis=1, tiled=True)  7.93 us
  transfers between devices with their start and end apart: 3, of which 3 were waited for; matrix products, arithmetic and copies ran while one was open for 1% of the time, Pallas kernels for 0%

commit v1 on v0

v1 whole, which is shorter than its diff:
```python
import functools

import jax
import jax.numpy as jnp
from jax import lax
from jax.experimental import pallas as pl
from jax.experimental.pallas import tpu as pltpu
from jax.sharding import PartitionSpec as P

CAP = 64
LANES = 128
F32 = jnp.float32
BF16 = jnp.bfloat16
VMEM_LIMIT = 40 * 2**20

whole = pl.BlockSpec(memory_space=pltpu.VMEM)
scalars = pl.BlockSpec(memory_space=pltpu.SMEM)
anywhere = pl.BlockSpec(memory_space=pl.ANY)


def params():
    return pltpu.CompilerParams(vmem_limit_bytes=VMEM_LIMIT)


def slot_source(slot, counts_ref, ranking_ref):
    images = counts_ref.shape[0]
    image, start, end = jnp.int32(0), jnp.int32(0), jnp.int32(0)
    for i in range(images - 1):
        end = end + counts_ref[i]
        past = slot >= end
        image = jnp.where(past, i + 1, image)
        start = jnp.where(past, end, start)
    return image, ranking_ref[image, slot - start]


def gather_kernel(counts_ref, ranking_ref, patches_ref, rows_ref, stats_ref, sem):
    def fetch(slot, carry):
        image, patch = slot_source(slot, counts_ref, ranking_ref)
        pltpu.make_async_copy(
            patches_ref.at[image, pl.ds(patch, 1)], rows_ref.at[pl.ds(slot, 1)], sem
        ).start()
        return carry

    lax.fori_loop(0, CAP, fetch, 0)
    pltpu.make_async_copy(patches_ref.at[0, pl.ds(0, CAP)], rows_ref, sem).wait()
    rows = rows_ref[...]
    first = jnp.sum(rows, axis=1, keepdims=True)
    second = jnp.sum(rows * rows, axis=1, keepdims=True)
    lane = lax.broadcasted_iota(jnp.int32, (CAP, LANES), 1)
    stats_ref[...] = jnp.where(lane < LANES // 2, first, second)


def norm_kernel(width, rows_ref, gain_ref, *refs):
    *stats_refs, out_ref = refs
    stats = stats_refs[0][...]
    for ref in stats_refs[1:]:
        stats = stats + ref[...]
    mean = stats[:, :1] / width
    var = stats[:, LANES - 1 :] / width - mean * mean
    scale = lax.rsqrt(var + 1e-06)
    out_ref[...] = ((rows_ref[...] - mean) * scale * gain_ref[...]).astype(BF16)


def expand_kernel(chunks, groups, index_ref, weight_ref, bias_ref, *refs):
    inputs, (out_ref, rows_ref, total_ref) = refs[:-3], refs[-3:]
    chunk, piece = pl.program_id(0), pl.program_id(1)
    pieces = pl.num_programs(1)
    for c in range(chunks):

        @pl.when(jnp.logical_and(chunk == c, piece == 0))
        def _():
            for g in range(groups):
                block = inputs[c * groups + g]
                rows_ref[:, g * CAP : (g + 1) * CAP] = jnp.stack(
                    jnp.split(block[...], rows_ref.shape[0], axis=1)
                )

    part = lax.dot_general(
        rows_ref[piece], weight_ref[...], (((1,), (1,)), ((), ())), preferred_element_type=F32
    )
    start = jnp.logical_and(chunk == 0, piece == 0)

    @pl.when(start)
    def _():
        total_ref[...] = part

    @pl.when(jnp.logical_not(start))
    def _():
        total_ref[...] += part

    @pl.when(jnp.logical_and(chunk == chunks - 1, piece == pieces - 1))
    def _():
        pre = total_ref[...] + bias_ref[...].astype(F32)
        out_ref[...] = jax.nn.gelu(pre, approximate=True).astype(BF16)


def piece_of(width):
    return 512 if width % 512 == 0 else width


def expand(index, weight, bias, blocks, chunks, groups):
    hidden, width = weight.shape
    chunk_width = width // chunks
    piece = piece_of(chunk_width)
    pieces = chunk_width // piece
    rows = groups * CAP
    return pl.pallas_call(
        functools.partial(expand_kernel, chunks, groups),
        grid_spec=pltpu.PrefetchScalarGridSpec(
            num_scalar_prefetch=1,
            grid=(chunks, pieces),
            in_specs=[
                pl.BlockSpec((hidden, piece), lambda c, p, t: (0, (t[0] ^ c) * pieces + p)),
                whole,
            ]
            + [whole] * len(blocks),
            out_specs=whole,
            scratch_shapes=[
                pltpu.VMEM((pieces, rows, piece), BF16),
                pltpu.VMEM((rows, hidden), F32),
            ],
        ),
        out_shape=jax.ShapeDtypeStruct((rows, hidden), BF16),
        compiler_params=params(),
        cost_estimate=pl.CostEstimate(
            flops=2 * rows * hidden * width,
            bytes_accessed=2 * hidden * width,
            transcendentals=rows * hidden,
        ),
        name="expand",
    )(index, weight, bias, *blocks)


def reduce_kernel(groups, index_ref, hidden_ref, weight_ref, *refs):
    part = jnp.dot(hidden_ref[...], weight_ref[...], preferred_element_type=F32)
    if len(refs) > groups:
        part = part + jnp.concatenate([ref[...] for ref in refs[:groups]], axis=0).astype(F32)
    for g, ref in enumerate(refs[-groups:]):
        ref[...] = part[g * CAP : (g + 1) * CAP].astype(ref.dtype)


def reduce(index, hidden, weight, offset, chunks, groups, received, dtype):
    rows, depth = hidden.shape
    chunk_width = weight.shape[1] // chunks
    piece = piece_of(chunk_width)
    pieces = chunk_width // piece
    block = pl.BlockSpec((CAP, piece), lambda p, t: (0, p))
    return pl.pallas_call(
        functools.partial(reduce_kernel, groups),
        grid_spec=pltpu.PrefetchScalarGridSpec(
            num_scalar_prefetch=1,
            grid=(pieces,),
            in_specs=[
                whole,
                pl.BlockSpec((depth, piece), lambda p, t: (0, (t[0] ^ offset) * pieces + p)),
            ]
            + [block] * len(received),
            out_specs=[block] * groups,
        ),
        out_shape=[jax.ShapeDtypeStruct((CAP, chunk_width), dtype)] * groups,
        compiler_params=params(),
        cost_estimate=pl.CostEstimate(
            flops=2 * rows * depth * chunk_width,
            bytes_accessed=2 * depth * chunk_width,
            transcendentals=0,
        ),
        name="reduce",
    )(index, hidden, weight, *received)


def scatter_kernel(counts_ref, ranking_ref, rows_ref, bias_ref, patches_ref, own_ref, *refs):
    *received, out_ref, new_ref, sem = refs
    branch = own_ref[...]
    for ref in received:
        branch = branch + ref[...].astype(F32)
    live_slots = counts_ref[0]
    for i in range(1, counts_ref.shape[0]):
        live_slots = live_slots + counts_ref[i]
    slot_index = lax.broadcasted_iota(jnp.int32, branch.shape, 0)
    rows = rows_ref[...]
    new_ref[...] = jnp.where(slot_index < live_slots, rows + (branch + bias_ref[...]), rows)

    def put(slot, carry):
        image, patch = slot_source(slot, counts_ref, ranking_ref)
        pltpu.make_async_copy(
            new_ref.at[pl.ds(slot, 1)], out_ref.at[image, pl.ds(patch, 1)], sem
        ).start()
        return carry

    lax.fori_loop(0, CAP, put, 0)
    pltpu.make_async_copy(new_ref, out_ref.at[0, pl.ds(0, CAP)], sem).wait()


def masks(size):
    return [(2 << k) - 1 for k in reversed(range(size.bit_length() - 1))]


def hops(offset, size, unit, axis):
    path = []
    for mask in masks(size):
        if offset & ((mask + 1) // 2):
            path.append((axis, mask * unit))
            offset ^= mask
    return path


def routes(groups, columns):
    found = {}
    for z in range(groups):
        for y in range(columns):
            along, across = hops(z, groups, 1, "dp"), hops(y, columns, 2, "tensor")
            found[z, y] = tuple(across + along) if z == 1 else tuple(along + across)
    return found


def body(
    sizes, patches, counts, ranking, norm_gain, expand_weight, expand_bias, reduce_weight, reduce_bias
):
    groups, parts = sizes["dp"], sizes["tensor"]
    columns = parts // 2
    images, patch_len, width_local = patches.shape
    width = expand_weight.shape[1]
    index = lax.axis_index("tensor").astype(jnp.int32).reshape(1)

    def hop(array, axis, mask):
        return lax.ppermute(array, axis, [(i, i ^ mask) for i in range(sizes[axis])])

    rows, stats = pl.pallas_call(
        gather_kernel,
        in_specs=[scalars, scalars, anywhere],
        out_specs=[whole, whole],
        out_shape=[
            jax.ShapeDtypeStruct((CAP, width_local), F32),
            jax.ShapeDtypeStruct((CAP, LANES), F32),
        ],
        scratch_shapes=[pltpu.SemaphoreType.DMA],
        compiler_params=params(),
        name="gather",
    )(counts, ranking, patches)
    all_stats = [stats] + [hop(stats, "tensor", k) for k in reversed(range(1, parts))]
    normed = pl.pallas_call(
        functools.partial(norm_kernel, width),
        in_specs=[whole] * (2 + parts),
        out_specs=whole,
        out_shape=jax.ShapeDtypeStruct((CAP, width_local), BF16),
        compiler_params=params(),
        name="norm",
    )(rows, norm_gain.reshape(1, -1), *all_stats)

    path_of = routes(groups, columns)
    offset_of = {path: offset for offset, path in path_of.items()}
    by_length = sorted((p for p in offset_of if p), key=len)
    block = {(): normed}
    for path in by_length:
        block[path] = hop(block[path[:-1]], *path[-1])
    inputs = []
    for y in range(columns):
        mine = [block[path_of[z, y]] for z in range(groups)]
        inputs += mine + [hop(b, "tensor", 1) for b in mine]
    hidden = expand(
        index, expand_weight, expand_bias.reshape(1, -1), inputs, parts, groups
    )

    total = {}
    for y in reversed(range(columns)):
        given = reduce(index, hidden, reduce_weight, 2 * y + 1, parts, groups, [], BF16)
        received = [hop(g, "tensor", 1) for g in given]
        kept = reduce(index, hidden, reduce_weight, 2 * y, parts, groups, received, F32)
        for z in range(groups):
            total[path_of[z, y]] = kept[z]
    arrived = []
    for path in reversed(by_length):
        got = hop(total[path].astype(BF16), *path[-1])
        if path[:-1]:
            total[path[:-1]] = total[path[:-1]] + got.astype(F32)
        else:
            arrived.append(got)

    return pl.pallas_call(
        scatter_kernel,
        in_specs=[scalars, scalars, whole, whole, anywhere, whole] + [whole] * len(arrived),
        out_specs=anywhere,
        out_shape=jax.ShapeDtypeStruct(patches.shape, F32),
        scratch_shapes=[pltpu.VMEM((CAP, width_local), F32), pltpu.SemaphoreType.DMA],
        input_output_aliases={4: 0},
        compiler_params=params(),
        name="scatter",
    )(counts, ranking, rows, reduce_bias.reshape(1, -1), patches, total[()], *arrived)


def solution(mesh):
    placed = (
        P(("groups", "dp"), None, "tensor"),
        P(("groups", "dp")),
        P(("groups", "dp"), None),
        P("tensor"),
        P(("dp", "tensor"), None),
        P(("dp", "tensor")),
        P(("dp", "tensor"), None),
        P("tensor"),
    )
    return jax.shard_map(
        functools.partial(body, dict(mesh.shape)),
        mesh=mesh,
        in_specs=placed,
        out_specs=P(("groups", "dp"), None, "tensor"),
        check_vma=False,
    )
```

time: 221 us -> 103 us (0.47)
  waiting for transfers between devices: 159 us -> 28.8 us
  Pallas kernels: 0 us -> 36.8 us
  starting transfers between devices: 0.09 us -> 25.1 us
  matrix products: 20.2 us -> 0 us
  blocking collectives: 16.9 us -> 0 us
  between operations: 13.2 us -> 0.25 us
  local copies, waits for them, and re-layouts: 7.03 us -> 11.6 us
  other arithmetic: 4.73 us -> 0.24 us
    reduce_scatter x2 -> x0, waiting for transfers between devices: 93.7 us -> none  [the longest x1 57.1 us: body(): lax.psum_scatter(partial_value, 'tensor', scatter_dimension=1, tiled=True)]
    all_gather x1 -> x0, waiting for transfers between devices: 65 us -> none  [body(): lax.all_gather(full_rows, 'dp', axis=0, tiled=True)]
    pallas_call x0 -> x8, Pallas kernels: none -> 36.8 us  [the longest x4 16.3 us: reduce(): pl.pallas_call(functools.partial(reduce_kernel, groups), grid_spec=pltpu....]
    ppermute x0 -> x33, waiting for transfers between devices: none -> 28.8 us  [hop(): lax.ppermute(array, axis, [(i, i ^ mask) for i in range(sizes[axis])])]
    ppermute x0 -> x33, starting transfers between devices: none -> 25.1 us  [hop(): lax.ppermute(array, axis, [(i, i ^ mask) for i in range(sizes[axis])])]
    dot_general x1 -> x0, matrix products: 20.2 us -> none  [body(): jnp.dot(hidden, reduce_weight, preferred_element_type=jnp.float32)]
    psum x1 -> x0, blocking collectives: 9 us -> none  [body(): lax.psum((jnp.sum(rows, axis=1), jnp.sum(rows * rows, axis=1)), 'tensor')]
    all_gather x1 -> x0, blocking collectives: 7.93 us -> none  [body(): full_rows = lax.all_gather(normed, 'tensor', axis=1, tiled=True)]
  transfers between devices with their start and end apart: 3 -> 33, of which waited for: 3 -> 10; matrix products, arithmetic and copies ran while one was open for 1% -> 0% of each run, Pallas kernels for 0% -> 12%
where the time goes in v1:
time: 103 us
  Pallas kernels  36.8 us (36%)
  waiting for transfers between devices  28.8 us (28%)
  starting transfers between devices  25.1 us (24%)
  local copies, waits for them, and re-layouts  11.6 us (11%)
    ppermute x33, waiting for transfers between devices, hop(): lax.ppermute(array, axis, [(i, i ^ mask) for i in range(sizes[axis])])  28.8 us
    ppermute x33, starting transfers between devices, hop(): lax.ppermute(array, axis, [(i, i ^ mask) for i in range(sizes[axis])])  25.1 us
    pallas_call x4, Pallas kernels, reduce(): pl.pallas_call(functools.partial(reduce_kernel, groups), grid_spec=pltpu....  16.3 us
    pallas_call x1, Pallas kernels, expand(): pl.pallas_call(functools.partial(expand_kernel, chunks, groups), grid_spe...  15.7 us
    unnamed x37, local copies, waits for them, and re-layouts  11.6 us
    pallas_call x1, Pallas kernels, body(): pl.pallas_call(scatter_kernel, in_specs=[scalars, scalars, whole, whole,...  2.35 us
    pallas_call x1, Pallas kernels, body(): pl.pallas_call(gather_kernel, in_specs=[scalars, scalars, anywhere], out_...  2.31 us
  transfers between devices with their start and end apart: 33, of which 10 were waited for; matrix products, arithmetic and copies ran while one was open for 0% of the time, Pallas kernels for 12%

profile of v1, /device:TPU:0, one launch (start us, length us, event | category | flops | bytes accessed | tf_op | source)
XLA Modules:
  0.0 102.8 jit_solution(6222138334657578464)
XLA Ops:
  0.0 1.9 %copy.12.patches_ref = f32[2,256,1536]{2,1,0:T(8,128)S(1)} copy(f32[2,256,1536]{2,1,0:T(8,128)} %param.8) | data formatting | bytes 6291456
  1.9 2.3 %gather.1 = (f32[64,1536]{1,0:T(8,128)S(1)}, f32[64,128]{1,0:T(8,128)S(1)}) custom-call(s32[2]{0:T(128)S(1)} %copy-done.14, s32[2,256]{1,0:T(2,128)S(1)} %copy-done.13, f32[2,256,1536]{2,1,0:T(8,128)S(1)} %copy.12.patches_ref), custom_call_target="tpu_custom_call" | custom-call | tf_op jit(solution)/shard_map/gather/pallas_call | solution.py:228
  4.3 0.5 collective-permute-start.2
  4.8 2.6 %collective-permute-start.1 = (f32[64,128]{1,0:T(8,128)S(1)}, f32[64,128]{1,0:T(8,128)S(1)}, u32[]{:S(2)}, u32[]{:S(2)}) collective-permute-start(f32[64,128]{1,0:T(8,128)S(1)} %get-tuple-element.24.refs_0_), channel_id=1, source_target_pairs={{0,2},{1,3},{2,0},{3,1},{4,6},{5,7},{6,4},{7,5},{8,10},{9,11},{10,... | collective-permute-start | bytes 98312 | tf_op jit(solution)/shard_map/ppermute | solution.py:226
  7.5 1.9 %collective-permute-done.1.refs_2_ = f32[64,128]{1,0:T(8,128)S(1)} collective-permute-done((f32[64,128]{1,0:T(8,128)S(1)}, f32[64,128]{1,0:T(8,128)S(1)}, u32[]{:S(2)}, u32[]{:S(2)}) %collective-permute-start.1) | collective-permute-done | bytes 32800 | tf_op jit(solution)/shard_map/ppermute | solution.py:226
  9.4 1.4 %collective-permute-done.refs_1_ = f32[64,128]{1,0:T(8,128)S(1)} collective-permute-done((f32[64,128]{1,0:T(8,128)S(1)}, f32[64,128]{1,0:T(8,128)S(1)}, u32[]{:S(2)}, u32[]{:S(2)}) %collective-permute-start) | collective-permute-done | bytes 32800 | tf_op jit(solution)/shard_map/ppermute | solution.py:226
  10.9 3.7 %collective-permute-start.4 = (bf16[64,1536]{1,0:T(8,128)(2,1)S(1)}, bf16[64,1536]{1,0:T(8,128)(2,1)S(1)}, u32[]{:S(2)}, u32[]{:S(2)}) collective-permute-start(bf16[64,1536]{1,0:T(8,128)(2,1)S(1)} %norm.1.refs_0_), channel_id=1, source_target_pairs={{0,12},{4,8},{8,4},{12,0},{1,13},{5,9},{9,5},{13,1},{2,14},{6,10},... | collective-permute-start | bytes 589832 | tf_op jit(solution)/shard_map/ppermute | solution.py:226
  14.6 0.9 collective-permute-start.10
  15.5 0.7 copy-done.1
  16.1 4.4 %collective-permute-done.4.refs_3_ = bf16[64,1536]{1,0:T(8,128)(2,1)S(1)} collective-permute-done((bf16[64,1536]{1,0:T(8,128)(2,1)S(1)}, bf16[64,1536]{1,0:T(8,128)(2,1)S(1)}, u32[]{:S(2)}, u32[]{:S(2)}) %collective-permute-start.4) | collective-permute-done | bytes 196640 | tf_op jit(solution)/shard_map/ppermute | solution.py:226
  20.6 3.2 %collective-permute-start.5 = (bf16[64,1536]{1,0:T(8,128)(2,1)S(1)}, bf16[64,1536]{1,0:T(8,128)(2,1)}, u32[]{:S(2)}, u32[]{:S(2)}) collective-permute-start(bf16[64,1536]{1,0:T(8,128)(2,1)S(1)} %collective-permute-done.4.refs_3_), channel_id=1, source_target_pairs={{0,4},{4,0},{8,12},{12,8},{1,5},{5,1},{9,13},{13,9},{2,6},{6,2},{1... | collective-permute-start | bytes 589832 | tf_op jit(solution)/shard_map/ppermute | solution.py:226
  23.8 0.7 copy-done.5
  24.5 0.7 copy-done.7
  25.2 0.9 collective-permute-start.13
  26.2 0.7 copy-done.3
  26.9 2.8 %collective-permute-done.5.refs_2_ = bf16[64,1536]{1,0:T(8,128)(2,1)} collective-permute-done((bf16[64,1536]{1,0:T(8,128)(2,1)S(1)}, bf16[64,1536]{1,0:T(8,128)(2,1)}, u32[]{:S(2)}, u32[]{:S(2)}) %collective-permute-start.5) | collective-permute-done | bytes 196640 | tf_op jit(solution)/shard_map/ppermute | solution.py:226
  29.7 0.9 collective-permute-start.12
  30.5 0.7 copy-done.9
  31.2 1.5 %collective-permute-done.11.refs_9_ = bf16[64,1536]{1,0:T(8,128)(2,1)} collective-permute-done((bf16[64,1536]{1,0:T(8,128)(2,1)S(1)}, bf16[64,1536]{1,0:T(8,128)(2,1)}, u32[]{:S(2)}, u32[]{:S(2)}) %collective-permute-start.11) | collective-permute-done | bytes 196640 | tf_op jit(solution)/shard_map/ppermute | solution.py:226
  32.7 0.3 collective-permute-done.13.refs_11_
  33.2 0.7 copy-done.11
  34.2 2.6 %collective-permute-done.12.refs_10_ = bf16[64,1536]{1,0:T(8,128)(2,1)} collective-permute-done((bf16[64,1536]{1,0:T(8,128)(2,1)}, bf16[64,1536]{1,0:T(8,128)(2,1)}, u32[]{:S(2)}, u32[]{:S(2)}) %collective-permute-start.12) | collective-permute-done | bytes 196640 | tf_op jit(solution)/shard_map/ppermute | solution.py:226
  36.8 1.7 %collective-permute-done.16.refs_14_ = bf16[64,1536]{1,0:T(8,128)(2,1)} collective-permute-done((bf16[64,1536]{1,0:T(8,128)(2,1)}, bf16[64,1536]{1,0:T(8,128)(2,1)}, u32[]{:S(2)}, u32[]{:S(2)}) %collective-permute-start.16) | collective-permute-done | bytes 196640 | tf_op jit(solution)/shard_map/ppermute | solution.py:226
  38.5 0.9 copy-done.2
  39.5 0.9 copy-done.4
  40.4 0.9 copy-done.6
  41.3 0.9 copy-done.8
  42.3 0.9 copy-done.10
  43.2 0.9 copy-done.12
  44.1 15.7 %expand.1.hidden_ref = bf16[256,1536]{1,0:T(8,128)(2,1)S(1)} custom-call(s32[1]{0:T(128)} %bitcast.index_ref, bf16[1536,6144]{1,0:T(8,128)(2,1)} %weight_ref.5, bf16[1,1536]{1,0:T(2,128)(2,1)S(1)} %reshape.14.bias_ref, bf16[64,1536]{1,0:T(8,128)(2,1)S(1)} %copy-done.2, bf16[64,1536]{1,0:T(8,128)(2,1)} %collective-permute-done.3.refs_1_, ...), custom_call_target="tpu_custom_call" | custom-call | flops 4831838208 | bytes 18874368 | tf_op jit(solution)/shard_map/expand/pallas_call | solution.py:107
  59.9 4.0 %reduce.6 = (bf16[64,1536]{1,0:T(8,128)(2,1)S(1)}, bf16[64,1536]{1,0:T(8,128)(2,1)S(1)}, bf16[64,1536]{1,0:T(8,128)(2,1)S(1)}, bf16[64,1536]{1,0:T(8,128)(2,1)S(1)}) custom-call(s32[1]{0:T(128)} %bitcast.index_ref, bf16[256,1536]{1,0:T(8,128)(2,1)S(1)} %expand.1.hidden_ref, bf16[1536,6144]{1,0:T(8,128)(2,1)} %weight_ref.9), custom_call_target="tpu_custom_call" | custom-call | flops 1207959552 | bytes 4718592 | tf_op jit(solution)/shard_map/reduce/pallas_call | solution.py:148
  64.1 0.4 collective-permute-start.23
  64.6 0.4 collective-permute-start.25
  65.0 4.0 %reduce.4 = (bf16[64,1536]{1,0:T(8,128)(2,1)S(1)}, bf16[64,1536]{1,0:T(8,128)(2,1)S(1)}, bf16[64,1536]{1,0:T(8,128)(2,1)S(1)}, bf16[64,1536]{1,0:T(8,128)(2,1)S(1)}) custom-call(s32[1]{0:T(128)} %bitcast.index_ref, bf16[256,1536]{1,0:T(8,128)(2,1)S(1)} %expand.1.hidden_ref, bf16[1536,6144]{1,0:T(8,128)(2,1)} %weight_ref.9), custom_call_target="tpu_custom_call" | custom-call | flops 1207959552 | bytes 4718592 | tf_op jit(solution)/shard_map/reduce/pallas_call | solution.py:148
  69.2 0.4 collective-permute-start.19
  69.8 0.4 collective-permute-start.21
  70.1 4.1 %reduce.7 = (f32[64,1536]{1,0:T(8,128)S(1)}, f32[64,1536]{1,0:T(8,128)S(1)}, f32[64,1536]{1,0:T(8,128)S(1)}, f32[64,1536]{1,0:T(8,128)S(1)}) custom-call(s32[1]{0:T(128)} %bitcast.index_ref, bf16[256,1536]{1,0:T(8,128)(2,1)S(1)} %expand.1.hidden_ref, bf16[1536,6144]{1,0:T(8,128)(2,1)} %weight_ref.9, bf16[64,1536]{1,0:T(8,128)(2,1)S(1)} %collective-permute-done.22.refs_0_, ...), custom_call_target="tpu_custom_call" | custom-call | flops 1207959552 | bytes 4718592 | tf_op jit(solution)/shard_map/reduce/pallas_call | solution.py:148
  74.3 0.9 collective-permute-start.27
  75.2 1.8 %collective-permute-start.31 = (bf16[64,1536]{1,0:T(8,128)(2,1)S(1)}, bf16[64,1536]{1,0:T(8,128)(2,1)S(1)}, u32[]{:S(2)}, u32[]{:S(2)}) collective-permute-start(bf16[64,1536]{1,0:T(8,128)(2,1)S(1)} %convert_element_type.41), channel_id=1, source_target_pairs={{0,4},{4,0},{8,12},{12,8},{1,5},{5,1},{9,13},{13,9},{2,6},{6,2},{1... | collective-permute-start | bytes 589832 | tf_op jit(solution)/shard_map/ppermute | solution.py:226
  77.1 1.2 %collective-permute-start.26 = (bf16[64,1536]{1,0:T(8,128)(2,1)S(1)}, bf16[64,1536]{1,0:T(8,128)(2,1)S(1)}, u32[]{:S(2)}, u32[]{:S(2)}) collective-permute-start(bf16[64,1536]{1,0:T(8,128)(2,1)S(1)} %convert_element_type.33), channel_id=1, source_target_pairs={{0,2},{1,3},{2,0},{3,1},{4,6},{5,7},{6,4},{7,5},{8,10},{9,11},{10,... | collective-permute-start | bytes 589832 | tf_op jit(solution)/shard_map/ppermute | solution.py:226
  78.2 4.1 %reduce.5 = (f32[64,1536]{1,0:T(8,128)S(1)}, f32[64,1536]{1,0:T(8,128)S(1)}, f32[64,1536]{1,0:T(8,128)S(1)}, f32[64,1536]{1,0:T(8,128)S(1)}) custom-call(s32[1]{0:T(128)} %bitcast.index_ref, bf16[256,1536]{1,0:T(8,128)(2,1)S(1)} %expand.1.hidden_ref, bf16[1536,6144]{1,0:T(8,128)(2,1)} %weight_ref.9, bf16[64,1536]{1,0:T(8,128)(2,1)S(1)} %collective-permute-done.18.refs_0_, ...), custom_call_target="tpu_custom_call" | custom-call | flops 1207959552 | bytes 4718592 | tf_op jit(solution)/shard_map/reduce/pallas_call | solution.py:148
  82.4 0.4 collective-permute-start.30
  82.8 1.8 %collective-permute-start.28 = (bf16[64,1536]{1,0:T(8,128)(2,1)S(1)}, bf16[64,1536]{1,0:T(8,128)(2,1)S(1)}, u32[]{:S(2)}, u32[]{:S(2)}) collective-permute-start(bf16[64,1536]{1,0:T(8,128)(2,1)S(1)} %add_convert_fusion.2), channel_id=1, source_target_pairs={{0,4},{4,0},{8,12},{12,8},{1,5},{5,1},{9,13},{13,9},{2,6},{6,2},{1... | collective-permute-start | bytes 589832 | tf_op jit(solution)/shard_map/ppermute | solution.py:226
  84.6 0.9 collective-permute-start.32
  85.6 7.2 %collective-permute-done.28 = bf16[64,1536]{1,0:T(8,128)(2,1)S(1)} collective-permute-done((bf16[64,1536]{1,0:T(8,128)(2,1)S(1)}, bf16[64,1536]{1,0:T(8,128)(2,1)S(1)}, u32[]{:S(2)}, u32[]{:S(2)}) %collective-permute-start.28) | collective-permute-done | bytes 196640 | tf_op jit(solution)/shard_map/ppermute | solution.py:226
  92.8 2.5 %collective-permute-start.29 = (bf16[64,1536]{1,0:T(8,128)(2,1)S(1)}, bf16[64,1536]{1,0:T(8,128)(2,1)S(1)}, u32[]{:S(2)}, u32[]{:S(2)}) collective-permute-start(bf16[64,1536]{1,0:T(8,128)(2,1)S(1)} %add_convert_fusion.1), channel_id=1, source_target_pairs={{0,12},{4,8},{8,4},{12,0},{1,13},{5,9},{9,5},{13,1},{2,14},{6,10},... | collective-permute-start | bytes 589832 | tf_op jit(solution)/shard_map/ppermute | solution.py:226
  95.4 5.0 %collective-permute-done.29.refs_0_ = bf16[64,1536]{1,0:T(8,128)(2,1)S(1)} collective-permute-done((bf16[64,1536]{1,0:T(8,128)(2,1)S(1)}, bf16[64,1536]{1,0:T(8,128)(2,1)S(1)}, u32[]{:S(2)}, u32[]{:S(2)}) %collective-permute-start.29) | collective-permute-done | bytes 196640 | tf_op jit(solution)/shard_map/ppermute | solution.py:226
  100.4 2.4 %scatter.1 = f32[2,256,1536]{2,1,0:T(8,128)} custom-call(s32[2]{0:T(128)S(1)} %copy-done.14, s32[2,256]{1,0:T(2,128)S(1)} %copy-done.13, f32[64,1536]{1,0:T(8,128)S(1)} %get-tuple-element.23.rows_ref, f32[1,1536]{1,0:T(1,128)S(1)} %reshape.12.bias_ref, f32[2,256,1536]{2,1,0:T(8,128)} %copy-done, ...), custom_call_target="tpu_custom_call", output_to_operand_aliasing={{}: (4, {})} | custom-call | tf_op jit(solution)/shard_map/scatter/pallas_call | solution.py:279
  (73 shorter events, 2.1 us)
Async XLA Ops:
  0.0 1.9 %copy-start.14 = (s32[2]{0:T(128)S(1)}, s32[2]{0:T(128)}, u32[]{:S(2)}) copy-start(s32[2]{0:T(128)} %counts_ref.3) | copy-start | bytes 28
  0.0 1.9 %copy-start.13 = (s32[2,256]{1,0:T(2,128)S(1)}, s32[2,256]{1,0:T(2,128)}, u32[]{:S(2)}) copy-start(s32[2,256]{1,0:T(2,128)} %ranking_ref.3) | copy-start | bytes 6148
  1.9 57.9 %copy-start = (f32[2,256,1536]{2,1,0:T(8,128)}, f32[2,256,1536]{2,1,0:T(8,128)S(1)}, u32[]{:S(2)}) copy-start(f32[2,256,1536]{2,1,0:T(8,128)S(1)} %copy.12.patches_ref) | copy-start | bytes 9437188
  1.9 5.5 %copy-start.15 = (f32[1536]{0:T(1024)S(1)}, f32[1536]{0:T(1024)}, u32[]{:S(2)}) copy-start(f32[1536]{0:T(1024)} %param.11) | copy-start | bytes 18436
  1.9 34.8 %copy-start.17 = (bf16[1536]{0:T(1024)(128)(2,1)S(1)}, bf16[1536]{0:T(1024)(128)(2,1)}, u32[]{:S(2)}) copy-start(bf16[1536]{0:T(1024)(128)(2,1)} %param.13) | copy-start | bytes 9220
  4.3 3.2 %collective-permute-start.2 = (f32[64,128]{1,0:T(8,128)S(1)}, f32[64,128]{1,0:T(8,128)S(1)}, u32[]{:S(2)}, u32[]{:S(2)}) collective-permute-start(f32[64,128]{1,0:T(8,128)S(1)} %get-tuple-element.24.refs_0_), channel_id=1, source_target_pairs={{0,1},{1,0},{2,3},{3,2},{4,5},{5,4},{6,7},{7,6},{8,9},{9,8},{10,11... | collective-permute-start | bytes 98312 | tf_op jit(solution)/shard_map/ppermute | solution.py:226
  4.8 4.6 %collective-permute-start.1 = (f32[64,128]{1,0:T(8,128)S(1)}, f32[64,128]{1,0:T(8,128)S(1)}, u32[]{:S(2)}, u32[]{:S(2)}) collective-permute-start(f32[64,128]{1,0:T(8,128)S(1)} %get-tuple-element.24.refs_0_), channel_id=1, source_target_pairs={{0,2},{1,3},{2,0},{3,1},{4,6},{5,7},{6,4},{7,5},{8,10},{9,11},{10,... | collective-permute-start | bytes 98312 | tf_op jit(solution)/shard_map/ppermute | solution.py:226
  7.4 3.3 %collective-permute-start = (f32[64,128]{1,0:T(8,128)S(1)}, f32[64,128]{1,0:T(8,128)S(1)}, u32[]{:S(2)}, u32[]{:S(2)}) collective-permute-start(f32[64,128]{1,0:T(8,128)S(1)} %get-tuple-element.24.refs_0_), channel_id=1, source_target_pairs={{0,3},{1,2},{2,1},{3,0},{4,7},{5,6},{6,5},{7,4},{8,11},{9,10},{10,... | collective-permute-start | bytes 98312 | tf_op jit(solution)/shard_map/ppermute | solution.py:226
  10.9 9.6 %collective-permute-start.4 = (bf16[64,1536]{1,0:T(8,128)(2,1)S(1)}, bf16[64,1536]{1,0:T(8,128)(2,1)S(1)}, u32[]{:S(2)}, u32[]{:S(2)}) collective-permute-start(bf16[64,1536]{1,0:T(8,128)(2,1)S(1)} %norm.1.refs_0_), channel_id=1, source_target_pairs={{0,12},{4,8},{8,4},{12,0},{1,13},{5,9},{9,5},{13,1},{2,14},{6,10},... | collective-permute-start | bytes 589832 | tf_op jit(solution)/shard_map/ppermute | solution.py:226
  14.6 9.2 %collective-permute-start.10 = (bf16[64,1536]{1,0:T(8,128)(2,1)S(1)}, bf16[64,1536]{1,0:T(8,128)(2,1)S(1)}, u32[]{:S(2)}, u32[]{:S(2)}) collective-permute-start(bf16[64,1536]{1,0:T(8,128)(2,1)S(1)} %norm.1.refs_0_), channel_id=1, source_target_pairs={{0,2},{1,3},{2,0},{3,1},{4,6},{5,7},{6,4},{7,5},{8,10},{9,11},{10,... | collective-permute-start | bytes 589832 | tf_op jit(solution)/shard_map/ppermute | solution.py:226
  15.5 9.1 %collective-permute-start.6 = (bf16[64,1536]{1,0:T(8,128)(2,1)S(1)}, bf16[64,1536]{1,0:T(8,128)(2,1)S(1)}, u32[]{:S(2)}, u32[]{:S(2)}) collective-permute-start(bf16[64,1536]{1,0:T(8,128)(2,1)S(1)} %norm.1.refs_0_), channel_id=1, source_target_pairs={{0,1},{1,0},{2,3},{3,2},{4,5},{5,4},{6,7},{7,6},{8,9},{9,8},{10,11... | collective-permute-start | bytes 589832 | tf_op jit(solution)/shard_map/ppermute | solution.py:226
  15.5 10.6 %collective-permute-start.3 = (bf16[64,1536]{1,0:T(8,128)(2,1)S(1)}, bf16[64,1536]{1,0:T(8,128)(2,1)}, u32[]{:S(2)}, u32[]{:S(2)}) collective-permute-start(bf16[64,1536]{1,0:T(8,128)(2,1)S(1)} %norm.1.refs_0_), channel_id=1, source_target_pairs={{0,4},{4,0},{8,12},{12,8},{1,5},{5,1},{9,13},{13,9},{2,6},{6,2},{1... | collective-permute-start | bytes 589832 | tf_op jit(solution)/shard_map/ppermute | solution.py:226
  15.5 0.7 copy-start.1
  20.6 9.1 %collective-permute-start.5 = (bf16[64,1536]{1,0:T(8,128)(2,1)S(1)}, bf16[64,1536]{1,0:T(8,128)(2,1)}, u32[]{:S(2)}, u32[]{:S(2)}) collective-permute-start(bf16[64,1536]{1,0:T(8,128)(2,1)S(1)} %collective-permute-done.4.refs_3_), channel_id=1, source_target_pairs={{0,4},{4,0},{8,12},{12,8},{1,5},{5,1},{9,13},{13,9},{2,6},{6,2},{1... | collective-permute-start | bytes 589832 | tf_op jit(solution)/shard_map/ppermute | solution.py:226
  23.8 6.8 %collective-permute-start.14 = (bf16[64,1536]{1,0:T(8,128)(2,1)S(1)}, bf16[64,1536]{1,0:T(8,128)(2,1)S(1)}, u32[]{:S(2)}, u32[]{:S(2)}) collective-permute-start(bf16[64,1536]{1,0:T(8,128)(2,1)S(1)} %collective-permute-done.10.refs_8_), channel_id=1, source_target_pairs={{0,1},{1,0},{2,3},{3,2},{4,5},{5,4},{6,7},{7,6},{8,9},{9,8},{10,11... | collective-permute-start | bytes 589832 | tf_op jit(solution)/shard_map/ppermute | solution.py:226
  23.8 8.9 %collective-permute-start.11 = (bf16[64,1536]{1,0:T(8,128)(2,1)S(1)}, bf16[64,1536]{1,0:T(8,128)(2,1)}, u32[]{:S(2)}, u32[]{:S(2)}) collective-permute-start(bf16[64,1536]{1,0:T(8,128)(2,1)S(1)} %collective-permute-done.10.refs_8_), channel_id=1, source_target_pairs={{0,4},{4,0},{8,12},{12,8},{1,5},{5,1},{9,13},{13,9},{2,6},{6,2},{1... | collective-permute-start | bytes 589832 | tf_op jit(solution)/shard_map/ppermute | solution.py:226
  24.5 0.7 copy-start.7
  25.2 7.8 %collective-permute-start.13 = (bf16[64,1536]{1,0:T(8,128)(2,1)S(1)}, bf16[64,1536]{1,0:T(8,128)(2,1)}, u32[]{:S(2)}, u32[]{:S(2)}) collective-permute-start(bf16[64,1536]{1,0:T(8,128)(2,1)S(1)} %collective-permute-done.4.refs_3_), channel_id=1, source_target_pairs={{0,2},{1,3},{2,0},{3,1},{4,6},{5,7},{6,4},{7,5},{8,10},{9,11},{10,... | collective-permute-start | bytes 589832 | tf_op jit(solution)/shard_map/ppermute | solution.py:226
  26.1 7.1 %collective-permute-start.9 = (bf16[64,1536]{1,0:T(8,128)(2,1)S(1)}, bf16[64,1536]{1,0:T(8,128)(2,1)S(1)}, u32[]{:S(2)}, u32[]{:S(2)}) collective-permute-start(bf16[64,1536]{1,0:T(8,128)(2,1)S(1)} %collective-permute-done.4.refs_3_), channel_id=1, source_target_pairs={{0,1},{1,0},{2,3},{3,2},{4,5},{5,4},{6,7},{7,6},{8,9},{9,8},{10,11... | collective-permute-start | bytes 589832 | tf_op jit(solution)/shard_map/ppermute | solution.py:226
  26.2 0.7 copy-start.3
  29.7 7.1 %collective-permute-start.12 = (bf16[64,1536]{1,0:T(8,128)(2,1)}, bf16[64,1536]{1,0:T(8,128)(2,1)}, u32[]{:S(2)}, u32[]{:S(2)}) collective-permute-start(bf16[64,1536]{1,0:T(8,128)(2,1)} %collective-permute-done.5.refs_2_), channel_id=1, source_target_pairs={{0,2},{1,3},{2,0},{3,1},{4,6},{5,7},{6,4},{7,5},{8,10},{9,11},{10,... | collective-permute-start | bytes 589832 | tf_op jit(solution)/shard_map/ppermute | solution.py:226
  31.2 5.6 %collective-permute-start.7 = (bf16[64,1536]{1,0:T(8,128)(2,1)}, bf16[64,1536]{1,0:T(8,128)(2,1)}, u32[]{:S(2)}, u32[]{:S(2)}) collective-permute-start(bf16[64,1536]{1,0:T(8,128)(2,1)} %collective-permute-done.3.refs_1_), channel_id=1, source_target_pairs={{0,1},{1,0},{2,3},{3,2},{4,5},{5,4},{6,7},{7,6},{8,9},{9,8},{10,11... | collective-permute-start | bytes 589832 | tf_op jit(solution)/shard_map/ppermute | solution.py:226
  32.7 4.1 %collective-permute-start.8 = (bf16[64,1536]{1,0:T(8,128)(2,1)}, bf16[64,1536]{1,0:T(8,128)(2,1)}, u32[]{:S(2)}, u32[]{:S(2)}) collective-permute-start(bf16[64,1536]{1,0:T(8,128)(2,1)} %collective-permute-done.5.refs_2_), channel_id=1, source_target_pairs={{0,1},{1,0},{2,3},{3,2},{4,5},{5,4},{6,7},{7,6},{8,9},{9,8},{10,11... | collective-permute-start | bytes 589832 | tf_op jit(solution)/shard_map/ppermute | solution.py:226
  33.0 3.8 %collective-permute-start.15 = (bf16[64,1536]{1,0:T(8,128)(2,1)}, bf16[64,1536]{1,0:T(8,128)(2,1)}, u32[]{:S(2)}, u32[]{:S(2)}) collective-permute-start(bf16[64,1536]{1,0:T(8,128)(2,1)} %collective-permute-done.11.refs_9_), channel_id=1, source_target_pairs={{0,1},{1,0},{2,3},{3,2},{4,5},{5,4},{6,7},{7,6},{8,9},{9,8},{10,11... | collective-permute-start | bytes 589832 | tf_op jit(solution)/shard_map/ppermute | solution.py:226
  33.9 2.9 %collective-permute-start.17 = (bf16[64,1536]{1,0:T(8,128)(2,1)}, bf16[64,1536]{1,0:T(8,128)(2,1)}, u32[]{:S(2)}, u32[]{:S(2)}) collective-permute-start(bf16[64,1536]{1,0:T(8,128)(2,1)} %collective-permute-done.13.refs_11_), channel_id=1, source_target_pairs={{0,1},{1,0},{2,3},{3,2},{4,5},{5,4},{6,7},{7,6},{8,9},{9,8},{10,11... | collective-permute-start | bytes 589832 | tf_op jit(solution)/shard_map/ppermute | solution.py:226
  36.8 1.8 %collective-permute-start.16 = (bf16[64,1536]{1,0:T(8,128)(2,1)}, bf16[64,1536]{1,0:T(8,128)(2,1)}, u32[]{:S(2)}, u32[]{:S(2)}) collective-permute-start(bf16[64,1536]{1,0:T(8,128)(2,1)} %collective-permute-done.12.refs_10_), channel_id=1, source_target_pairs={{0,1},{1,0},{2,3},{3,2},{4,5},{5,4},{6,7},{7,6},{8,9},{9,8},{10,11... | collective-permute-start | bytes 589832 | tf_op jit(solution)/shard_map/ppermute | solution.py:226
  38.5 0.9 copy-start.2
  39.5 0.9 copy-start.4
  40.4 0.9 copy-start.6
  41.3 0.9 copy-start.8
  42.3 0.9 copy-start.10
  43.2 0.9 copy-start.12
  63.9 5.3 %collective-permute-start.22 = (bf16[64,1536]{1,0:T(8,128)(2,1)S(1)}, bf16[64,1536]{1,0:T(8,128)(2,1)S(1)}, u32[]{:S(2)}, u32[]{:S(2)}) collective-permute-start(bf16[64,1536]{1,0:T(8,128)(2,1)S(1)} %get-tuple-element.31), channel_id=1, source_target_pairs={{0,1},{1,0},{2,3},{3,2},{4,5},{5,4},{6,7},{7,6},{8,9},{9,8},{10,11... | collective-permute-start | bytes 589832 | tf_op jit(solution)/shard_map/ppermute | solution.py:226
  64.1 5.5 %collective-permute-start.23 = (bf16[64,1536]{1,0:T(8,128)(2,1)S(1)}, bf16[64,1536]{1,0:T(8,128)(2,1)S(1)}, u32[]{:S(2)}, u32[]{:S(2)}) collective-permute-start(bf16[64,1536]{1,0:T(8,128)(2,1)S(1)} %get-tuple-element.32), channel_id=1, source_target_pairs={{0,1},{1,0},{2,3},{3,2},{4,5},{5,4},{6,7},{7,6},{8,9},{9,8},{10,11... | collective-permute-start | bytes 589832 | tf_op jit(solution)/shard_map/ppermute | solution.py:226
  64.5 5.3 %collective-permute-start.24 = (bf16[64,1536]{1,0:T(8,128)(2,1)S(1)}, bf16[64,1536]{1,0:T(8,128)(2,1)S(1)}, u32[]{:S(2)}, u32[]{:S(2)}) collective-permute-start(bf16[64,1536]{1,0:T(8,128)(2,1)S(1)} %get-tuple-element.33), channel_id=1, source_target_pairs={{0,1},{1,0},{2,3},{3,2},{4,5},{5,4},{6,7},{7,6},{8,9},{9,8},{10,11... | collective-permute-start | bytes 589832 | tf_op jit(solution)/shard_map/ppermute | solution.py:226
  64.6 5.5 %collective-permute-start.25 = (bf16[64,1536]{1,0:T(8,128)(2,1)S(1)}, bf16[64,1536]{1,0:T(8,128)(2,1)S(1)}, u32[]{:S(2)}, u32[]{:S(2)}) collective-permute-start(bf16[64,1536]{1,0:T(8,128)(2,1)S(1)} %get-tuple-element.34), channel_id=1, source_target_pairs={{0,1},{1,0},{2,3},{3,2},{4,5},{5,4},{6,7},{7,6},{8,9},{9,8},{10,11... | collective-permute-start | bytes 589832 | tf_op jit(solution)/shard_map/ppermute | solution.py:226
  69.0 6.2 %collective-permute-start.18 = (bf16[64,1536]{1,0:T(8,128)(2,1)S(1)}, bf16[64,1536]{1,0:T(8,128)(2,1)S(1)}, u32[]{:S(2)}, u32[]{:S(2)}) collective-permute-start(bf16[64,1536]{1,0:T(8,128)(2,1)S(1)} %get-tuple-element.25), channel_id=1, source_target_pairs={{0,1},{1,0},{2,3},{3,2},{4,5},{5,4},{6,7},{7,6},{8,9},{9,8},{10,11... | collective-permute-start | bytes 589832 | tf_op jit(solution)/shard_map/ppermute | solution.py:226
  69.2 7.8 %collective-permute-start.19 = (bf16[64,1536]{1,0:T(8,128)(2,1)S(1)}, bf16[64,1536]{1,0:T(8,128)(2,1)S(1)}, u32[]{:S(2)}, u32[]{:S(2)}) collective-permute-start(bf16[64,1536]{1,0:T(8,128)(2,1)S(1)} %get-tuple-element.26), channel_id=1, source_target_pairs={{0,1},{1,0},{2,3},{3,2},{4,5},{5,4},{6,7},{7,6},{8,9},{9,8},{10,11... | collective-permute-start | bytes 589832 | tf_op jit(solution)/shard_map/ppermute | solution.py:226
  69.6 8.6 %collective-permute-start.20 = (bf16[64,1536]{1,0:T(8,128)(2,1)S(1)}, bf16[64,1536]{1,0:T(8,128)(2,1)S(1)}, u32[]{:S(2)}, u32[]{:S(2)}) collective-permute-start(bf16[64,1536]{1,0:T(8,128)(2,1)S(1)} %get-tuple-element.27), channel_id=1, source_target_pairs={{0,1},{1,0},{2,3},{3,2},{4,5},{5,4},{6,7},{7,6},{8,9},{9,8},{10,11... | collective-permute-start | bytes 589832 | tf_op jit(solution)/shard_map/ppermute | solution.py:226
  69.8 8.5 %collective-permute-start.21 = (bf16[64,1536]{1,0:T(8,128)(2,1)S(1)}, bf16[64,1536]{1,0:T(8,128)(2,1)S(1)}, u32[]{:S(2)}, u32[]{:S(2)}) collective-permute-start(bf16[64,1536]{1,0:T(8,128)(2,1)S(1)} %get-tuple-element.28), channel_id=1, source_target_pairs={{0,1},{1,0},{2,3},{3,2},{4,5},{5,4},{6,7},{7,6},{8,9},{9,8},{10,11... | collective-permute-start | bytes 589832 | tf_op jit(solution)/shard_map/ppermute | solution.py:226
  74.3 8.5 %collective-permute-start.27 = (bf16[64,1536]{1,0:T(8,128)(2,1)S(1)}, bf16[64,1536]{1,0:T(8,128)(2,1)S(1)}, u32[]{:S(2)}, u32[]{:S(2)}) collective-permute-start(bf16[64,1536]{1,0:T(8,128)(2,1)S(1)} %convert_element_type.35), channel_id=1, source_target_pairs={{0,2},{1,3},{2,0},{3,1},{4,6},{5,7},{6,4},{7,5},{8,10},{9,11},{10,... | collective-permute-start | bytes 589832 | tf_op jit(solution)/shard_map/ppermute | solution.py:226
  75.2 9.3 %collective-permute-start.31 = (bf16[64,1536]{1,0:T(8,128)(2,1)S(1)}, bf16[64,1536]{1,0:T(8,128)(2,1)S(1)}, u32[]{:S(2)}, u32[]{:S(2)}) collective-permute-start(bf16[64,1536]{1,0:T(8,128)(2,1)S(1)} %convert_element_type.41), channel_id=1, source_target_pairs={{0,4},{4,0},{8,12},{12,8},{1,5},{5,1},{9,13},{13,9},{2,6},{6,2},{1... | collective-permute-start | bytes 589832 | tf_op jit(solution)/shard_map/ppermute | solution.py:226
  77.1 8.5 %collective-permute-start.26 = (bf16[64,1536]{1,0:T(8,128)(2,1)S(1)}, bf16[64,1536]{1,0:T(8,128)(2,1)S(1)}, u32[]{:S(2)}, u32[]{:S(2)}) collective-permute-start(bf16[64,1536]{1,0:T(8,128)(2,1)S(1)} %convert_element_type.33), channel_id=1, source_target_pairs={{0,2},{1,3},{2,0},{3,1},{4,6},{5,7},{6,4},{7,5},{8,10},{9,11},{10,... | collective-permute-start | bytes 589832 | tf_op jit(solution)/shard_map/ppermute | solution.py:226
  82.3 13.0 %copy-start.16 = (f32[1536]{0:T(1024)S(1)}, f32[1536]{0:T(1024)}, u32[]{:S(2)}) copy-start(f32[1536]{0:T(1024)} %param.15) | copy-start | bytes 18436
  82.4 13.0 %collective-permute-start.30 = (bf16[64,1536]{1,0:T(8,128)(2,1)S(1)}, bf16[64,1536]{1,0:T(8,128)(2,1)S(1)}, u32[]{:S(2)}, u32[]{:S(2)}) collective-permute-start(bf16[64,1536]{1,0:T(8,128)(2,1)S(1)} %convert_element_type.40), channel_id=1, source_target_pairs={{0,4},{4,0},{8,12},{12,8},{1,5},{5,1},{9,13},{13,9},{2,6},{6,2},{1... | collective-permute-start | bytes 589832 | tf_op jit(solution)/shard_map/ppermute | solution.py:226
  82.8 10.0 %collective-permute-start.28 = (bf16[64,1536]{1,0:T(8,128)(2,1)S(1)}, bf16[64,1536]{1,0:T(8,128)(2,1)S(1)}, u32[]{:S(2)}, u32[]{:S(2)}) collective-permute-start(bf16[64,1536]{1,0:T(8,128)(2,1)S(1)} %add_convert_fusion.2), channel_id=1, source_target_pairs={{0,4},{4,0},{8,12},{12,8},{1,5},{5,1},{9,13},{13,9},{2,6},{6,2},{1... | collective-permute-start | bytes 589832 | tf_op jit(solution)/shard_map/ppermute | solution.py:226
  84.6 10.8 %collective-permute-start.32 = (bf16[64,1536]{1,0:T(8,128)(2,1)S(1)}, bf16[64,1536]{1,0:T(8,128)(2,1)S(1)}, u32[]{:S(2)}, u32[]{:S(2)}) collective-permute-start(bf16[64,1536]{1,0:T(8,128)(2,1)S(1)} %add_convert_fusion), channel_id=1, source_target_pairs={{0,2},{1,3},{2,0},{3,1},{4,6},{5,7},{6,4},{7,5},{8,10},{9,11},{10,... | collective-permute-start | bytes 589832 | tf_op jit(solution)/shard_map/ppermute | solution.py:226
  92.8 7.6 %collective-permute-start.29 = (bf16[64,1536]{1,0:T(8,128)(2,1)S(1)}, bf16[64,1536]{1,0:T(8,128)(2,1)S(1)}, u32[]{:S(2)}, u32[]{:S(2)}) collective-permute-start(bf16[64,1536]{1,0:T(8,128)(2,1)S(1)} %add_convert_fusion.1), channel_id=1, source_target_pairs={{0,12},{4,8},{8,4},{12,0},{1,13},{5,9},{9,5},{13,1},{2,14},{6,10},... | collective-permute-start | bytes 589832 | tf_op jit(solution)/shard_map/ppermute | solution.py:226
  (3 other events, 2.0 us)

commit v2 on v1

v2 whole, which is shorter than its diff:
```python
import functools

import jax
import jax.numpy as jnp
from jax import lax
from jax.experimental import pallas as pl
from jax.experimental.pallas import tpu as pltpu
from jax.sharding import PartitionSpec as P

CAP = 64
LANES = 128
F32 = jnp.float32
BF16 = jnp.bfloat16

whole = pl.BlockSpec(memory_space=pltpu.VMEM)
scalars = pl.BlockSpec(memory_space=pltpu.SMEM)
outside = pl.BlockSpec(memory_space=pltpu.HBM)


def params(mib=6):
    return pltpu.CompilerParams(vmem_limit_bytes=mib * 2**20)


def slot_source(slot, counts_ref, ranking_ref):
    images = counts_ref.shape[0]
    image, start, end = jnp.int32(0), jnp.int32(0), jnp.int32(0)
    for i in range(images - 1):
        end = end + counts_ref[i]
        past = slot >= end
        image = jnp.where(past, i + 1, image)
        start = jnp.where(past, end, start)
    return image, ranking_ref[image, slot - start]


def gather_kernel(counts_ref, ranking_ref, patches_ref, *refs):
    *_, rows_ref, stats_ref, sem = refs
    def fetch(slot, carry):
        image, patch = slot_source(slot, counts_ref, ranking_ref)
        pltpu.make_async_copy(
            patches_ref.at[image, pl.ds(patch, 1)], rows_ref.at[pl.ds(slot, 1)], sem
        ).start()
        return carry

    lax.fori_loop(0, CAP, fetch, 0)
    pltpu.make_async_copy(patches_ref.at[0, pl.ds(0, CAP)], rows_ref, sem).wait()
    rows = rows_ref[...]
    first = jnp.sum(rows, axis=1, keepdims=True)
    second = jnp.sum(rows * rows, axis=1, keepdims=True)
    lane = lax.broadcasted_iota(jnp.int32, (CAP, LANES), 1)
    stats_ref[...] = jnp.where(lane < LANES // 2, first, second)


def load_kernel(weight_ref, after_ref, *refs):
    *more, sems = refs
    if len(more) == 3:
        patches_ref, out_ref, copy_ref = more
    else:
        [out_ref] = more
    count = sems.shape[0] - 1
    share = weight_ref.shape[0] // count
    copies = [
        pltpu.make_async_copy(
            weight_ref.at[pl.ds(i * share, share)], out_ref.at[pl.ds(i * share, share)], sems.at[i]
        )
        for i in range(count)
    ]
    if len(more) == 3:
        copies.append(pltpu.make_async_copy(patches_ref, copy_ref, sems.at[count]))
    for copy in copies:
        copy.start()
    for copy in copies:
        copy.wait()


def load(weight, after, mib, patches=None):
    shapes = [pltpu.VMEM(weight.shape, weight.dtype)]
    size = 2 * weight.size * weight.dtype.itemsize
    args, specs = [weight, after], [whole]
    if patches is not None:
        args.append(patches)
        shapes.append(pltpu.HBM(patches.shape, patches.dtype))
        specs.append(outside)
    return pl.pallas_call(
        load_kernel,
        in_specs=[outside] * len(args),
        out_specs=specs,
        out_shape=shapes,
        scratch_shapes=[pltpu.SemaphoreType.DMA((5,))],
        compiler_params=params(mib),
        cost_estimate=pl.CostEstimate(flops=0, bytes_accessed=size, transcendentals=0),
        name="load",
    )(*args)


def pass_kernel(block_ref, after_ref, out_ref):
    pass


def pass_on(block, after):
    return pl.pallas_call(
        pass_kernel,
        in_specs=[outside, whole],
        out_specs=outside,
        out_shape=jax.ShapeDtypeStruct(block.shape, block.dtype),
        input_output_aliases={0: 0},
        compiler_params=params(1),
        name="pass_on",
    )(block, after)


def norm_kernel(width, rows_ref, gain_ref, after_ref, *refs):
    *stats_refs, out_ref = refs
    stats = stats_refs[0][...]
    for ref in stats_refs[1:]:
        stats = stats + ref[...]
    mean = stats[:, :1] / width
    var = stats[:, LANES - 1 :] / width - mean * mean
    scale = lax.rsqrt(var + 1e-06)
    out_ref[...] = ((rows_ref[...] - mean) * scale * gain_ref[...]).astype(BF16)


def expand_kernel(first, chunks, groups, last, weight_ref, *refs):
    refs = list(refs)
    total_in = refs.pop(0) if first else None
    bias_ref = refs.pop(0) if last else None
    count = chunks * groups
    inputs, refs = refs[:count], refs[count:]
    out_ref = refs.pop(0)
    rows_ref, sems = refs[:2]
    refs = refs[2:]
    total_ref = refs.pop(0) if last else out_ref
    hidden = weight_ref.shape[0]
    width = rows_ref.shape[2]
    tile = piece_of(hidden)

    def fetch(c, g):
        return pltpu.make_async_copy(
            inputs[c * groups + g], rows_ref.at[c, pl.ds(g * CAP, CAP)], sems.at[c, g]
        )

    for c in range(chunks):
        for g in range(groups):
            fetch(c, g).start()
    for c in range(chunks):
        for g in range(groups):
            fetch(c, g).wait()
        column = pl.multiple_of((lax.axis_index("tensor") ^ (first + c)) * width, width)
        for f in range(hidden // tile):
            part = lax.dot_general(
                rows_ref[c],
                weight_ref[f * tile : (f + 1) * tile, pl.ds(column, width)],
                (((1,), (1,)), ((), ())),
                preferred_element_type=F32,
            )
            tiles = slice(f * tile, (f + 1) * tile)
            if c > 0:
                part = part + total_ref[:, tiles]
            elif first:
                part = part + total_in[:, tiles]
            if last and c == chunks - 1:
                pre = part + bias_ref[:, tiles].astype(F32)
                out_ref[:, tiles] = jax.nn.gelu(pre, approximate=True).astype(BF16)
            else:
                total_ref[:, tiles] = part


def piece_of(width):
    return 512 if width % 512 == 0 else width


def expand(weight, first, total, bias, blocks, groups):
    hidden, width = weight.shape
    chunks = len(blocks) // groups
    chunk_width = blocks[0].shape[1]
    rows = groups * CAP
    last = bias is not None
    args, specs = [weight], [whole]
    scratch = [
        pltpu.VMEM((chunks, rows, chunk_width), BF16),
        pltpu.SemaphoreType.DMA((chunks, groups)),
    ]
    if first:
        args.append(total)
        specs.append(whole)
    if last:
        args.append(bias)
        specs.append(whole)
        scratch.append(pltpu.VMEM((rows, hidden), F32))
    return pl.pallas_call(
        functools.partial(expand_kernel, first, chunks, groups, last),
        in_specs=specs + [outside if first or i else whole for i in range(len(blocks))],
        out_specs=whole,
        out_shape=jax.ShapeDtypeStruct((rows, hidden), BF16 if last else F32),
        scratch_shapes=scratch,
        compiler_params=params(),
        cost_estimate=pl.CostEstimate(
            flops=2 * rows * hidden * chunk_width * chunks,
            bytes_accessed=2 * rows * chunk_width * chunks,
            transcendentals=0,
        ),
        name="expand",
    )(*args, *blocks)


def reduce_kernel(groups, offset, hidden_ref, weight_ref, *refs):
    width = refs[-1].shape[1]
    tile = piece_of(width)
    column = pl.multiple_of((lax.axis_index("tensor") ^ offset) * width, width)
    for n in range(width // tile):
        tiles = slice(n * tile, (n + 1) * tile)
        part = jnp.dot(
            hidden_ref[...],
            weight_ref[:, pl.ds(pl.multiple_of(column + n * tile, LANES), tile)],
            preferred_element_type=F32,
        )
        for g, ref in enumerate(refs[-groups:]):
            piece = part[g * CAP : (g + 1) * CAP]
            if len(refs) > groups:
                piece = piece + refs[g][:, tiles].astype(F32)
            ref[:, tiles] = piece.astype(ref.dtype)


def reduce(hidden, weight, offset, chunks, groups, received, dtypes):
    rows, depth = hidden.shape
    chunk_width = weight.shape[1] // chunks
    return pl.pallas_call(
        functools.partial(reduce_kernel, groups, offset),
        in_specs=[whole, whole] + [whole] * len(received),
        out_specs=[whole] * groups,
        out_shape=[jax.ShapeDtypeStruct((CAP, chunk_width), dtype) for dtype in dtypes],
        compiler_params=params(),
        cost_estimate=pl.CostEstimate(
            flops=2 * rows * depth * chunk_width,
            bytes_accessed=2 * rows * chunk_width,
            transcendentals=0,
        ),
        name="reduce",
    )(hidden, weight, *received)


def add_kernel(*refs):
    *given, out_ref = refs
    value = given[0][...]
    for ref in given[1:]:
        value = value + ref[...].astype(F32)
    out_ref[...] = value.astype(out_ref.dtype)


def add(parts):
    if len(parts) == 1:
        return parts[0]
    return pl.pallas_call(
        add_kernel,
        in_specs=[whole] * len(parts),
        out_specs=whole,
        out_shape=pltpu.VMEM(parts[0].shape, BF16),
        compiler_params=params(4),
        name="add",
    )(*parts)


def scatter_kernel(counts_ref, ranking_ref, rows_ref, bias_ref, patches_ref, own_ref, *refs):
    *received, out_ref, new_ref, sem = refs
    branch = own_ref[...]
    for ref in received:
        branch = branch + ref[...].astype(F32)
    live_slots = counts_ref[0]
    for i in range(1, counts_ref.shape[0]):
        live_slots = live_slots + counts_ref[i]
    slot_index = lax.broadcasted_iota(jnp.int32, branch.shape, 0)
    rows = rows_ref[...]
    new_ref[...] = jnp.where(slot_index < live_slots, rows + (branch + bias_ref[...]), rows)

    def put(slot, carry):
        image, patch = slot_source(slot, counts_ref, ranking_ref)
        pltpu.make_async_copy(
            new_ref.at[pl.ds(slot, 1)], out_ref.at[image, pl.ds(patch, 1)], sem
        ).start()
        return carry

    lax.fori_loop(0, CAP, put, 0)
    pltpu.make_async_copy(new_ref, out_ref.at[0, pl.ds(0, CAP)], sem).wait()


def masks(size):
    return [(2 << k) - 1 for k in reversed(range(size.bit_length() - 1))]


def hops(offset, size, unit, axis):
    path = []
    for mask in masks(size):
        if offset & ((mask + 1) // 2):
            path.append((axis, mask * unit))
            offset ^= mask
    return path


def routes(groups, columns):
    found = {}
    for z in range(groups):
        for y in range(columns):
            along, across = hops(z, groups, 1, "dp"), hops(y, columns, 2, "tensor")
            found[z, y] = tuple(across + along) if z == 1 else tuple(along + across)
    return found


def body(
    sizes, patches, counts, ranking, norm_gain, expand_weight, expand_bias, reduce_weight, reduce_bias
):
    groups, parts = sizes["dp"], sizes["tensor"]
    columns = parts // 2
    images, patch_len, width_local = patches.shape
    width = expand_weight.shape[1]
    patches, expand_weight, reduce_weight = (
        pltpu.with_memory_space_constraint(a, pltpu.HBM)
        for a in (patches, expand_weight, reduce_weight)
    )
    gain, bias, last_bias = (
        a.reshape(1, -1) for a in (norm_gain, expand_bias, reduce_bias)
    )

    def hop(array, axis, mask):
        return lax.ppermute(array, axis, [(i, i ^ mask) for i in range(sizes[axis])])

    rows, stats = pl.pallas_call(
        gather_kernel,
        in_specs=[scalars, scalars, outside] + [pl.BlockSpec(memory_space=pl.ANY)] * 3,
        out_specs=[whole, whole],
        out_shape=[
            pltpu.VMEM((CAP, width_local), F32),
            pltpu.VMEM((CAP, LANES), F32),
        ],
        scratch_shapes=[pltpu.SemaphoreType.DMA],
        compiler_params=params(),
        name="gather",
    )(counts, ranking, patches, gain, bias, last_bias)
    expand_weight, copied = load(expand_weight, stats, 8, patches)
    expand_weight = pltpu.with_memory_space_constraint(expand_weight, pltpu.VMEM)
    all_stats = [stats] + [hop(stats, "tensor", k) for k in reversed(range(1, parts))]
    normed = pl.pallas_call(
        functools.partial(norm_kernel, width),
        in_specs=[whole] * (3 + parts),
        out_specs=whole,
        out_shape=jax.ShapeDtypeStruct((CAP, width_local), BF16),
        compiler_params=params(),
        name="norm",
    )(rows, gain, expand_weight, *all_stats)

    [reduce_weight] = load(reduce_weight, normed, 8)
    reduce_weight = pltpu.with_memory_space_constraint(reduce_weight, pltpu.VMEM)
    path_of = routes(groups, columns)
    offset_of = {path: offset for offset, path in path_of.items()}
    by_length = sorted((p for p in offset_of if p), key=len)
    block = {(): normed}
    for path in by_length:
        block[path] = hop(block[path[:-1]], *path[-1])
        if path == (("dp", groups - 1),):
            block[path] = pass_on(block[path], reduce_weight)
    running = None
    for y in range(columns):
        mine = [block[path_of[z, y]] for z in range(groups)]
        inputs = mine + [hop(b, "tensor", 1) for b in mine]
        running = expand(
            expand_weight,
            2 * y,
            running,
            bias if y == columns - 1 else None,
            inputs,
            groups,
        )
    hidden = running

    total = {}
    for y in reversed(range(columns)):
        given = reduce(
            hidden, reduce_weight, 2 * y + 1, parts, groups, [], [BF16] * groups
        )
        received = [hop(g, "tensor", 1) for g in given]
        paths = [path_of[z, y] for z in range(groups)]
        parents = {p[:-1] for p in by_length}
        dtypes = [F32 if p in parents else BF16 for p in paths]
        kept = reduce(hidden, reduce_weight, 2 * y, parts, groups, received, dtypes)
        total.update(zip(paths, kept))
    terms = {path: [value] for path, value in total.items()}
    for path in reversed(by_length):
        terms[path[:-1]].append(hop(add(terms[path]), *path[-1]))
    own, *arrived = terms[()]

    return pl.pallas_call(
        scatter_kernel,
        in_specs=[scalars, scalars, whole, whole, outside, whole] + [whole] * len(arrived),
        out_specs=outside,
        out_shape=jax.ShapeDtypeStruct(patches.shape, F32),
        scratch_shapes=[pltpu.VMEM((CAP, width_local), F32), pltpu.SemaphoreType.DMA],
        input_output_aliases={4: 0},
        compiler_params=params(),
        name="scatter",
    )(counts, ranking, rows, last_bias, copied, own, *arrived)


def solution(mesh):
    placed = (
        P(("groups", "dp"), None, "tensor"),
        P(("groups", "dp")),
        P(("groups", "dp"), None),
        P("tensor"),
        P(("dp", "tensor"), None),
        P(("dp", "tensor")),
        P(("dp", "tensor"), None),
        P("tensor"),
    )
    return jax.shard_map(
        functools.partial(body, dict(mesh.shape)),
        mesh=mesh,
        in_specs=placed,
        out_specs=P(("groups", "dp"), None, "tensor"),
        check_vma=False,
    )
```

time: 103 us -> 175 us (1.70)
  Pallas kernels: 36.8 us -> 124 us
  local copies, waits for them, and re-layouts: 11.6 us -> 3.44 us
  waiting for transfers between devices: 28.8 us -> 22.3 us
    pallas_call x6 -> x13, Pallas kernels: 34.3 us -> 121 us  [the longest x2 103 us: load(): pl.pallas_call(load_kernel, in_specs=[outside] * len(args), out_specs=spe...]
    unnamed x37 -> x8, local copies, waits for them, and re-layouts: 11.6 us -> 1.34 us
    ppermute x33, waiting for transfers between devices: 28.8 us -> 22.3 us  [hop(): lax.ppermute(array, axis, [(i, i ^ mask) for i in range(sizes[axis])])]
    reshape x3, local copies, waits for them, and re-layouts: 0.02 us -> 2.09 us  [body(): a.reshape(1, -1)]
  transfers between devices with their start and end apart: 33 -> 33, of which waited for: 10 -> 8; matrix products, arithmetic and copies ran while one was open for 0% -> 0% of each run, Pallas kernels for 12% -> 64%
where the time goes in v2:
time: 175 us
  Pallas kernels  124 us (71%)
  starting transfers between devices  25 us (14%)
  waiting for transfers between devices  22.3 us (13%)
  local copies, waits for them, and re-layouts  3.44 us (2%)
    pallas_call x2, Pallas kernels, load(): pl.pallas_call(load_kernel, in_specs=[outside] * len(args), out_specs=spe...  103 us
    ppermute x33, starting transfers between devices, hop(): lax.ppermute(array, axis, [(i, i ^ mask) for i in range(sizes[axis])])  25 us
    ppermute x33, waiting for transfers between devices, hop(): lax.ppermute(array, axis, [(i, i ^ mask) for i in range(sizes[axis])])  22.3 us
    pallas_call x2, Pallas kernels, expand(): pl.pallas_call(functools.partial(expand_kernel, first, chunks, groups, la...  10.2 us
    pallas_call x4, Pallas kernels, reduce(): pl.pallas_call(functools.partial(reduce_kernel, groups, offset), in_specs...  5.55 us
  transfers between devices with their start and end apart: 33, of which 8 were waited for; matrix products, arithmetic and copies ran while one was open for 0% of the time, Pallas kernels for 64%

profile of v2, /device:TPU:0, one launch (start us, length us, event | category | flops | bytes accessed | tf_op | source)
XLA Modules:
  0.0 174.7 jit_solution(10553679488190570058)
XLA Ops:
  0.0 0.7 reshape.9.refs_0_.gain_ref
  0.7 0.7 reshape.10.refs_1_
  1.4 0.7 reshape.11.refs_2_.bias_ref
  2.1 0.7 copy-done
  2.8 0.7 copy-done.2
  3.4 2.4 %gather.1 = (f32[64,1536]{1,0:T(8,128)S(1)}, f32[64,128]{1,0:T(8,128)S(1)}) custom-call(s32[2]{0:T(128)S(1)} %copy-done.2, s32[2,256]{1,0:T(2,128)S(1)} %copy-done, f32[2,256,1536]{2,1,0:T(8,128)} %refs_0_.1, f32[1,1536]{1,0:T(1,128)S(1)} %reshape.9.refs_0_.gain_ref, bf16[1,1536]{1,0:T(2,128)(2,1)S(1)} %reshape.10.refs_1_, ...), custom_call_target="tpu_custom_call" | custom-call | tf_op jit(solution)/shard_map/gather/pallas_call | solution.py:325
  5.9 2.5 %collective-permute-start = (f32[64,128]{1,0:T(8,128)S(1)}, f32[64,128]{1,0:T(8,128)S(1)}, u32[]{:S(2)}, u32[]{:S(2)}) collective-permute-start(f32[64,128]{1,0:T(8,128)S(1)} %get-tuple-element.26.after_ref.refs_0_), channel_id=1, source_target_pairs={{0,3},{1,2},{2,1},{3,0},{4,7},{5,6},{6,5},{7,4},{8,11},{9,10},{10,... | collective-permute-start | bytes 98312 | tf_op jit(solution)/shard_map/ppermute | solution.py:323
  8.4 0.6 collective-permute-start.1
  9.0 96.4 %load.2 = (bf16[1536,6144]{1,0:T(8,128)(2,1)S(1)}, f32[2,256,1536]{2,1,0:T(8,128)}) custom-call(bf16[1536,6144]{1,0:T(8,128)(2,1)} %weight_ref.2, f32[64,128]{1,0:T(8,128)S(1)} %get-tuple-element.26.after_ref.refs_0_, f32[2,256,1536]{2,1,0:T(8,128)} %refs_0_.1), custom_call_target="tpu_custom_call" | custom-call | bytes 37748736 | tf_op jit(solution)/shard_map/load/pallas_call | solution.py:83
  105.5 0.2 norm.1.after_ref.refs_0_
  105.7 3.9 %collective-permute-start.4 = (bf16[64,1536]{1,0:T(8,128)(2,1)S(1)}, bf16[64,1536]{1,0:T(8,128)(2,1)S(1)}, u32[]{:S(2)}, u32[]{:S(2)}) collective-permute-start(bf16[64,1536]{1,0:T(8,128)(2,1)S(1)} %norm.1.after_ref.refs_0_), channel_id=1, source_target_pairs={{0,12},{4,8},{8,4},{12,0},{1,13},{5,9},{9,5},{13,1},{2,14},{6,10},... | collective-permute-start | bytes 589832 | tf_op jit(solution)/shard_map/ppermute | solution.py:323
  109.6 1.5 collective-permute-start.10
  111.1 6.5 %load.3.after_ref.weight_ref = bf16[1536,6144]{1,0:T(8,128)(2,1)S(1)} custom-call(bf16[1536,6144]{1,0:T(8,128)(2,1)} %weight_ref.3, bf16[64,1536]{1,0:T(8,128)(2,1)S(1)} %norm.1.after_ref.refs_0_), custom_call_target="tpu_custom_call" | custom-call | bytes 37748736 | tf_op jit(solution)/shard_map/load/pallas_call | solution.py:83
  117.7 2.1 %collective-permute-start.5 = (bf16[64,1536]{1,0:T(8,128)(2,1)S(1)}, bf16[64,1536]{1,0:T(8,128)(2,1)S(1)}, u32[]{:S(2)}, u32[]{:S(2)}) collective-permute-start(bf16[64,1536]{1,0:T(8,128)(2,1)S(1)} %pass_on.1.refs_3_), channel_id=1, source_target_pairs={{0,4},{4,0},{8,12},{12,8},{1,5},{5,1},{9,13},{13,9},{2,6},{6,2},{1... | collective-permute-start | bytes 589832 | tf_op jit(solution)/shard_map/ppermute | solution.py:323
  119.8 0.5 collective-permute-start.9
  120.3 1.2 collective-permute-start.11
  121.4 1.4 collective-permute-start.13
  122.8 2.6 %collective-permute-done.5.refs_2_ = bf16[64,1536]{1,0:T(8,128)(2,1)S(1)} collective-permute-done((bf16[64,1536]{1,0:T(8,128)(2,1)S(1)}, bf16[64,1536]{1,0:T(8,128)(2,1)S(1)}, u32[]{:S(2)}, u32[]{:S(2)}) %collective-permute-start.5) | collective-permute-done | bytes 196640 | tf_op jit(solution)/shard_map/ppermute | solution.py:323
  125.4 0.5 collective-permute-start.12
  126.0 0.5 collective-permute-start.14
  126.5 2.8 %collective-permute-done.11.refs_3_ = bf16[64,1536]{1,0:T(8,128)(2,1)S(1)} collective-permute-done((bf16[64,1536]{1,0:T(8,128)(2,1)S(1)}, bf16[64,1536]{1,0:T(8,128)(2,1)S(1)}, u32[]{:S(2)}, u32[]{:S(2)}) %collective-permute-start.11) | collective-permute-done | bytes 196640 | tf_op jit(solution)/shard_map/ppermute | solution.py:323
  129.3 0.5 collective-permute-start.17
  129.8 2.4 %collective-permute-done.12.refs_4_ = bf16[64,1536]{1,0:T(8,128)(2,1)S(1)} collective-permute-done((bf16[64,1536]{1,0:T(8,128)(2,1)S(1)}, bf16[64,1536]{1,0:T(8,128)(2,1)S(1)}, u32[]{:S(2)}, u32[]{:S(2)}) %collective-permute-start.12) | collective-permute-done | bytes 196640 | tf_op jit(solution)/shard_map/ppermute | solution.py:323
  132.2 4.8 %expand.2.refs_0_ = f32[256,1536]{1,0:T(8,128)S(1)} custom-call(bf16[1536,6144]{1,0:T(8,128)(2,1)S(1)} %get-tuple-element.28.after_ref.weight_ref, bf16[64,1536]{1,0:T(8,128)(2,1)S(1)} %norm.1.after_ref.refs_0_, bf16[64,1536]{1,0:T(8,128)(2,1)S(1)} %collective-permute-done.3.refs_1_, bf16[64,1536]{1,0:T(8,128)(2,1)S(1)} %collective-permute-done.5.refs_2_, ...), custom_call_target="tpu_custom_call" | custom-call | flops 2415919104 | bytes 1572864 | tf_op jit(solution)/shard_map/expand/pallas_call | solution.py:189
  137.1 5.4 %expand.3.hidden_ref = bf16[256,1536]{1,0:T(8,128)(2,1)S(1)} custom-call(bf16[1536,6144]{1,0:T(8,128)(2,1)S(1)} %get-tuple-element.28.after_ref.weight_ref, f32[256,1536]{1,0:T(8,128)S(1)} %expand.2.refs_0_, bf16[1,1536]{1,0:T(2,128)(2,1)S(1)} %reshape.10.refs_1_, bf16[64,1536]{1,0:T(8,128)(2,1)S(1)} %collective-permute-done.10.refs_2_, ...), custom_call_target="tpu_custom_call" | custom-call | flops 2415919104 | bytes 1572864 | tf_op jit(solution)/shard_map/expand/pallas_call | solution.py:189
  142.5 1.4 reduce.6
  143.9 0.6 collective-permute-start.22
  144.5 0.4 collective-permute-start.24
  145.0 1.4 reduce.4
  146.4 0.5 collective-permute-start.18
  146.9 0.1 collective-permute-start.19
  147.0 0.4 collective-permute-start.20
  147.4 0.1 collective-permute-start.21
  147.6 1.4 reduce.7
  148.9 1.5 collective-permute-start.27
  150.4 0.6 collective-permute-start.26
  151.1 1.0 collective-permute-start.31
  152.1 1.4 reduce.5
  153.5 3.3 %collective-permute-done.27.refs_1_ = bf16[64,1536]{1,0:T(8,128)(2,1)S(1)} collective-permute-done((bf16[64,1536]{1,0:T(8,128)(2,1)S(1)}, bf16[64,1536]{1,0:T(8,128)(2,1)S(1)}, u32[]{:S(2)}, u32[]{:S(2)}) %collective-permute-start.27) | collective-permute-done | bytes 196640 | tf_op jit(solution)/shard_map/ppermute | solution.py:323
  156.8 1.0 collective-permute-start.28
  157.8 1.1 collective-permute-start.30
  158.9 1.4 collective-permute-start.32
  160.4 0.3 collective-permute-done.26.refs_1_
  160.7 4.0 %collective-permute-done.28.refs_2_ = bf16[64,1536]{1,0:T(8,128)(2,1)S(1)} collective-permute-done((bf16[64,1536]{1,0:T(8,128)(2,1)S(1)}, bf16[64,1536]{1,0:T(8,128)(2,1)S(1)}, u32[]{:S(2)}, u32[]{:S(2)}) %collective-permute-start.28) | collective-permute-done | bytes 196640 | tf_op jit(solution)/shard_map/ppermute | solution.py:323
  164.8 0.8 collective-permute-start.29
  165.6 2.7 %collective-permute-done.30.refs_1_ = bf16[64,1536]{1,0:T(8,128)(2,1)S(1)} collective-permute-done((bf16[64,1536]{1,0:T(8,128)(2,1)S(1)}, bf16[64,1536]{1,0:T(8,128)(2,1)S(1)}, u32[]{:S(2)}, u32[]{:S(2)}) %collective-permute-start.30) | collective-permute-done | bytes 196640 | tf_op jit(solution)/shard_map/ppermute | solution.py:323
  168.3 4.1 %collective-permute-done.29.refs_0_ = bf16[64,1536]{1,0:T(8,128)(2,1)S(1)} collective-permute-done((bf16[64,1536]{1,0:T(8,128)(2,1)S(1)}, bf16[64,1536]{1,0:T(8,128)(2,1)S(1)}, u32[]{:S(2)}, u32[]{:S(2)}) %collective-permute-start.29) | collective-permute-done | bytes 196640 | tf_op jit(solution)/shard_map/ppermute | solution.py:323
  172.4 2.3 %scatter.1 = f32[2,256,1536]{2,1,0:T(8,128)} custom-call(s32[2]{0:T(128)S(1)} %copy-done.3, s32[2,256]{1,0:T(2,128)S(1)} %copy-done.1, f32[64,1536]{1,0:T(8,128)S(1)} %get-tuple-element.25.rows_ref, f32[1,1536]{1,0:T(1,128)S(1)} %reshape.11.refs_2_.bias_ref, f32[2,256,1536]{2,1,0:T(8,128)} %get-tuple-element.27.patches_ref, ...), custom_call_target="tpu_custom_call", output_to_operand_aliasing={{}: (4, {})} | custom-call | tf_op jit(solution)/shard_map/scatter/pallas_call | solution.py:389
  (44 shorter events, 0.4 us)
Async XLA Ops:
  2.1 0.7 copy-start
  2.8 0.7 copy-start.2
  5.9 99.6 %collective-permute-start = (f32[64,128]{1,0:T(8,128)S(1)}, f32[64,128]{1,0:T(8,128)S(1)}, u32[]{:S(2)}, u32[]{:S(2)}) collective-permute-start(f32[64,128]{1,0:T(8,128)S(1)} %get-tuple-element.26.after_ref.refs_0_), channel_id=1, source_target_pairs={{0,3},{1,2},{2,1},{3,0},{4,7},{5,6},{6,5},{7,4},{8,11},{9,10},{10,... | collective-permute-start | bytes 98312 | tf_op jit(solution)/shard_map/ppermute | solution.py:323
  8.4 97.1 %collective-permute-start.1 = (f32[64,128]{1,0:T(8,128)S(1)}, f32[64,128]{1,0:T(8,128)S(1)}, u32[]{:S(2)}, u32[]{:S(2)}) collective-permute-start(f32[64,128]{1,0:T(8,128)S(1)} %get-tuple-element.26.after_ref.refs_0_), channel_id=1, source_target_pairs={{0,2},{1,3},{2,0},{3,1},{4,6},{5,7},{6,4},{7,5},{8,10},{9,11},{10,... | collective-permute-start | bytes 98312 | tf_op jit(solution)/shard_map/ppermute | solution.py:323
  9.0 96.5 %collective-permute-start.2 = (f32[64,128]{1,0:T(8,128)S(1)}, f32[64,128]{1,0:T(8,128)S(1)}, u32[]{:S(2)}, u32[]{:S(2)}) collective-permute-start(f32[64,128]{1,0:T(8,128)S(1)} %get-tuple-element.26.after_ref.refs_0_), channel_id=1, source_target_pairs={{0,1},{1,0},{2,3},{3,2},{4,5},{5,4},{6,7},{7,6},{8,9},{9,8},{10,11... | collective-permute-start | bytes 98312 | tf_op jit(solution)/shard_map/ppermute | solution.py:323
  105.7 11.9 %collective-permute-start.4 = (bf16[64,1536]{1,0:T(8,128)(2,1)S(1)}, bf16[64,1536]{1,0:T(8,128)(2,1)S(1)}, u32[]{:S(2)}, u32[]{:S(2)}) collective-permute-start(bf16[64,1536]{1,0:T(8,128)(2,1)S(1)} %norm.1.after_ref.refs_0_), channel_id=1, source_target_pairs={{0,12},{4,8},{8,4},{12,0},{1,13},{5,9},{9,5},{13,1},{2,14},{6,10},... | collective-permute-start | bytes 589832 | tf_op jit(solution)/shard_map/ppermute | solution.py:323
  109.6 10.1 %collective-permute-start.3 = (bf16[64,1536]{1,0:T(8,128)(2,1)S(1)}, bf16[64,1536]{1,0:T(8,128)(2,1)S(1)}, u32[]{:S(2)}, u32[]{:S(2)}) collective-permute-start(bf16[64,1536]{1,0:T(8,128)(2,1)S(1)} %norm.1.after_ref.refs_0_), channel_id=1, source_target_pairs={{0,4},{4,0},{8,12},{12,8},{1,5},{5,1},{9,13},{13,9},{2,6},{6,2},{1... | collective-permute-start | bytes 589832 | tf_op jit(solution)/shard_map/ppermute | solution.py:323
  109.6 11.8 %collective-permute-start.6 = (bf16[64,1536]{1,0:T(8,128)(2,1)S(1)}, bf16[64,1536]{1,0:T(8,128)(2,1)S(1)}, u32[]{:S(2)}, u32[]{:S(2)}) collective-permute-start(bf16[64,1536]{1,0:T(8,128)(2,1)S(1)} %norm.1.after_ref.refs_0_), channel_id=1, source_target_pairs={{0,1},{1,0},{2,3},{3,2},{4,5},{5,4},{6,7},{7,6},{8,9},{9,8},{10,11... | collective-permute-start | bytes 589832 | tf_op jit(solution)/shard_map/ppermute | solution.py:323
  109.6 10.7 %collective-permute-start.10 = (bf16[64,1536]{1,0:T(8,128)(2,1)S(1)}, bf16[64,1536]{1,0:T(8,128)(2,1)S(1)}, u32[]{:S(2)}, u32[]{:S(2)}) collective-permute-start(bf16[64,1536]{1,0:T(8,128)(2,1)S(1)} %norm.1.after_ref.refs_0_), channel_id=1, source_target_pairs={{0,2},{1,3},{2,0},{3,1},{4,6},{5,7},{6,4},{7,5},{8,10},{9,11},{10,... | collective-permute-start | bytes 589832 | tf_op jit(solution)/shard_map/ppermute | solution.py:323
  117.7 7.8 %collective-permute-start.5 = (bf16[64,1536]{1,0:T(8,128)(2,1)S(1)}, bf16[64,1536]{1,0:T(8,128)(2,1)S(1)}, u32[]{:S(2)}, u32[]{:S(2)}) collective-permute-start(bf16[64,1536]{1,0:T(8,128)(2,1)S(1)} %pass_on.1.refs_3_), channel_id=1, source_target_pairs={{0,4},{4,0},{8,12},{12,8},{1,5},{5,1},{9,13},{13,9},{2,6},{6,2},{1... | collective-permute-start | bytes 589832 | tf_op jit(solution)/shard_map/ppermute | solution.py:323
  119.8 6.2 %collective-permute-start.7 = (bf16[64,1536]{1,0:T(8,128)(2,1)S(1)}, bf16[64,1536]{1,0:T(8,128)(2,1)S(1)}, u32[]{:S(2)}, u32[]{:S(2)}) collective-permute-start(bf16[64,1536]{1,0:T(8,128)(2,1)S(1)} %collective-permute-done.3.refs_1_), channel_id=1, source_target_pairs={{0,1},{1,0},{2,3},{3,2},{4,5},{5,4},{6,7},{7,6},{8,9},{9,8},{10,11... | collective-permute-start | bytes 589832 | tf_op jit(solution)/shard_map/ppermute | solution.py:323
  119.8 6.2 %collective-permute-start.9 = (bf16[64,1536]{1,0:T(8,128)(2,1)S(1)}, bf16[64,1536]{1,0:T(8,128)(2,1)S(1)}, u32[]{:S(2)}, u32[]{:S(2)}) collective-permute-start(bf16[64,1536]{1,0:T(8,128)(2,1)S(1)} %pass_on.1.refs_3_), channel_id=1, source_target_pairs={{0,1},{1,0},{2,3},{3,2},{4,5},{5,4},{6,7},{7,6},{8,9},{9,8},{10,11... | collective-permute-start | bytes 589832 | tf_op jit(solution)/shard_map/ppermute | solution.py:323
  120.3 9.0 %collective-permute-start.11 = (bf16[64,1536]{1,0:T(8,128)(2,1)S(1)}, bf16[64,1536]{1,0:T(8,128)(2,1)S(1)}, u32[]{:S(2)}, u32[]{:S(2)}) collective-permute-start(bf16[64,1536]{1,0:T(8,128)(2,1)S(1)} %collective-permute-done.10.refs_2_), channel_id=1, source_target_pairs={{0,4},{4,0},{8,12},{12,8},{1,5},{5,1},{9,13},{13,9},{2,6},{6,2},{1... | collective-permute-start | bytes 589832 | tf_op jit(solution)/shard_map/ppermute | solution.py:323
  121.4 7.8 %collective-permute-start.13 = (bf16[64,1536]{1,0:T(8,128)(2,1)S(1)}, bf16[64,1536]{1,0:T(8,128)(2,1)S(1)}, u32[]{:S(2)}, u32[]{:S(2)}) collective-permute-start(bf16[64,1536]{1,0:T(8,128)(2,1)S(1)} %pass_on.1.refs_3_), channel_id=1, source_target_pairs={{0,2},{1,3},{2,0},{3,1},{4,6},{5,7},{6,4},{7,5},{8,10},{9,11},{10,... | collective-permute-start | bytes 589832 | tf_op jit(solution)/shard_map/ppermute | solution.py:323
  125.4 6.8 %collective-permute-start.12 = (bf16[64,1536]{1,0:T(8,128)(2,1)S(1)}, bf16[64,1536]{1,0:T(8,128)(2,1)S(1)}, u32[]{:S(2)}, u32[]{:S(2)}) collective-permute-start(bf16[64,1536]{1,0:T(8,128)(2,1)S(1)} %collective-permute-done.5.refs_2_), channel_id=1, source_target_pairs={{0,2},{1,3},{2,0},{3,1},{4,6},{5,7},{6,4},{7,5},{8,10},{9,11},{10,... | collective-permute-start | bytes 589832 | tf_op jit(solution)/shard_map/ppermute | solution.py:323
  125.9 6.2 %collective-permute-start.8 = (bf16[64,1536]{1,0:T(8,128)(2,1)S(1)}, bf16[64,1536]{1,0:T(8,128)(2,1)S(1)}, u32[]{:S(2)}, u32[]{:S(2)}) collective-permute-start(bf16[64,1536]{1,0:T(8,128)(2,1)S(1)} %collective-permute-done.5.refs_2_), channel_id=1, source_target_pairs={{0,1},{1,0},{2,3},{3,2},{4,5},{5,4},{6,7},{7,6},{8,9},{9,8},{10,11... | collective-permute-start | bytes 589832 | tf_op jit(solution)/shard_map/ppermute | solution.py:323
  126.0 11.1 %collective-permute-start.14 = (bf16[64,1536]{1,0:T(8,128)(2,1)S(1)}, bf16[64,1536]{1,0:T(8,128)(2,1)S(1)}, u32[]{:S(2)}, u32[]{:S(2)}) collective-permute-start(bf16[64,1536]{1,0:T(8,128)(2,1)S(1)} %collective-permute-done.10.refs_2_), channel_id=1, source_target_pairs={{0,1},{1,0},{2,3},{3,2},{4,5},{5,4},{6,7},{7,6},{8,9},{9,8},{10,11... | collective-permute-start | bytes 589832 | tf_op jit(solution)/shard_map/ppermute | solution.py:323
  129.3 7.8 %collective-permute-start.15 = (bf16[64,1536]{1,0:T(8,128)(2,1)S(1)}, bf16[64,1536]{1,0:T(8,128)(2,1)S(1)}, u32[]{:S(2)}, u32[]{:S(2)}) collective-permute-start(bf16[64,1536]{1,0:T(8,128)(2,1)S(1)} %collective-permute-done.11.refs_3_), channel_id=1, source_target_pairs={{0,1},{1,0},{2,3},{3,2},{4,5},{5,4},{6,7},{7,6},{8,9},{9,8},{10,11... | collective-permute-start | bytes 589832 | tf_op jit(solution)/shard_map/ppermute | solution.py:323
  129.3 7.8 %collective-permute-start.17 = (bf16[64,1536]{1,0:T(8,128)(2,1)S(1)}, bf16[64,1536]{1,0:T(8,128)(2,1)S(1)}, u32[]{:S(2)}, u32[]{:S(2)}) collective-permute-start(bf16[64,1536]{1,0:T(8,128)(2,1)S(1)} %collective-permute-done.13.refs_5_), channel_id=1, source_target_pairs={{0,1},{1,0},{2,3},{3,2},{4,5},{5,4},{6,7},{7,6},{8,9},{9,8},{10,11... | collective-permute-start | bytes 589832 | tf_op jit(solution)/shard_map/ppermute | solution.py:323
  132.2 4.9 %collective-permute-start.16 = (bf16[64,1536]{1,0:T(8,128)(2,1)S(1)}, bf16[64,1536]{1,0:T(8,128)(2,1)S(1)}, u32[]{:S(2)}, u32[]{:S(2)}) collective-permute-start(bf16[64,1536]{1,0:T(8,128)(2,1)S(1)} %collective-permute-done.12.refs_4_), channel_id=1, source_target_pairs={{0,1},{1,0},{2,3},{3,2},{4,5},{5,4},{6,7},{7,6},{8,9},{9,8},{10,11... | collective-permute-start | bytes 589832 | tf_op jit(solution)/shard_map/ppermute | solution.py:323
  143.9 3.0 %collective-permute-start.22 = (bf16[64,1536]{1,0:T(8,128)(2,1)S(1)}, bf16[64,1536]{1,0:T(8,128)(2,1)S(1)}, u32[]{:S(2)}, u32[]{:S(2)}) collective-permute-start(bf16[64,1536]{1,0:T(8,128)(2,1)S(1)} %get-tuple-element.35), channel_id=1, source_target_pairs={{0,1},{1,0},{2,3},{3,2},{4,5},{5,4},{6,7},{7,6},{8,9},{9,8},{10,11... | collective-permute-start | bytes 589832 | tf_op jit(solution)/shard_map/ppermute | solution.py:323
  144.4 2.6 %collective-permute-start.23 = (bf16[64,1536]{1,0:T(8,128)(2,1)S(1)}, bf16[64,1536]{1,0:T(8,128)(2,1)S(1)}, u32[]{:S(2)}, u32[]{:S(2)}) collective-permute-start(bf16[64,1536]{1,0:T(8,128)(2,1)S(1)} %get-tuple-element.36), channel_id=1, source_target_pairs={{0,1},{1,0},{2,3},{3,2},{4,5},{5,4},{6,7},{7,6},{8,9},{9,8},{10,11... | collective-permute-start | bytes 589832 | tf_op jit(solution)/shard_map/ppermute | solution.py:323
  144.5 2.9 %collective-permute-start.24 = (bf16[64,1536]{1,0:T(8,128)(2,1)S(1)}, bf16[64,1536]{1,0:T(8,128)(2,1)S(1)}, u32[]{:S(2)}, u32[]{:S(2)}) collective-permute-start(bf16[64,1536]{1,0:T(8,128)(2,1)S(1)} %get-tuple-element.37), channel_id=1, source_target_pairs={{0,1},{1,0},{2,3},{3,2},{4,5},{5,4},{6,7},{7,6},{8,9},{9,8},{10,11... | collective-permute-start | bytes 589832 | tf_op jit(solution)/shard_map/ppermute | solution.py:323
  144.9 2.6 %collective-permute-start.25 = (bf16[64,1536]{1,0:T(8,128)(2,1)S(1)}, bf16[64,1536]{1,0:T(8,128)(2,1)S(1)}, u32[]{:S(2)}, u32[]{:S(2)}) collective-permute-start(bf16[64,1536]{1,0:T(8,128)(2,1)S(1)} %get-tuple-element.38), channel_id=1, source_target_pairs={{0,1},{1,0},{2,3},{3,2},{4,5},{5,4},{6,7},{7,6},{8,9},{9,8},{10,11... | collective-permute-start | bytes 589832 | tf_op jit(solution)/shard_map/ppermute | solution.py:323
  146.4 4.0 %collective-permute-start.18 = (bf16[64,1536]{1,0:T(8,128)(2,1)S(1)}, bf16[64,1536]{1,0:T(8,128)(2,1)S(1)}, u32[]{:S(2)}, u32[]{:S(2)}) collective-permute-start(bf16[64,1536]{1,0:T(8,128)(2,1)S(1)} %get-tuple-element.29), channel_id=1, source_target_pairs={{0,1},{1,0},{2,3},{3,2},{4,5},{5,4},{6,7},{7,6},{8,9},{9,8},{10,11... | collective-permute-start | bytes 589832 | tf_op jit(solution)/shard_map/ppermute | solution.py:323
  146.9 4.2 %collective-permute-start.19 = (bf16[64,1536]{1,0:T(8,128)(2,1)S(1)}, bf16[64,1536]{1,0:T(8,128)(2,1)S(1)}, u32[]{:S(2)}, u32[]{:S(2)}) collective-permute-start(bf16[64,1536]{1,0:T(8,128)(2,1)S(1)} %get-tuple-element.30), channel_id=1, source_target_pairs={{0,1},{1,0},{2,3},{3,2},{4,5},{5,4},{6,7},{7,6},{8,9},{9,8},{10,11... | collective-permute-start | bytes 589832 | tf_op jit(solution)/shard_map/ppermute | solution.py:323
  147.0 5.1 %collective-permute-start.20 = (bf16[64,1536]{1,0:T(8,128)(2,1)S(1)}, bf16[64,1536]{1,0:T(8,128)(2,1)S(1)}, u32[]{:S(2)}, u32[]{:S(2)}) collective-permute-start(bf16[64,1536]{1,0:T(8,128)(2,1)S(1)} %get-tuple-element.31), channel_id=1, source_target_pairs={{0,1},{1,0},{2,3},{3,2},{4,5},{5,4},{6,7},{7,6},{8,9},{9,8},{10,11... | collective-permute-start | bytes 589832 | tf_op jit(solution)/shard_map/ppermute | solution.py:323
  147.4 25.0 %copy-start.1 = (s32[2,256]{1,0:T(2,128)S(1)}, s32[2,256]{1,0:T(2,128)}, u32[]{:S(2)}) copy-start(s32[2,256]{1,0:T(2,128)} %ranking_ref.3) | copy-start | bytes 6148
  147.4 25.0 %copy-start.3 = (s32[2]{0:T(128)S(1)}, s32[2]{0:T(128)}, u32[]{:S(2)}) copy-start(s32[2]{0:T(128)} %counts_ref.3) | copy-start | bytes 28
  147.4 4.6 %collective-permute-start.21 = (bf16[64,1536]{1,0:T(8,128)(2,1)S(1)}, bf16[64,1536]{1,0:T(8,128)(2,1)S(1)}, u32[]{:S(2)}, u32[]{:S(2)}) collective-permute-start(bf16[64,1536]{1,0:T(8,128)(2,1)S(1)} %get-tuple-element.32), channel_id=1, source_target_pairs={{0,1},{1,0},{2,3},{3,2},{4,5},{5,4},{6,7},{7,6},{8,9},{9,8},{10,11... | collective-permute-start | bytes 589832 | tf_op jit(solution)/shard_map/ppermute | solution.py:323
  148.9 7.8 %collective-permute-start.27 = (bf16[64,1536]{1,0:T(8,128)(2,1)S(1)}, bf16[64,1536]{1,0:T(8,128)(2,1)S(1)}, u32[]{:S(2)}, u32[]{:S(2)}) collective-permute-start(bf16[64,1536]{1,0:T(8,128)(2,1)S(1)} %get-tuple-element.41), channel_id=1, source_target_pairs={{0,2},{1,3},{2,0},{3,1},{4,6},{5,7},{6,4},{7,5},{8,10},{9,11},{10,... | collective-permute-start | bytes 589832 | tf_op jit(solution)/shard_map/ppermute | solution.py:323
  150.4 10.3 %collective-permute-start.26 = (bf16[64,1536]{1,0:T(8,128)(2,1)S(1)}, bf16[64,1536]{1,0:T(8,128)(2,1)S(1)}, u32[]{:S(2)}, u32[]{:S(2)}) collective-permute-start(bf16[64,1536]{1,0:T(8,128)(2,1)S(1)} %get-tuple-element.39), channel_id=1, source_target_pairs={{0,2},{1,3},{2,0},{3,1},{4,6},{5,7},{6,4},{7,5},{8,10},{9,11},{10,... | collective-permute-start | bytes 589832 | tf_op jit(solution)/shard_map/ppermute | solution.py:323
  151.1 7.8 %collective-permute-start.31 = (bf16[64,1536]{1,0:T(8,128)(2,1)S(1)}, bf16[64,1536]{1,0:T(8,128)(2,1)S(1)}, u32[]{:S(2)}, u32[]{:S(2)}) collective-permute-start(bf16[64,1536]{1,0:T(8,128)(2,1)S(1)} %get-tuple-element.44), channel_id=1, source_target_pairs={{0,4},{4,0},{8,12},{12,8},{1,5},{5,1},{9,13},{13,9},{2,6},{6,2},{1... | collective-permute-start | bytes 589832 | tf_op jit(solution)/shard_map/ppermute | solution.py:323
  156.8 7.9 %collective-permute-start.28 = (bf16[64,1536]{1,0:T(8,128)(2,1)S(1)}, bf16[64,1536]{1,0:T(8,128)(2,1)S(1)}, u32[]{:S(2)}, u32[]{:S(2)}) collective-permute-start(bf16[64,1536]{1,0:T(8,128)(2,1)S(1)} %add.3), channel_id=1, source_target_pairs={{0,4},{4,0},{8,12},{12,8},{1,5},{5,1},{9,13},{13,9},{2,6},{6,2},{1... | collective-permute-start | bytes 589832 | tf_op jit(solution)/shard_map/ppermute | solution.py:323
  157.8 10.4 %collective-permute-start.30 = (bf16[64,1536]{1,0:T(8,128)(2,1)S(1)}, bf16[64,1536]{1,0:T(8,128)(2,1)S(1)}, u32[]{:S(2)}, u32[]{:S(2)}) collective-permute-start(bf16[64,1536]{1,0:T(8,128)(2,1)S(1)} %get-tuple-element.42), channel_id=1, source_target_pairs={{0,4},{4,0},{8,12},{12,8},{1,5},{5,1},{9,13},{13,9},{2,6},{6,2},{1... | collective-permute-start | bytes 589832 | tf_op jit(solution)/shard_map/ppermute | solution.py:323
  158.9 9.4 %collective-permute-start.32 = (bf16[64,1536]{1,0:T(8,128)(2,1)S(1)}, bf16[64,1536]{1,0:T(8,128)(2,1)S(1)}, u32[]{:S(2)}, u32[]{:S(2)}) collective-permute-start(bf16[64,1536]{1,0:T(8,128)(2,1)S(1)} %add.5), channel_id=1, source_target_pairs={{0,2},{1,3},{2,0},{3,1},{4,6},{5,7},{6,4},{7,5},{8,10},{9,11},{10,... | collective-permute-start | bytes 589832 | tf_op jit(solution)/shard_map/ppermute | solution.py:323
  164.8 7.6 %collective-permute-start.29 = (bf16[64,1536]{1,0:T(8,128)(2,1)S(1)}, bf16[64,1536]{1,0:T(8,128)(2,1)S(1)}, u32[]{:S(2)}, u32[]{:S(2)}) collective-permute-start(bf16[64,1536]{1,0:T(8,128)(2,1)S(1)} %add.4), channel_id=1, source_target_pairs={{0,12},{4,8},{8,4},{12,0},{1,13},{5,9},{9,5},{13,1},{2,14},{6,10},... | collective-permute-start | bytes 589832 | tf_op jit(solution)/shard_map/ppermute | solution.py:323

commit v3 on v2

v3 whole, which is shorter than its diff:
```python
import functools

import jax
import jax.numpy as jnp
from jax import lax
from jax.experimental import pallas as pl
from jax.experimental.pallas import tpu as pltpu
from jax.sharding import PartitionSpec as P

CAP = 64
LANES = 128
PARTS = 2
F32 = jnp.float32
BF16 = jnp.bfloat16

whole = pl.BlockSpec(memory_space=pltpu.VMEM)
scalars = pl.BlockSpec(memory_space=pltpu.SMEM)
outside = pl.BlockSpec(memory_space=pltpu.HBM)


def params(mib=6):
    return pltpu.CompilerParams(vmem_limit_bytes=mib * 2**20)


def slot_source(slot, counts_ref, ranking_ref):
    images = counts_ref.shape[0]
    image, start, end = jnp.int32(0), jnp.int32(0), jnp.int32(0)
    for i in range(images - 1):
        end = end + counts_ref[i]
        past = slot >= end
        image = jnp.where(past, i + 1, image)
        start = jnp.where(past, end, start)
    return image, ranking_ref[image, slot - start]


def gather_kernel(
    counts_any, ranking_any, patches_ref, rows_ref, stats_ref, counts_ref, ranking_ref, sem, sems
):
    copies = [
        pltpu.make_async_copy(counts_any, counts_ref, sems.at[0]),
        pltpu.make_async_copy(ranking_any, ranking_ref, sems.at[1]),
    ]
    for copy in copies:
        copy.start()
    for copy in copies:
        copy.wait()

    def fetch(slot, carry):
        image, patch = slot_source(slot, counts_ref, ranking_ref)
        pltpu.make_async_copy(
            patches_ref.at[image, pl.ds(patch, 1)], rows_ref.at[pl.ds(slot, 1)], sem
        ).start()
        return carry

    lax.fori_loop(0, CAP, fetch, 0)
    pltpu.make_async_copy(patches_ref.at[0, pl.ds(0, CAP)], rows_ref, sem).wait()
    rows = rows_ref[...]
    first = jnp.sum(rows, axis=1, keepdims=True)
    second = jnp.sum(rows * rows, axis=1, keepdims=True)
    lane = lax.broadcasted_iota(jnp.int32, (CAP, LANES), 1)
    stats_ref[...] = jnp.where(lane < LANES // 2, first, second)


def load_kernel(parts, after_ref, *refs):
    weights, refs, sems = refs[: len(parts)], refs[len(parts) : -1], refs[-1]
    copies = []
    for w, part in enumerate(parts):
        share = refs[w].shape[0] // sems.shape[1]
        for i in range(sems.shape[1]):
            row = part * refs[w].shape[0] + i * share
            copies.append(
                pltpu.make_async_copy(
                    weights[w].at[pl.ds(row, share)],
                    refs[w].at[pl.ds(i * share, share)],
                    sems.at[w, i],
                )
            )
    for copy in copies:
        copy.start()
    for copy in copies:
        copy.wait()


def load(after, *shares):
    weights = [weight for weight, _ in shares]
    shapes = [pltpu.VMEM((w.shape[0] // PARTS, w.shape[1]), w.dtype) for w in weights]
    size = sum(w.size * w.dtype.itemsize // PARTS for w in weights)
    loaded = pl.pallas_call(
        functools.partial(load_kernel, tuple(part for _, part in shares)),
        in_specs=[pl.BlockSpec(memory_space=pl.ANY)] + [outside] * len(shares),
        out_specs=[whole] * len(shares),
        out_shape=shapes,
        scratch_shapes=[pltpu.SemaphoreType.DMA((len(shares), 2))],
        compiler_params=params(),
        cost_estimate=pl.CostEstimate(flops=0, bytes_accessed=2 * size, transcendentals=0),
        name="load",
    )(after, *weights)
    return [pltpu.with_memory_space_constraint(w, pltpu.VMEM) for w in loaded]


def copy_kernel(patches_ref, after_ref, out_ref, held_ref, sems):
    images = patches_ref.shape[0]
    inward = [
        pltpu.make_async_copy(patches_ref.at[i], held_ref.at[i], sems.at[0, i])
        for i in range(images)
    ]
    outward = [
        pltpu.make_async_copy(held_ref.at[i], out_ref.at[i], sems.at[1, i]) for i in range(images)
    ]
    for copy in inward:
        copy.start()
    for i in range(images):
        inward[i].wait()
        outward[i].start()
    for copy in outward:
        copy.wait()


def copy(patches, after):
    return pl.pallas_call(
        copy_kernel,
        in_specs=[outside, pl.BlockSpec(memory_space=pl.ANY)],
        out_specs=outside,
        out_shape=pltpu.HBM(patches.shape, patches.dtype),
        scratch_shapes=[
            pltpu.VMEM(patches.shape, patches.dtype),
            pltpu.SemaphoreType.DMA((2, patches.shape[0])),
        ],
        compiler_params=params(),
        cost_estimate=pl.CostEstimate(
            flops=0, bytes_accessed=2 * patches.size * 4, transcendentals=0
        ),
        name="copy",
    )(patches, after)


def pass_kernel(*refs):
    pass


def pass_on(block, after):
    return pl.pallas_call(
        pass_kernel,
        in_specs=[whole] * (1 + len(after)),
        out_specs=whole,
        out_shape=pltpu.VMEM(block.shape, block.dtype),
        input_output_aliases={0: 0},
        compiler_params=params(1),
        name="pass_on",
    )(block, *after)


def norm_kernel(width, rows_ref, gain_ref, after_ref, *refs):
    *stats_refs, out_ref = refs
    stats = stats_refs[0][...]
    for ref in stats_refs[1:]:
        stats = stats + ref[...]
    mean = stats[:, :1] / width
    var = stats[:, LANES - 1 :] / width - mean * mean
    scale = lax.rsqrt(var + 1e-06)
    out_ref[...] = ((rows_ref[...] - mean) * scale * gain_ref[...].reshape(1, -1)).astype(BF16)


def tile_of(width, most):
    return most if width % most == 0 else width


def expand_kernel(first, chunks, groups, last, *refs):
    refs = list(refs)
    weights, refs = refs[:PARTS], refs[PARTS:]
    total_in = refs.pop(0) if first else None
    bias_ref = refs.pop(0) if last else None
    inputs, refs = refs[: chunks * groups], refs[chunks * groups :]
    out_ref, rows_ref = refs[:2]
    total_ref = refs[2] if last else out_ref
    height, width = weights[0].shape[0], rows_ref.shape[1]
    tile = tile_of(height, 256)
    for c in range(chunks):
        for g in range(groups):
            rows_ref[g * CAP : (g + 1) * CAP, :] = inputs[c * groups + g][...]
        column = pl.multiple_of((lax.axis_index("tensor") ^ (first + c)) * width, width)
        for f in range(PARTS * height // tile):
            weight_ref, row = weights[f * tile // height], f * tile % height
            part = lax.dot_general(
                rows_ref[...],
                weight_ref[row : row + tile, pl.ds(column, width)],
                (((1,), (1,)), ((), ())),
                preferred_element_type=F32,
            )
            tiles = slice(f * tile, (f + 1) * tile)
            if c > 0:
                part = part + total_ref[:, tiles]
            elif first:
                part = part + total_in[:, tiles]
            if last and c == chunks - 1:
                pre = part + bias_ref[tiles].reshape(1, -1).astype(F32)
                out_ref[:, tiles] = jax.nn.gelu(pre, approximate=True).astype(BF16)
            else:
                total_ref[:, tiles] = part


def expand(weights, first, total, bias, blocks, groups):
    hidden = PARTS * weights[0].shape[0]
    chunks = len(blocks) // groups
    chunk_width = blocks[0].shape[1]
    rows = groups * CAP
    last = bias is not None
    args = [*weights]
    scratch = [pltpu.VMEM((rows, chunk_width), BF16)]
    if first:
        args.append(total)
    if last:
        args.append(bias)
        scratch.append(pltpu.VMEM((rows, hidden), F32))
    args += blocks
    return pl.pallas_call(
        functools.partial(expand_kernel, first, chunks, groups, last),
        in_specs=[whole] * len(args),
        out_specs=whole,
        out_shape=pltpu.VMEM((rows, hidden), BF16 if last else F32),
        scratch_shapes=scratch,
        compiler_params=params(),
        cost_estimate=pl.CostEstimate(
            flops=2 * rows * hidden * chunk_width * chunks,
            bytes_accessed=2 * rows * chunk_width * chunks,
            transcendentals=0,
        ),
        name="expand",
    )(*args)


def reduce_kernel(groups, start, offset, hidden_ref, *refs):
    weights, refs = refs[:PARTS], refs[PARTS:]
    height, width = weights[0].shape[0], refs[-1].shape[1]
    tile = tile_of(width, 512)
    column = pl.multiple_of((lax.axis_index("tensor") ^ offset) * width, width)
    for n in range(width // tile):
        tiles = slice(n * tile, (n + 1) * tile)
        columns = pl.ds(pl.multiple_of(column + n * tile, LANES), tile)
        part = None
        for i, ref in enumerate(weights):
            term = jnp.dot(
                hidden_ref[start * CAP : (start + groups) * CAP, i * height : (i + 1) * height],
                ref[:, columns],
                preferred_element_type=F32,
            )
            part = term if part is None else part + term
        for g, ref in enumerate(refs[-groups:]):
            piece = part[g * CAP : (g + 1) * CAP]
            if len(refs) > groups:
                piece = piece + refs[g][:, tiles].astype(F32)
            ref[:, tiles] = piece.astype(ref.dtype)


def reduce(hidden, weights, offset, chunks, offsets, received, dtypes):
    groups, depth = len(offsets), hidden.shape[1]
    rows = groups * CAP
    chunk_width = weights[0].shape[1] // chunks
    return pl.pallas_call(
        functools.partial(reduce_kernel, groups, offsets[0], offset),
        in_specs=[whole] * (1 + PARTS + len(received)),
        out_specs=[whole] * groups,
        out_shape=[pltpu.VMEM((CAP, chunk_width), dtype) for dtype in dtypes],
        compiler_params=params(),
        cost_estimate=pl.CostEstimate(
            flops=2 * rows * depth * chunk_width,
            bytes_accessed=2 * rows * chunk_width,
            transcendentals=0,
        ),
        name="reduce",
    )(hidden, *weights, *received)


def add_kernel(*refs):
    *given, out_ref = refs
    value = given[0][...]
    for ref in given[1:]:
        value = value + ref[...].astype(F32)
    out_ref[...] = value.astype(out_ref.dtype)


def add(parts):
    if len(parts) == 1:
        return parts[0]
    return pl.pallas_call(
        add_kernel,
        in_specs=[whole] * len(parts),
        out_specs=whole,
        out_shape=pltpu.VMEM(parts[0].shape, BF16),
        compiler_params=params(4),
        name="add",
    )(*parts)


def scatter_kernel(counts_ref, ranking_ref, rows_ref, bias_ref, patches_ref, own_ref, *refs):
    *received, out_ref, new_ref, sem = refs
    branch = own_ref[...]
    for ref in received:
        branch = branch + ref[...].astype(F32)
    live_slots = counts_ref[0]
    for i in range(1, counts_ref.shape[0]):
        live_slots = live_slots + counts_ref[i]
    slot_index = lax.broadcasted_iota(jnp.int32, branch.shape, 0)
    rows = rows_ref[...]
    new_ref[...] = jnp.where(slot_index < live_slots, rows + (branch + bias_ref[...].reshape(1, -1)), rows)

    def put(slot, carry):
        image, patch = slot_source(slot, counts_ref, ranking_ref)
        pltpu.make_async_copy(
            new_ref.at[pl.ds(slot, 1)], out_ref.at[image, pl.ds(patch, 1)], sem
        ).start()
        return carry

    lax.fori_loop(0, CAP, put, 0)
    pltpu.make_async_copy(new_ref, out_ref.at[0, pl.ds(0, CAP)], sem).wait()


def masks(size):
    return [(2 << k) - 1 for k in reversed(range(size.bit_length() - 1))]


def hops(offset, size, unit, axis):
    path = []
    for mask in masks(size):
        if offset & ((mask + 1) // 2):
            path.append((axis, mask * unit))
            offset ^= mask
    return path


def routes(groups, columns):
    found = {}
    for z in range(groups):
        for y in range(columns):
            along, across = hops(z, groups, 1, "dp"), hops(y, columns, 2, "tensor")
            found[z, y] = tuple(across + along) if z == 1 else tuple(along + across)
    return found


def body(
    sizes, patches, counts, ranking, norm_gain, expand_weight, expand_bias, reduce_weight, reduce_bias
):
    groups, parts = sizes["dp"], sizes["tensor"]
    columns = parts // 2
    images, patch_len, width_local = patches.shape
    width = expand_weight.shape[1]
    patches, counts, ranking, expand_weight, reduce_weight = (
        pltpu.with_memory_space_constraint(a, pltpu.HBM)
        for a in (patches, counts, ranking, expand_weight, reduce_weight)
    )

    def hop(array, axis, mask):
        return lax.ppermute(array, axis, [(i, i ^ mask) for i in range(sizes[axis])])

    rows, stats = pl.pallas_call(
        gather_kernel,
        in_specs=[outside] * 3,
        out_specs=[whole, whole],
        out_shape=[
            pltpu.VMEM((CAP, width_local), F32),
            pltpu.VMEM((CAP, LANES), F32),
        ],
        scratch_shapes=[
            pltpu.SMEM(counts.shape, jnp.int32),
            pltpu.SMEM(ranking.shape, jnp.int32),
            pltpu.SemaphoreType.DMA,
            pltpu.SemaphoreType.DMA((2,)),
        ],
        compiler_params=params(),
        name="gather",
    )(counts, ranking, patches)
    [early] = load(stats, (expand_weight, 0))
    all_stats = [stats] + [hop(stats, "tensor", k) for k in reversed(range(1, parts))]
    normed = pl.pallas_call(
        functools.partial(norm_kernel, width),
        in_specs=[whole] * (3 + parts),
        out_specs=whole,
        out_shape=jax.ShapeDtypeStruct((CAP, width_local), BF16),
        compiler_params=params(),
        name="norm",
    )(rows, norm_gain, early, *all_stats)

    path_of = routes(groups, columns)
    offset_of = {path: offset for offset, path in path_of.items()}
    by_length = sorted((p for p in offset_of if p), key=len)
    late = [(w, i) for w in (expand_weight, reduce_weight) for i in range(1, PARTS)]
    late = load(normed, *late)
    expand_weights = [early] + late[: PARTS - 1]
    half, last = groups // 2, columns - 1
    block = {(): normed}
    far, mid = path_of[groups - 1, 0], path_of[half, 0]
    block[far] = hop(normed, *far[0])
    for path in by_length:
        if len(path) == 1 and path != far:
            block[path] = hop(normed, *path[0])
    near = [block[p] for p in (path_of[0, y] for y in range(1, columns)) if p in block]
    block[far] = pass_on(block[far], late + near)
    block[mid] = hop(block[far], *mid[-1])
    for y in range(1, columns):
        path = path_of[groups - 1, y]
        if path[:-1] == far:
            block[path] = hop(block[far], *path[-1])
    [reduce_early] = load(block[far], (reduce_weight, 0))
    reduce_weights = [reduce_early] + late[PARTS - 1 :]
    block[mid] = pass_on(
        block[mid],
        [reduce_early] + [block[p] for p in by_length if p[:-1] == far and p != mid and p in block],
    )
    for path in by_length:
        if path not in block:
            block[path] = hop(block[path[:-1]], *path[-1])

    running = None
    for y in range(columns):
        mine = [block[path_of[z, y]] for z in range(groups)]
        if y:
            mine[half] = pass_on(mine[half], [running])
        inputs = mine + [hop(b, "tensor", 1) for b in mine]
        bias = expand_bias if y == last else None
        running = expand(expand_weights, 2 * y, running, bias, inputs, groups)

    terms = {}
    parents = {p[:-1] for p in by_length}
    for y in reversed(range(columns)):
        ranges = (range(half, groups), range(half))
        received = []
        for offsets in ranges:
            given = reduce(
                running, reduce_weights, 2 * y + 1, parts, offsets, [], [BF16] * half
            )
            received.append([hop(g, "tensor", 1) for g in given])
        for offsets, got in zip(ranges, received):
            paths = [path_of[z, y] for z in offsets]
            dtypes = [F32 if p in parents else BF16 for p in paths]
            kept = reduce(running, reduce_weights, 2 * y, parts, offsets, got, dtypes)
            terms.update((p, [k]) for p, k in zip(paths, kept))
    copied = copy(patches, terms[()][0])
    order = list(reversed(by_length))
    for path in order:
        value = add(terms[path])
        if path != order[0] and path[-1] == order[0][-1]:
            value = pass_on(value, [got])
        sent = hop(value, *path[-1])
        if path == order[0]:
            got = sent
        terms[path[:-1]].append(sent)
    own, *arrived = terms[()]

    return pl.pallas_call(
        scatter_kernel,
        in_specs=[scalars, scalars, whole, whole, outside, whole] + [whole] * len(arrived),
        out_specs=outside,
        out_shape=jax.ShapeDtypeStruct(patches.shape, F32),
        scratch_shapes=[pltpu.VMEM((CAP, width_local), F32), pltpu.SemaphoreType.DMA],
        input_output_aliases={4: 0},
        compiler_params=params(),
        name="scatter",
    )(counts, ranking, rows, reduce_bias, copied, own, *arrived)


def solution(mesh):
    placed = (
        P(("groups", "dp"), None, "tensor"),
        P(("groups", "dp")),
        P(("groups", "dp"), None),
        P("tensor"),
        P(("dp", "tensor"), None),
        P(("dp", "tensor")),
        P(("dp", "tensor"), None),
        P("tensor"),
    )
    return jax.shard_map(
        functools.partial(body, dict(mesh.shape)),
        mesh=mesh,
        in_specs=placed,
        out_specs=P(("groups", "dp"), None, "tensor"),
        check_vma=False,
    )
```

time: 175 us -> 75.6 us (0.43)
  Pallas kernels: 124 us -> 34.7 us
  waiting for transfers between devices: 22.3 us -> 14.5 us
  local copies, waits for them, and re-layouts: 3.44 us -> 0.01 us
    pallas_call x8 -> x18, Pallas kernels: 111 us -> 26.2 us  [the longest x3 14.1 us: load(): pl.pallas_call(functools.partial(load_kernel, tuple((part for _, part in...]
    ppermute x33, waiting for transfers between devices: 22.3 us -> 14.5 us  [hop(): lax.ppermute(array, axis, [(i, i ^ mask) for i in range(sizes[axis])])]
    pallas_call x2, Pallas kernels: 10.2 us -> 5.74 us  [expand(): pl.pallas_call(functools.partial(expand_kernel, first, chunks, groups, la...]
    reshape x3 -> x0, local copies, waits for them, and re-layouts: 2.09 us -> none  [body(): a.reshape(1, -1)]
  transfers between devices with their start and end apart: 33 -> 33, of which waited for: 8 -> 5; matrix products, arithmetic and copies ran while one was open for 0% -> 0% of each run, Pallas kernels for 64% -> 34%
where the time goes in v3:
time: 75.6 us; the launch traced here: 75.4 us
  Pallas kernels  34.7 us (46%)
  starting transfers between devices  26 us (34%)
  waiting for transfers between devices  14.5 us (19%)
    ppermute x33, starting transfers between devices, hop(): lax.ppermute(array, axis, [(i, i ^ mask) for i in range(sizes[axis])])  26 us
    ppermute x33, waiting for transfers between devices, hop(): lax.ppermute(array, axis, [(i, i ^ mask) for i in range(sizes[axis])])  14.5 us
    pallas_call x3, Pallas kernels, load(): pl.pallas_call(functools.partial(load_kernel, tuple((part for _, part in...  14.1 us
    pallas_call x8, Pallas kernels, reduce(): pl.pallas_call(functools.partial(reduce_kernel, groups, offsets[0], offse...  6.38 us
    pallas_call x2, Pallas kernels, expand(): pl.pallas_call(functools.partial(expand_kernel, first, chunks, groups, la...  5.74 us
    pallas_call x1, Pallas kernels, copy(): pl.pallas_call(copy_kernel, in_specs=[outside, pl.BlockSpec(memory_space=...  3.1 us
    pallas_call x1, Pallas kernels, body(): pl.pallas_call(gather_kernel, in_specs=[outside] * 3, out_specs=[whole, w...  2.59 us
    pallas_call x1, Pallas kernels, body(): pl.pallas_call(scatter_kernel, in_specs=[scalars, scalars, whole, whole,...  2.46 us
  transfers between devices with their start and end apart: 33, of which 5 were waited for; matrix products, arithmetic and copies ran while one was open for 0% of the time, Pallas kernels for 34%

profile of v3, /device:TPU:0, one launch (start us, length us, event | category | flops | bytes accessed | tf_op | source)
XLA Modules:
  0.0 75.4 jit_solution(14146429682555714747)
XLA Ops:
  0.0 2.6 %gather.1 = (f32[64,1536]{1,0:T(8,128)S(1)}, f32[64,128]{1,0:T(8,128)S(1)}) custom-call(s32[2]{0:T(128)} %counts_ref.1, s32[2,256]{1,0:T(2,128)} %ranking_ref.1, f32[2,256,1536]{2,1,0:T(8,128)} %patches_ref.3), custom_call_target="tpu_custom_call" | custom-call | tf_op jit(solution)/shard_map/gather/pallas_call | solution.py:355
  2.6 2.5 %collective-permute-start = (f32[64,128]{1,0:T(8,128)S(1)}, f32[64,128]{1,0:T(8,128)S(1)}, u32[]{:S(2)}, u32[]{:S(2)}) collective-permute-start(f32[64,128]{1,0:T(8,128)S(1)} %get-tuple-element.26.after_ref.refs_0_), channel_id=1, source_target_pairs={{0,3},{1,2},{2,1},{3,0},{4,7},{5,6},{6,5},{7,4},{8,11},{9,10},{10,... | collective-permute-start | bytes 98312 | tf_op jit(solution)/shard_map/ppermute | solution.py:353
  5.1 0.6 collective-permute-start.1
  5.8 3.8 %load.3.after_ref.refs_0_ = bf16[768,6144]{1,0:T(8,128)(2,1)S(1)} custom-call(f32[64,128]{1,0:T(8,128)S(1)} %get-tuple-element.26.after_ref.refs_0_, bf16[1536,6144]{1,0:T(8,128)(2,1)} %refs_0_.4), custom_call_target="tpu_custom_call" | custom-call | bytes 18874368 | tf_op jit(solution)/shard_map/load/pallas_call | solution.py:88
  9.6 0.2 norm.1.after_ref.refs_2_
  9.8 1.8 %collective-permute-start.5 = (bf16[64,1536]{1,0:T(8,128)(2,1)S(1)}, bf16[64,1536]{1,0:T(8,128)(2,1)S(1)}, u32[]{:S(2)}, u32[]{:S(2)}) collective-permute-start(bf16[64,1536]{1,0:T(8,128)(2,1)S(1)} %norm.1.after_ref.refs_2_), channel_id=1, source_target_pairs={{0,2},{1,3},{2,0},{3,1},{4,6},{5,7},{6,4},{7,5},{8,10},{9,11},{10,... | collective-permute-start | bytes 589832 | tf_op jit(solution)/shard_map/ppermute | solution.py:353
  11.6 3.6 %collective-permute-start.4 = (bf16[64,1536]{1,0:T(8,128)(2,1)S(1)}, bf16[64,1536]{1,0:T(8,128)(2,1)S(1)}, u32[]{:S(2)}, u32[]{:S(2)}) collective-permute-start(bf16[64,1536]{1,0:T(8,128)(2,1)S(1)} %norm.1.after_ref.refs_2_), channel_id=1, source_target_pairs={{0,12},{4,8},{8,4},{12,0},{1,13},{5,9},{9,5},{13,1},{2,14},{6,10},... | collective-permute-start | bytes 589832 | tf_op jit(solution)/shard_map/ppermute | solution.py:353
  15.2 6.5 %load.4 = (bf16[768,6144]{1,0:T(8,128)(2,1)S(1)}, bf16[768,6144]{1,0:T(8,128)(2,1)S(1)}) custom-call(bf16[64,1536]{1,0:T(8,128)(2,1)S(1)} %norm.1.after_ref.refs_2_, bf16[1536,6144]{1,0:T(8,128)(2,1)} %refs_0_.4, bf16[1536,6144]{1,0:T(8,128)(2,1)} %refs_0_.5), custom_call_target="tpu_custom_call" | custom-call | bytes 37748736 | tf_op jit(solution)/shard_map/load/pallas_call | solution.py:88
  21.8 2.3 %collective-permute-start.6 = (bf16[64,1536]{1,0:T(8,128)(2,1)S(1)}, bf16[64,1536]{1,0:T(8,128)(2,1)S(1)}, u32[]{:S(2)}, u32[]{:S(2)}) collective-permute-start(bf16[64,1536]{1,0:T(8,128)(2,1)S(1)} %pass_on.5.after_ref.refs_5_), channel_id=1, source_target_pairs={{0,4},{4,0},{8,12},{12,8},{1,5},{5,1},{9,13},{13,9},{2,6},{6,2},{1... | collective-permute-start | bytes 589832 | tf_op jit(solution)/shard_map/ppermute | solution.py:353
  24.1 0.6 collective-permute-start.7
  24.7 3.8 %load.5.refs_1_.refs_0_ = bf16[768,6144]{1,0:T(8,128)(2,1)S(1)} custom-call(bf16[64,1536]{1,0:T(8,128)(2,1)S(1)} %pass_on.5.after_ref.refs_5_, bf16[1536,6144]{1,0:T(8,128)(2,1)} %refs_0_.5), custom_call_target="tpu_custom_call" | custom-call | bytes 18874368 | tf_op jit(solution)/shard_map/load/pallas_call | solution.py:88
  28.5 0.6 collective-permute-start.11
  29.2 1.2 %collective-permute-start.12 = (bf16[64,1536]{1,0:T(8,128)(2,1)S(1)}, bf16[64,1536]{1,0:T(8,128)(2,1)S(1)}, u32[]{:S(2)}, u32[]{:S(2)}) collective-permute-start(bf16[64,1536]{1,0:T(8,128)(2,1)S(1)} %collective-permute-done.5.refs_3_.refs_4_), channel_id=1, source_target_pairs={{0,4},{4,0},{8,12},{12,8},{1,5},{5,1},{9,13},{13,9},{2,6},{6,2},{1... | collective-permute-start | bytes 589832 | tf_op jit(solution)/shard_map/ppermute | solution.py:353
  30.4 0.5 collective-permute-start.14
  30.9 0.7 collective-permute-start.13
  31.6 4.8 %collective-permute-done.12.refs_5_ = bf16[64,1536]{1,0:T(8,128)(2,1)S(1)} collective-permute-done((bf16[64,1536]{1,0:T(8,128)(2,1)S(1)}, bf16[64,1536]{1,0:T(8,128)(2,1)S(1)}, u32[]{:S(2)}, u32[]{:S(2)}) %collective-permute-start.12) | collective-permute-done | bytes 196640 | tf_op jit(solution)/shard_map/ppermute | solution.py:353
  36.4 2.7 %expand.2.refs_1_.refs_2_ = f32[256,1536]{1,0:T(8,128)S(1)} custom-call(bf16[768,6144]{1,0:T(8,128)(2,1)S(1)} %load.3.after_ref.refs_0_, bf16[768,6144]{1,0:T(8,128)(2,1)S(1)} %get-tuple-element.27.refs_1_, bf16[64,1536]{1,0:T(8,128)(2,1)S(1)} %norm.1.after_ref.refs_2_, bf16[64,1536]{1,0:T(8,128)(2,1)S(1)} %collective-permute-done.3.refs_3_, ...), custom_call_target="tpu_custom_call" | custom-call | flops 2415919104 | bytes 1572864 | tf_op jit(solution)/shard_map/expand/pallas_call | solution.py:216
  39.1 0.6 collective-permute-start.16
  39.7 1.1 %collective-permute-done.16.refs_10_ = bf16[64,1536]{1,0:T(8,128)(2,1)S(1)} collective-permute-done((bf16[64,1536]{1,0:T(8,128)(2,1)S(1)}, bf16[64,1536]{1,0:T(8,128)(2,1)S(1)}, u32[]{:S(2)}, u32[]{:S(2)}) %collective-permute-start.16) | collective-permute-done | bytes 196640 | tf_op jit(solution)/shard_map/ppermute | solution.py:353
  40.7 3.1 %expand.3.hidden_ref = bf16[256,1536]{1,0:T(8,128)(2,1)S(1)} custom-call(bf16[768,6144]{1,0:T(8,128)(2,1)S(1)} %load.3.after_ref.refs_0_, bf16[768,6144]{1,0:T(8,128)(2,1)S(1)} %get-tuple-element.27.refs_1_, f32[256,1536]{1,0:T(8,128)S(1)} %expand.2.refs_1_.refs_2_, bf16[1536]{0:T(1024)(128)(2,1)S(1)} %copy-done.2, ...), custom_call_target="tpu_custom_call" | custom-call | flops 2415919104 | bytes 1572864 | tf_op jit(solution)/shard_map/expand/pallas_call | solution.py:216
  43.8 0.8 %reduce.12 = (bf16[64,1536]{1,0:T(8,128)(2,1)S(1)}, bf16[64,1536]{1,0:T(8,128)(2,1)S(1)}) custom-call(bf16[256,1536]{1,0:T(8,128)(2,1)S(1)} %expand.3.hidden_ref, bf16[768,6144]{1,0:T(8,128)(2,1)S(1)} %load.5.refs_1_.refs_0_, bf16[768,6144]{1,0:T(8,128)(2,1)S(1)} %get-tuple-element.28.refs_2_.refs_1_), custom_call_target="tpu_custom_call" | custom-call | flops 603979776 | bytes 393216 | tf_op jit(solution)/shard_map/reduce/pallas_call | solution.py:259
  44.6 0.4 collective-permute-start.22
  45.1 0.1 collective-permute-start.23
  45.2 0.8 %reduce.14 = (bf16[64,1536]{1,0:T(8,128)(2,1)S(1)}, bf16[64,1536]{1,0:T(8,128)(2,1)S(1)}) custom-call(bf16[256,1536]{1,0:T(8,128)(2,1)S(1)} %expand.3.hidden_ref, bf16[768,6144]{1,0:T(8,128)(2,1)S(1)} %load.5.refs_1_.refs_0_, bf16[768,6144]{1,0:T(8,128)(2,1)S(1)} %get-tuple-element.28.refs_2_.refs_1_), custom_call_target="tpu_custom_call" | custom-call | flops 603979776 | bytes 393216 | tf_op jit(solution)/shard_map/reduce/pallas_call | solution.py:259
  46.0 0.5 collective-permute-start.29
  46.5 0.1 collective-permute-start.30
  46.6 0.8 %reduce.10 = (bf16[64,1536]{1,0:T(8,128)(2,1)S(1)}, bf16[64,1536]{1,0:T(8,128)(2,1)S(1)}) custom-call(bf16[256,1536]{1,0:T(8,128)(2,1)S(1)} %expand.3.hidden_ref, bf16[768,6144]{1,0:T(8,128)(2,1)S(1)} %load.5.refs_1_.refs_0_, bf16[768,6144]{1,0:T(8,128)(2,1)S(1)} %get-tuple-element.28.refs_2_.refs_1_), custom_call_target="tpu_custom_call" | custom-call | flops 603979776 | bytes 393216 | tf_op jit(solution)/shard_map/reduce/pallas_call | solution.py:259
  47.4 0.5 collective-permute-start.20
  47.9 0.1 collective-permute-start.21
  48.0 0.8 %reduce.13 = (bf16[64,1536]{1,0:T(8,128)(2,1)S(1)}, bf16[64,1536]{1,0:T(8,128)(2,1)S(1)}) custom-call(bf16[256,1536]{1,0:T(8,128)(2,1)S(1)} %expand.3.hidden_ref, bf16[768,6144]{1,0:T(8,128)(2,1)S(1)} %load.5.refs_1_.refs_0_, bf16[768,6144]{1,0:T(8,128)(2,1)S(1)} %get-tuple-element.28.refs_2_.refs_1_, bf16[64,1536]{1,0:T(8,128)(2,1)S(1)} %collective-permute-done.22.refs_2_, ...), custom_call_target="tpu_custom_call" | custom-call | flops 603979776 | bytes 393216 | tf_op jit(solution)/shard_map/reduce/pallas_call | solution.py:259
  48.8 1.5 %collective-permute-start.24 = (bf16[64,1536]{1,0:T(8,128)(2,1)S(1)}, bf16[64,1536]{1,0:T(8,128)(2,1)S(1)}, u32[]{:S(2)}, u32[]{:S(2)}) collective-permute-start(bf16[64,1536]{1,0:T(8,128)(2,1)S(1)} %get-tuple-element.38), channel_id=1, source_target_pairs={{0,2},{1,3},{2,0},{3,1},{4,6},{5,7},{6,4},{7,5},{8,10},{9,11},{10,... | collective-permute-start | bytes 589832 | tf_op jit(solution)/shard_map/ppermute | solution.py:353
  50.3 0.8 %reduce.8 = (bf16[64,1536]{1,0:T(8,128)(2,1)S(1)}, bf16[64,1536]{1,0:T(8,128)(2,1)S(1)}) custom-call(bf16[256,1536]{1,0:T(8,128)(2,1)S(1)} %expand.3.hidden_ref, bf16[768,6144]{1,0:T(8,128)(2,1)S(1)} %load.5.refs_1_.refs_0_, bf16[768,6144]{1,0:T(8,128)(2,1)S(1)} %get-tuple-element.28.refs_2_.refs_1_), custom_call_target="tpu_custom_call" | custom-call | flops 603979776 | bytes 393216 | tf_op jit(solution)/shard_map/reduce/pallas_call | solution.py:259
  51.1 0.2 collective-permute-start.18
  51.2 0.4 collective-permute-start.19
  51.6 0.8 %reduce.15 = (f32[64,1536]{1,0:T(8,128)S(1)}, bf16[64,1536]{1,0:T(8,128)(2,1)S(1)}) custom-call(bf16[256,1536]{1,0:T(8,128)(2,1)S(1)} %expand.3.hidden_ref, bf16[768,6144]{1,0:T(8,128)(2,1)S(1)} %load.5.refs_1_.refs_0_, bf16[768,6144]{1,0:T(8,128)(2,1)S(1)} %get-tuple-element.28.refs_2_.refs_1_, bf16[64,1536]{1,0:T(8,128)(2,1)S(1)} %collective-permute-done.29.refs_2_, ...), custom_call_target="tpu_custom_call" | custom-call | flops 603979776 | bytes 393216 | tf_op jit(solution)/shard_map/reduce/pallas_call | solution.py:259
  52.5 0.3 collective-permute-start.31
  52.8 0.8 %reduce.11 = (f32[64,1536]{1,0:T(8,128)S(1)}, f32[64,1536]{1,0:T(8,128)S(1)}) custom-call(bf16[256,1536]{1,0:T(8,128)(2,1)S(1)} %expand.3.hidden_ref, bf16[768,6144]{1,0:T(8,128)(2,1)S(1)} %load.5.refs_1_.refs_0_, bf16[768,6144]{1,0:T(8,128)(2,1)S(1)} %get-tuple-element.28.refs_2_.refs_1_, bf16[64,1536]{1,0:T(8,128)(2,1)S(1)} %collective-permute-done.20.refs_2_, ...), custom_call_target="tpu_custom_call" | custom-call | flops 603979776 | bytes 393216 | tf_op jit(solution)/shard_map/reduce/pallas_call | solution.py:259
  53.6 2.5 %collective-permute-done.24.refs_1_ = bf16[64,1536]{1,0:T(8,128)(2,1)S(1)} collective-permute-done((bf16[64,1536]{1,0:T(8,128)(2,1)S(1)}, bf16[64,1536]{1,0:T(8,128)(2,1)S(1)}, u32[]{:S(2)}, u32[]{:S(2)}) %collective-permute-start.24) | collective-permute-done | bytes 196640 | tf_op jit(solution)/shard_map/ppermute | solution.py:353
  56.1 0.3 collective-permute-start.26
  56.5 1.4 %collective-permute-start.25 = (bf16[64,1536]{1,0:T(8,128)(2,1)S(1)}, bf16[64,1536]{1,0:T(8,128)(2,1)S(1)}, u32[]{:S(2)}, u32[]{:S(2)}) collective-permute-start(bf16[64,1536]{1,0:T(8,128)(2,1)S(1)} %pass_on.8), channel_id=1, source_target_pairs={{0,2},{1,3},{2,0},{3,1},{4,6},{5,7},{6,4},{7,5},{8,10},{9,11},{10,... | collective-permute-start | bytes 589832 | tf_op jit(solution)/shard_map/ppermute | solution.py:353
  57.9 0.8 %reduce.9 = (f32[64,1536]{1,0:T(8,128)S(1)}, bf16[64,1536]{1,0:T(8,128)(2,1)S(1)}) custom-call(bf16[256,1536]{1,0:T(8,128)(2,1)S(1)} %expand.3.hidden_ref, bf16[768,6144]{1,0:T(8,128)(2,1)S(1)} %load.5.refs_1_.refs_0_, bf16[768,6144]{1,0:T(8,128)(2,1)S(1)} %get-tuple-element.28.refs_2_.refs_1_, bf16[64,1536]{1,0:T(8,128)(2,1)S(1)} %collective-permute-done.18.refs_2_, ...), custom_call_target="tpu_custom_call" | custom-call | flops 603979776 | bytes 393216 | tf_op jit(solution)/shard_map/reduce/pallas_call | solution.py:259
  58.7 1.8 %collective-permute-start.28 = (bf16[64,1536]{1,0:T(8,128)(2,1)S(1)}, bf16[64,1536]{1,0:T(8,128)(2,1)S(1)}, u32[]{:S(2)}, u32[]{:S(2)}) collective-permute-start(bf16[64,1536]{1,0:T(8,128)(2,1)S(1)} %get-tuple-element.40), channel_id=1, source_target_pairs={{0,4},{4,0},{8,12},{12,8},{1,5},{5,1},{9,13},{13,9},{2,6},{6,2},{1... | collective-permute-start | bytes 589832 | tf_op jit(solution)/shard_map/ppermute | solution.py:353
  60.5 0.7 collective-permute-start.32
  61.2 3.3 %collective-permute-done.26.refs_2_ = bf16[64,1536]{1,0:T(8,128)(2,1)S(1)} collective-permute-done((bf16[64,1536]{1,0:T(8,128)(2,1)S(1)}, bf16[64,1536]{1,0:T(8,128)(2,1)S(1)}, u32[]{:S(2)}, u32[]{:S(2)}) %collective-permute-start.26) | collective-permute-done | bytes 196640 | tf_op jit(solution)/shard_map/ppermute | solution.py:353
  64.6 2.5 %collective-permute-start.27 = (bf16[64,1536]{1,0:T(8,128)(2,1)S(1)}, bf16[64,1536]{1,0:T(8,128)(2,1)S(1)}, u32[]{:S(2)}, u32[]{:S(2)}) collective-permute-start(bf16[64,1536]{1,0:T(8,128)(2,1)S(1)} %add.4), channel_id=1, source_target_pairs={{0,12},{4,8},{8,4},{12,0},{1,13},{5,9},{9,5},{13,1},{2,14},{6,10},... | collective-permute-start | bytes 589832 | tf_op jit(solution)/shard_map/ppermute | solution.py:353
  67.1 3.1 %copy.22.patches_ref = f32[2,256,1536]{2,1,0:T(8,128)} custom-call(f32[2,256,1536]{2,1,0:T(8,128)} %patches_ref.3, f32[64,1536]{1,0:T(8,128)S(1)} %get-tuple-element.31.after_ref.own_ref), custom_call_target="tpu_custom_call" | custom-call | bytes 6291456 | tf_op jit(solution)/shard_map/copy/pallas_call | solution.py:120
  70.2 2.8 %collective-permute-done.27.refs_0_ = bf16[64,1536]{1,0:T(8,128)(2,1)S(1)} collective-permute-done((bf16[64,1536]{1,0:T(8,128)(2,1)S(1)}, bf16[64,1536]{1,0:T(8,128)(2,1)S(1)}, u32[]{:S(2)}, u32[]{:S(2)}) %collective-permute-start.27) | collective-permute-done | bytes 196640 | tf_op jit(solution)/shard_map/ppermute | solution.py:353
  73.0 2.5 %scatter.1 = f32[2,256,1536]{2,1,0:T(8,128)} custom-call(s32[2]{0:T(128)} %counts_ref.1, s32[2,256]{1,0:T(2,128)} %ranking_ref.1, f32[64,1536]{1,0:T(8,128)S(1)} %get-tuple-element.25.rows_ref, f32[1536]{0:T(1024)S(1)} %copy-done.1, f32[2,256,1536]{2,1,0:T(8,128)} %copy.22.patches_ref, ...), custom_call_target="tpu_custom_call", output_to_operand_aliasing={{}: (4, {})} | custom-call | tf_op jit(solution)/shard_map/scatter/pallas_call | solution.py:449
  (49 shorter events, 0.4 us)
Async XLA Ops:
  2.6 7.0 %copy-start = (f32[1536]{0:T(1024)S(1)}, f32[1536]{0:T(1024)}, u32[]{:S(2)}) copy-start(f32[1536]{0:T(1024)} %gain_ref.1) | copy-start | bytes 18436
  2.6 7.0 %collective-permute-start = (f32[64,128]{1,0:T(8,128)S(1)}, f32[64,128]{1,0:T(8,128)S(1)}, u32[]{:S(2)}, u32[]{:S(2)}) collective-permute-start(f32[64,128]{1,0:T(8,128)S(1)} %get-tuple-element.26.after_ref.refs_0_), channel_id=1, source_target_pairs={{0,3},{1,2},{2,1},{3,0},{4,7},{5,6},{6,5},{7,4},{8,11},{9,10},{10,... | collective-permute-start | bytes 98312 | tf_op jit(solution)/shard_map/ppermute | solution.py:353
  5.1 4.5 %collective-permute-start.1 = (f32[64,128]{1,0:T(8,128)S(1)}, f32[64,128]{1,0:T(8,128)S(1)}, u32[]{:S(2)}, u32[]{:S(2)}) collective-permute-start(f32[64,128]{1,0:T(8,128)S(1)} %get-tuple-element.26.after_ref.refs_0_), channel_id=1, source_target_pairs={{0,2},{1,3},{2,0},{3,1},{4,6},{5,7},{6,4},{7,5},{8,10},{9,11},{10,... | collective-permute-start | bytes 98312 | tf_op jit(solution)/shard_map/ppermute | solution.py:353
  5.7 3.9 %collective-permute-start.2 = (f32[64,128]{1,0:T(8,128)S(1)}, f32[64,128]{1,0:T(8,128)S(1)}, u32[]{:S(2)}, u32[]{:S(2)}) collective-permute-start(f32[64,128]{1,0:T(8,128)S(1)} %get-tuple-element.26.after_ref.refs_0_), channel_id=1, source_target_pairs={{0,1},{1,0},{2,3},{3,2},{4,5},{5,4},{6,7},{7,6},{8,9},{9,8},{10,11... | collective-permute-start | bytes 98312 | tf_op jit(solution)/shard_map/ppermute | solution.py:353
  9.8 11.9 %collective-permute-start.5 = (bf16[64,1536]{1,0:T(8,128)(2,1)S(1)}, bf16[64,1536]{1,0:T(8,128)(2,1)S(1)}, u32[]{:S(2)}, u32[]{:S(2)}) collective-permute-start(bf16[64,1536]{1,0:T(8,128)(2,1)S(1)} %norm.1.after_ref.refs_2_), channel_id=1, source_target_pairs={{0,2},{1,3},{2,0},{3,1},{4,6},{5,7},{6,4},{7,5},{8,10},{9,11},{10,... | collective-permute-start | bytes 589832 | tf_op jit(solution)/shard_map/ppermute | solution.py:353
  11.6 10.1 %collective-permute-start.4 = (bf16[64,1536]{1,0:T(8,128)(2,1)S(1)}, bf16[64,1536]{1,0:T(8,128)(2,1)S(1)}, u32[]{:S(2)}, u32[]{:S(2)}) collective-permute-start(bf16[64,1536]{1,0:T(8,128)(2,1)S(1)} %norm.1.after_ref.refs_2_), channel_id=1, source_target_pairs={{0,12},{4,8},{8,4},{12,0},{1,13},{5,9},{9,5},{13,1},{2,14},{6,10},... | collective-permute-start | bytes 589832 | tf_op jit(solution)/shard_map/ppermute | solution.py:353
  15.2 13.8 %collective-permute-start.3 = (bf16[64,1536]{1,0:T(8,128)(2,1)S(1)}, bf16[64,1536]{1,0:T(8,128)(2,1)S(1)}, u32[]{:S(2)}, u32[]{:S(2)}) collective-permute-start(bf16[64,1536]{1,0:T(8,128)(2,1)S(1)} %norm.1.after_ref.refs_2_), channel_id=1, source_target_pairs={{0,4},{4,0},{8,12},{12,8},{1,5},{5,1},{9,13},{13,9},{2,6},{6,2},{1... | collective-permute-start | bytes 589832 | tf_op jit(solution)/shard_map/ppermute | solution.py:353
  21.8 7.4 %collective-permute-start.6 = (bf16[64,1536]{1,0:T(8,128)(2,1)S(1)}, bf16[64,1536]{1,0:T(8,128)(2,1)S(1)}, u32[]{:S(2)}, u32[]{:S(2)}) collective-permute-start(bf16[64,1536]{1,0:T(8,128)(2,1)S(1)} %pass_on.5.after_ref.refs_5_), channel_id=1, source_target_pairs={{0,4},{4,0},{8,12},{12,8},{1,5},{5,1},{9,13},{13,9},{2,6},{6,2},{1... | collective-permute-start | bytes 589832 | tf_op jit(solution)/shard_map/ppermute | solution.py:353
  24.1 6.3 %collective-permute-start.7 = (bf16[64,1536]{1,0:T(8,128)(2,1)S(1)}, bf16[64,1536]{1,0:T(8,128)(2,1)S(1)}, u32[]{:S(2)}, u32[]{:S(2)}) collective-permute-start(bf16[64,1536]{1,0:T(8,128)(2,1)S(1)} %pass_on.5.after_ref.refs_5_), channel_id=1, source_target_pairs={{0,2},{1,3},{2,0},{3,1},{4,6},{5,7},{6,4},{7,5},{8,10},{9,11},{10,... | collective-permute-start | bytes 589832 | tf_op jit(solution)/shard_map/ppermute | solution.py:353
  24.7 5.7 %collective-permute-start.8 = (bf16[64,1536]{1,0:T(8,128)(2,1)S(1)}, bf16[64,1536]{1,0:T(8,128)(2,1)S(1)}, u32[]{:S(2)}, u32[]{:S(2)}) collective-permute-start(bf16[64,1536]{1,0:T(8,128)(2,1)S(1)} %norm.1.after_ref.refs_2_), channel_id=1, source_target_pairs={{0,1},{1,0},{2,3},{3,2},{4,5},{5,4},{6,7},{7,6},{8,9},{9,8},{10,11... | collective-permute-start | bytes 589832 | tf_op jit(solution)/shard_map/ppermute | solution.py:353
  28.5 2.4 %collective-permute-start.11 = (bf16[64,1536]{1,0:T(8,128)(2,1)S(1)}, bf16[64,1536]{1,0:T(8,128)(2,1)S(1)}, u32[]{:S(2)}, u32[]{:S(2)}) collective-permute-start(bf16[64,1536]{1,0:T(8,128)(2,1)S(1)} %pass_on.5.after_ref.refs_5_), channel_id=1, source_target_pairs={{0,1},{1,0},{2,3},{3,2},{4,5},{5,4},{6,7},{7,6},{8,9},{9,8},{10,11... | collective-permute-start | bytes 589832 | tf_op jit(solution)/shard_map/ppermute | solution.py:353
  29.1 2.5 %collective-permute-start.9 = (bf16[64,1536]{1,0:T(8,128)(2,1)S(1)}, bf16[64,1536]{1,0:T(8,128)(2,1)S(1)}, u32[]{:S(2)}, u32[]{:S(2)}) collective-permute-start(bf16[64,1536]{1,0:T(8,128)(2,1)S(1)} %collective-permute-done.3.refs_3_), channel_id=1, source_target_pairs={{0,1},{1,0},{2,3},{3,2},{4,5},{5,4},{6,7},{7,6},{8,9},{9,8},{10,11... | collective-permute-start | bytes 589832 | tf_op jit(solution)/shard_map/ppermute | solution.py:353
  29.2 7.2 %collective-permute-start.12 = (bf16[64,1536]{1,0:T(8,128)(2,1)S(1)}, bf16[64,1536]{1,0:T(8,128)(2,1)S(1)}, u32[]{:S(2)}, u32[]{:S(2)}) collective-permute-start(bf16[64,1536]{1,0:T(8,128)(2,1)S(1)} %collective-permute-done.5.refs_3_.refs_4_), channel_id=1, source_target_pairs={{0,4},{4,0},{8,12},{12,8},{1,5},{5,1},{9,13},{13,9},{2,6},{6,2},{1... | collective-permute-start | bytes 589832 | tf_op jit(solution)/shard_map/ppermute | solution.py:353
  30.3 10.4 %copy-start.2 = (bf16[1536]{0:T(1024)(128)(2,1)S(1)}, bf16[1536]{0:T(1024)(128)(2,1)}, u32[]{:S(2)}) copy-start(bf16[1536]{0:T(1024)(128)(2,1)} %refs_3_.1) | copy-start | bytes 9220
  30.3 6.1 %collective-permute-start.10 = (bf16[64,1536]{1,0:T(8,128)(2,1)S(1)}, bf16[64,1536]{1,0:T(8,128)(2,1)S(1)}, u32[]{:S(2)}, u32[]{:S(2)}) collective-permute-start(bf16[64,1536]{1,0:T(8,128)(2,1)S(1)} %pass_on.6.refs_4_), channel_id=1, source_target_pairs={{0,1},{1,0},{2,3},{3,2},{4,5},{5,4},{6,7},{7,6},{8,9},{9,8},{10,11... | collective-permute-start | bytes 589832 | tf_op jit(solution)/shard_map/ppermute | solution.py:353
  30.4 9.3 %collective-permute-start.14 = (bf16[64,1536]{1,0:T(8,128)(2,1)S(1)}, bf16[64,1536]{1,0:T(8,128)(2,1)S(1)}, u32[]{:S(2)}, u32[]{:S(2)}) collective-permute-start(bf16[64,1536]{1,0:T(8,128)(2,1)S(1)} %collective-permute-done.5.refs_3_.refs_4_), channel_id=1, source_target_pairs={{0,1},{1,0},{2,3},{3,2},{4,5},{5,4},{6,7},{7,6},{8,9},{9,8},{10,11... | collective-permute-start | bytes 589832 | tf_op jit(solution)/shard_map/ppermute | solution.py:353
  30.9 8.2 %collective-permute-start.13 = (bf16[64,1536]{1,0:T(8,128)(2,1)S(1)}, bf16[64,1536]{1,0:T(8,128)(2,1)S(1)}, u32[]{:S(2)}, u32[]{:S(2)}) collective-permute-start(bf16[64,1536]{1,0:T(8,128)(2,1)S(1)} %pass_on.6.refs_4_), channel_id=1, source_target_pairs={{0,2},{1,3},{2,0},{3,1},{4,6},{5,7},{6,4},{7,5},{8,10},{9,11},{10,... | collective-permute-start | bytes 589832 | tf_op jit(solution)/shard_map/ppermute | solution.py:353
  31.5 8.1 %collective-permute-start.17 = (bf16[64,1536]{1,0:T(8,128)(2,1)S(1)}, bf16[64,1536]{1,0:T(8,128)(2,1)S(1)}, u32[]{:S(2)}, u32[]{:S(2)}) collective-permute-start(bf16[64,1536]{1,0:T(8,128)(2,1)S(1)} %collective-permute-done.7.refs_2_.refs_7_), channel_id=1, source_target_pairs={{0,1},{1,0},{2,3},{3,2},{4,5},{5,4},{6,7},{7,6},{8,9},{9,8},{10,11... | collective-permute-start | bytes 589832 | tf_op jit(solution)/shard_map/ppermute | solution.py:353
  36.4 3.3 %collective-permute-start.15 = (bf16[64,1536]{1,0:T(8,128)(2,1)S(1)}, bf16[64,1536]{1,0:T(8,128)(2,1)S(1)}, u32[]{:S(2)}, u32[]{:S(2)}) collective-permute-start(bf16[64,1536]{1,0:T(8,128)(2,1)S(1)} %collective-permute-done.12.refs_5_), channel_id=1, source_target_pairs={{0,1},{1,0},{2,3},{3,2},{4,5},{5,4},{6,7},{7,6},{8,9},{9,8},{10,11... | collective-permute-start | bytes 589832 | tf_op jit(solution)/shard_map/ppermute | solution.py:353
  39.1 1.6 %collective-permute-start.16 = (bf16[64,1536]{1,0:T(8,128)(2,1)S(1)}, bf16[64,1536]{1,0:T(8,128)(2,1)S(1)}, u32[]{:S(2)}, u32[]{:S(2)}) collective-permute-start(bf16[64,1536]{1,0:T(8,128)(2,1)S(1)} %pass_on.7.refs_6_), channel_id=1, source_target_pairs={{0,1},{1,0},{2,3},{3,2},{4,5},{5,4},{6,7},{7,6},{8,9},{9,8},{10,11... | collective-permute-start | bytes 589832 | tf_op jit(solution)/shard_map/ppermute | solution.py:353
  44.6 3.2 %collective-permute-start.22 = (bf16[64,1536]{1,0:T(8,128)(2,1)S(1)}, bf16[64,1536]{1,0:T(8,128)(2,1)S(1)}, u32[]{:S(2)}, u32[]{:S(2)}) collective-permute-start(bf16[64,1536]{1,0:T(8,128)(2,1)S(1)} %get-tuple-element.35), channel_id=1, source_target_pairs={{0,1},{1,0},{2,3},{3,2},{4,5},{5,4},{6,7},{7,6},{8,9},{9,8},{10,11... | collective-permute-start | bytes 589832 | tf_op jit(solution)/shard_map/ppermute | solution.py:353
  45.1 2.9 %collective-permute-start.23 = (bf16[64,1536]{1,0:T(8,128)(2,1)S(1)}, bf16[64,1536]{1,0:T(8,128)(2,1)S(1)}, u32[]{:S(2)}, u32[]{:S(2)}) collective-permute-start(bf16[64,1536]{1,0:T(8,128)(2,1)S(1)} %get-tuple-element.36), channel_id=1, source_target_pairs={{0,1},{1,0},{2,3},{3,2},{4,5},{5,4},{6,7},{7,6},{8,9},{9,8},{10,11... | collective-permute-start | bytes 589832 | tf_op jit(solution)/shard_map/ppermute | solution.py:353
  46.0 5.0 %collective-permute-start.29 = (bf16[64,1536]{1,0:T(8,128)(2,1)S(1)}, bf16[64,1536]{1,0:T(8,128)(2,1)S(1)}, u32[]{:S(2)}, u32[]{:S(2)}) collective-permute-start(bf16[64,1536]{1,0:T(8,128)(2,1)S(1)} %get-tuple-element.41), channel_id=1, source_target_pairs={{0,1},{1,0},{2,3},{3,2},{4,5},{5,4},{6,7},{7,6},{8,9},{9,8},{10,11... | collective-permute-start | bytes 589832 | tf_op jit(solution)/shard_map/ppermute | solution.py:353
  46.5 4.7 %collective-permute-start.30 = (bf16[64,1536]{1,0:T(8,128)(2,1)S(1)}, bf16[64,1536]{1,0:T(8,128)(2,1)S(1)}, u32[]{:S(2)}, u32[]{:S(2)}) collective-permute-start(bf16[64,1536]{1,0:T(8,128)(2,1)S(1)} %get-tuple-element.42), channel_id=1, source_target_pairs={{0,1},{1,0},{2,3},{3,2},{4,5},{5,4},{6,7},{7,6},{8,9},{9,8},{10,11... | collective-permute-start | bytes 589832 | tf_op jit(solution)/shard_map/ppermute | solution.py:353
  47.4 5.1 %collective-permute-start.20 = (bf16[64,1536]{1,0:T(8,128)(2,1)S(1)}, bf16[64,1536]{1,0:T(8,128)(2,1)S(1)}, u32[]{:S(2)}, u32[]{:S(2)}) collective-permute-start(bf16[64,1536]{1,0:T(8,128)(2,1)S(1)} %get-tuple-element.32), channel_id=1, source_target_pairs={{0,1},{1,0},{2,3},{3,2},{4,5},{5,4},{6,7},{7,6},{8,9},{9,8},{10,11... | collective-permute-start | bytes 589832 | tf_op jit(solution)/shard_map/ppermute | solution.py:353
  47.9 4.9 %collective-permute-start.21 = (bf16[64,1536]{1,0:T(8,128)(2,1)S(1)}, bf16[64,1536]{1,0:T(8,128)(2,1)S(1)}, u32[]{:S(2)}, u32[]{:S(2)}) collective-permute-start(bf16[64,1536]{1,0:T(8,128)(2,1)S(1)} %get-tuple-element.33), channel_id=1, source_target_pairs={{0,1},{1,0},{2,3},{3,2},{4,5},{5,4},{6,7},{7,6},{8,9},{9,8},{10,11... | collective-permute-start | bytes 589832 | tf_op jit(solution)/shard_map/ppermute | solution.py:353
  48.8 7.3 %collective-permute-start.24 = (bf16[64,1536]{1,0:T(8,128)(2,1)S(1)}, bf16[64,1536]{1,0:T(8,128)(2,1)S(1)}, u32[]{:S(2)}, u32[]{:S(2)}) collective-permute-start(bf16[64,1536]{1,0:T(8,128)(2,1)S(1)} %get-tuple-element.38), channel_id=1, source_target_pairs={{0,2},{1,3},{2,0},{3,1},{4,6},{5,7},{6,4},{7,5},{8,10},{9,11},{10,... | collective-permute-start | bytes 589832 | tf_op jit(solution)/shard_map/ppermute | solution.py:353
  51.1 6.8 %collective-permute-start.18 = (bf16[64,1536]{1,0:T(8,128)(2,1)S(1)}, bf16[64,1536]{1,0:T(8,128)(2,1)S(1)}, u32[]{:S(2)}, u32[]{:S(2)}) collective-permute-start(bf16[64,1536]{1,0:T(8,128)(2,1)S(1)} %get-tuple-element.29), channel_id=1, source_target_pairs={{0,1},{1,0},{2,3},{3,2},{4,5},{5,4},{6,7},{7,6},{8,9},{9,8},{10,11... | collective-permute-start | bytes 589832 | tf_op jit(solution)/shard_map/ppermute | solution.py:353
  51.2 6.6 %collective-permute-start.19 = (bf16[64,1536]{1,0:T(8,128)(2,1)S(1)}, bf16[64,1536]{1,0:T(8,128)(2,1)S(1)}, u32[]{:S(2)}, u32[]{:S(2)}) collective-permute-start(bf16[64,1536]{1,0:T(8,128)(2,1)S(1)} %get-tuple-element.30), channel_id=1, source_target_pairs={{0,1},{1,0},{2,3},{3,2},{4,5},{5,4},{6,7},{7,6},{8,9},{9,8},{10,11... | collective-permute-start | bytes 589832 | tf_op jit(solution)/shard_map/ppermute | solution.py:353
  52.5 8.0 %collective-permute-start.31 = (bf16[64,1536]{1,0:T(8,128)(2,1)S(1)}, bf16[64,1536]{1,0:T(8,128)(2,1)S(1)}, u32[]{:S(2)}, u32[]{:S(2)}) collective-permute-start(bf16[64,1536]{1,0:T(8,128)(2,1)S(1)} %get-tuple-element.44), channel_id=1, source_target_pairs={{0,4},{4,0},{8,12},{12,8},{1,5},{5,1},{9,13},{13,9},{2,6},{6,2},{1... | collective-permute-start | bytes 589832 | tf_op jit(solution)/shard_map/ppermute | solution.py:353
  56.1 8.4 %collective-permute-start.26 = (bf16[64,1536]{1,0:T(8,128)(2,1)S(1)}, bf16[64,1536]{1,0:T(8,128)(2,1)S(1)}, u32[]{:S(2)}, u32[]{:S(2)}) collective-permute-start(bf16[64,1536]{1,0:T(8,128)(2,1)S(1)} %add.3), channel_id=1, source_target_pairs={{0,4},{4,0},{8,12},{12,8},{1,5},{5,1},{9,13},{13,9},{2,6},{6,2},{1... | collective-permute-start | bytes 589832 | tf_op jit(solution)/shard_map/ppermute | solution.py:353
  56.5 16.5 %copy-start.1 = (f32[1536]{0:T(1024)S(1)}, f32[1536]{0:T(1024)}, u32[]{:S(2)}) copy-start(f32[1536]{0:T(1024)} %bias_ref.1) | copy-start | bytes 18436
  56.5 8.1 %collective-permute-start.25 = (bf16[64,1536]{1,0:T(8,128)(2,1)S(1)}, bf16[64,1536]{1,0:T(8,128)(2,1)S(1)}, u32[]{:S(2)}, u32[]{:S(2)}) collective-permute-start(bf16[64,1536]{1,0:T(8,128)(2,1)S(1)} %pass_on.8), channel_id=1, source_target_pairs={{0,2},{1,3},{2,0},{3,1},{4,6},{5,7},{6,4},{7,5},{8,10},{9,11},{10,... | collective-permute-start | bytes 589832 | tf_op jit(solution)/shard_map/ppermute | solution.py:353
  58.7 11.5 %collective-permute-start.28 = (bf16[64,1536]{1,0:T(8,128)(2,1)S(1)}, bf16[64,1536]{1,0:T(8,128)(2,1)S(1)}, u32[]{:S(2)}, u32[]{:S(2)}) collective-permute-start(bf16[64,1536]{1,0:T(8,128)(2,1)S(1)} %get-tuple-element.40), channel_id=1, source_target_pairs={{0,4},{4,0},{8,12},{12,8},{1,5},{5,1},{9,13},{13,9},{2,6},{6,2},{1... | collective-permute-start | bytes 589832 | tf_op jit(solution)/shard_map/ppermute | solution.py:353
  60.5 9.7 %collective-permute-start.32 = (bf16[64,1536]{1,0:T(8,128)(2,1)S(1)}, bf16[64,1536]{1,0:T(8,128)(2,1)S(1)}, u32[]{:S(2)}, u32[]{:S(2)}) collective-permute-start(bf16[64,1536]{1,0:T(8,128)(2,1)S(1)} %pass_on.9), channel_id=1, source_target_pairs={{0,2},{1,3},{2,0},{3,1},{4,6},{5,7},{6,4},{7,5},{8,10},{9,11},{10,... | collective-permute-start | bytes 589832 | tf_op jit(solution)/shard_map/ppermute | solution.py:353
  64.6 8.4 %collective-permute-start.27 = (bf16[64,1536]{1,0:T(8,128)(2,1)S(1)}, bf16[64,1536]{1,0:T(8,128)(2,1)S(1)}, u32[]{:S(2)}, u32[]{:S(2)}) collective-permute-start(bf16[64,1536]{1,0:T(8,128)(2,1)S(1)} %add.4), channel_id=1, source_target_pairs={{0,12},{4,8},{8,4},{12,0},{1,13},{5,9},{9,5},{13,1},{2,14},{6,10},... | collective-permute-start | bytes 589832 | tf_op jit(solution)/shard_map/ppermute | solution.py:353

commit v4 on v3

--- a/solution.py
+++ b/solution.py
@@ -52,7 +52,7 @@
         ).start()
         return carry
 
-    lax.fori_loop(0, CAP, fetch, 0)
+    lax.fori_loop(0, CAP, fetch, 0, unroll=8)
     pltpu.make_async_copy(patches_ref.at[0, pl.ds(0, CAP)], rows_ref, sem).wait()
     rows = rows_ref[...]
     first = jnp.sum(rows, axis=1, keepdims=True)
@@ -311,7 +311,7 @@
         ).start()
         return carry
 
-    lax.fori_loop(0, CAP, put, 0)
+    lax.fori_loop(0, CAP, put, 0, unroll=8)
     pltpu.make_async_copy(new_ref, out_ref.at[0, pl.ds(0, CAP)], sem).wait()
 
 
@@ -394,7 +394,7 @@
         if len(path) == 1 and path != far:
             block[path] = hop(normed, *path[0])
     near = [block[p] for p in (path_of[0, y] for y in range(1, columns)) if p in block]
-    block[far] = pass_on(block[far], late + near)
+    block[far] = pass_on(block[far], late)
     block[mid] = hop(block[far], *mid[-1])
     for y in range(1, columns):
         path = path_of[groups - 1, y]
@@ -404,17 +404,21 @@
     reduce_weights = [reduce_early] + late[PARTS - 1 :]
     block[mid] = pass_on(
         block[mid],
-        [reduce_early] + [block[p] for p in by_length if p[:-1] == far and p != mid and p in block],
+        [reduce_early] + near + [block[p] for p in by_length if p[:-1] == far and p != mid and p in block],
     )
     for path in by_length:
         if path not in block:
-            block[path] = hop(block[path[:-1]], *path[-1])
+            source = block[path[:-1]]
+            if path[-1] == mid[-1]:
+                source = pass_on(source, [block[mid]])
+            block[path] = hop(source, *path[-1])
 
     running = None
     for y in range(columns):
         mine = [block[path_of[z, y]] for z in range(groups)]
         if y:
-            mine[half] = pass_on(mine[half], [running])
+            for z in (1, half):
+                mine[z] = pass_on(mine[z], [running])
         inputs = mine + [hop(b, "tensor", 1) for b in mine]
         bias = expand_bias if y == last else None
         running = expand(expand_weights, 2 * y, running, bias, inputs, groups)
@@ -434,6 +438,8 @@
             dtypes = [F32 if p in parents else BF16 for p in paths]
             kept = reduce(running, reduce_weights, 2 * y, parts, offsets, got, dtypes)
             terms.update((p, [k]) for p, k in zip(paths, kept))
+            if y == last and offsets[0]:
+                running = pass_on(running, [kept[0]] + [g for b in received for g in b])
     copied = copy(patches, terms[()][0])
     order = list(reversed(by_length))
     for path in order:

time: 75.6 us -> 73.5 us (0.972)
  waiting for transfers between devices: 14.5 us -> 13.6 us
    ppermute x33, waiting for transfers between devices: 14.5 us -> 13.6 us  [hop(): lax.ppermute(array, axis, [(i, i ^ mask) for i in range(sizes[axis])])]
  transfers between devices with their start and end apart: 33 -> 33, of which waited for: 5 -> 10; matrix products, arithmetic and copies ran while one was open for 0% -> 0% of each run, Pallas kernels for 34% -> 34%
where the time goes in v4:
time: 73.5 us; the launch traced here: 73.3 us
  Pallas kernels  34 us (46%)
  starting transfers between devices  25.3 us (34%)
  waiting for transfers between devices  13.6 us (19%)
    ppermute x33, starting transfers between devices, hop(): lax.ppermute(array, axis, [(i, i ^ mask) for i in range(sizes[axis])])  25.3 us
    pallas_call x3, Pallas kernels, load(): pl.pallas_call(functools.partial(load_kernel, tuple((part for _, part in...  14.1 us
    ppermute x33, waiting for transfers between devices, hop(): lax.ppermute(array, axis, [(i, i ^ mask) for i in range(sizes[axis])])  13.6 us
    pallas_call x8, Pallas kernels, reduce(): pl.pallas_call(functools.partial(reduce_kernel, groups, offsets[0], offse...  6.36 us
    pallas_call x2, Pallas kernels, expand(): pl.pallas_call(functools.partial(expand_kernel, first, chunks, groups, la...  5.75 us
    pallas_call x1, Pallas kernels, copy(): pl.pallas_call(copy_kernel, in_specs=[outside, pl.BlockSpec(memory_space=...  3.1 us
    pallas_call x1, Pallas kernels, body(): pl.pallas_call(gather_kernel, in_specs=[outside] * 3, out_specs=[whole, w...  2.27 us
    pallas_call x1, Pallas kernels, body(): pl.pallas_call(scatter_kernel, in_specs=[scalars, scalars, whole, whole,...  2.1 us
  transfers between devices with their start and end apart: 33, of which 10 were waited for; matrix products, arithmetic and copies ran while one was open for 0% of the time, Pallas kernels for 34%

profile of v4, /device:TPU:0, one launch (start us, length us, event | category | flops | bytes accessed | tf_op | source)
XLA Modules:
  0.0 73.3 jit_solution(6798245715894539159)
XLA Ops:
  0.0 2.3 %gather.1 = (f32[64,1536]{1,0:T(8,128)S(1)}, f32[64,128]{1,0:T(8,128)S(1)}) custom-call(s32[2]{0:T(128)} %counts_ref.1, s32[2,256]{1,0:T(2,128)} %ranking_ref.1, f32[2,256,1536]{2,1,0:T(8,128)} %patches_ref.3), custom_call_target="tpu_custom_call" | custom-call | tf_op jit(solution)/shard_map/gather/pallas_call | solution.py:355
  2.3 2.5 %collective-permute-start = (f32[64,128]{1,0:T(8,128)S(1)}, f32[64,128]{1,0:T(8,128)S(1)}, u32[]{:S(2)}, u32[]{:S(2)}) collective-permute-start(f32[64,128]{1,0:T(8,128)S(1)} %get-tuple-element.26.after_ref.refs_0_), channel_id=1, source_target_pairs={{0,3},{1,2},{2,1},{3,0},{4,7},{5,6},{6,5},{7,4},{8,11},{9,10},{10,... | collective-permute-start | bytes 98312 | tf_op jit(solution)/shard_map/ppermute | solution.py:353
  4.8 0.6 collective-permute-start.1
  5.4 3.8 %load.3.after_ref.refs_0_ = bf16[768,6144]{1,0:T(8,128)(2,1)S(1)} custom-call(f32[64,128]{1,0:T(8,128)S(1)} %get-tuple-element.26.after_ref.refs_0_, bf16[1536,6144]{1,0:T(8,128)(2,1)} %refs_0_.4), custom_call_target="tpu_custom_call" | custom-call | bytes 18874368 | tf_op jit(solution)/shard_map/load/pallas_call | solution.py:88
  9.5 3.9 %collective-permute-start.4 = (bf16[64,1536]{1,0:T(8,128)(2,1)S(1)}, bf16[64,1536]{1,0:T(8,128)(2,1)S(1)}, u32[]{:S(2)}, u32[]{:S(2)}) collective-permute-start(bf16[64,1536]{1,0:T(8,128)(2,1)S(1)} %norm.1.after_ref.refs_2_), channel_id=1, source_target_pairs={{0,12},{4,8},{8,4},{12,0},{1,13},{5,9},{9,5},{13,1},{2,14},{6,10},... | collective-permute-start | bytes 589832 | tf_op jit(solution)/shard_map/ppermute | solution.py:353
  13.4 1.5 %collective-permute-start.6 = (bf16[64,1536]{1,0:T(8,128)(2,1)S(1)}, bf16[64,1536]{1,0:T(8,128)(2,1)S(1)}, u32[]{:S(2)}, u32[]{:S(2)}) collective-permute-start(bf16[64,1536]{1,0:T(8,128)(2,1)S(1)} %norm.1.after_ref.refs_2_), channel_id=1, source_target_pairs={{0,2},{1,3},{2,0},{3,1},{4,6},{5,7},{6,4},{7,5},{8,10},{9,11},{10,... | collective-permute-start | bytes 589832 | tf_op jit(solution)/shard_map/ppermute | solution.py:353
  14.9 6.5 %load.4 = (bf16[768,6144]{1,0:T(8,128)(2,1)S(1)}, bf16[768,6144]{1,0:T(8,128)(2,1)S(1)}) custom-call(bf16[64,1536]{1,0:T(8,128)(2,1)S(1)} %norm.1.after_ref.refs_2_, bf16[1536,6144]{1,0:T(8,128)(2,1)} %refs_0_.4, bf16[1536,6144]{1,0:T(8,128)(2,1)} %refs_0_.5), custom_call_target="tpu_custom_call" | custom-call | bytes 37748736 | tf_op jit(solution)/shard_map/load/pallas_call | solution.py:88
  21.4 0.6 collective-permute-start.7
  22.0 2.0 %collective-permute-start.5 = (bf16[64,1536]{1,0:T(8,128)(2,1)S(1)}, bf16[64,1536]{1,0:T(8,128)(2,1)S(1)}, u32[]{:S(2)}, u32[]{:S(2)}) collective-permute-start(bf16[64,1536]{1,0:T(8,128)(2,1)S(1)} %pass_on.8.after_ref.refs_5_), channel_id=1, source_target_pairs={{0,4},{4,0},{8,12},{12,8},{1,5},{5,1},{9,13},{13,9},{2,6},{6,2},{1... | collective-permute-start | bytes 589832 | tf_op jit(solution)/shard_map/ppermute | solution.py:353
  24.0 3.8 %load.5.refs_1_.refs_0_ = bf16[768,6144]{1,0:T(8,128)(2,1)S(1)} custom-call(bf16[64,1536]{1,0:T(8,128)(2,1)S(1)} %pass_on.8.after_ref.refs_5_, bf16[1536,6144]{1,0:T(8,128)(2,1)} %refs_0_.5), custom_call_target="tpu_custom_call" | custom-call | bytes 18874368 | tf_op jit(solution)/shard_map/load/pallas_call | solution.py:88
  27.8 0.6 collective-permute-start.11
  28.5 0.4 collective-permute-start.10
  29.1 1.5 %collective-permute-start.13 = (bf16[64,1536]{1,0:T(8,128)(2,1)S(1)}, bf16[64,1536]{1,0:T(8,128)(2,1)S(1)}, u32[]{:S(2)}, u32[]{:S(2)}) collective-permute-start(bf16[64,1536]{1,0:T(8,128)(2,1)S(1)} %pass_on.9.refs_4_.refs_1_), channel_id=1, source_target_pairs={{0,2},{1,3},{2,0},{3,1},{4,6},{5,7},{6,4},{7,5},{8,10},{9,11},{10,... | collective-permute-start | bytes 589832 | tf_op jit(solution)/shard_map/ppermute | solution.py:353
  30.7 1.3 %collective-permute-start.12 = (bf16[64,1536]{1,0:T(8,128)(2,1)S(1)}, bf16[64,1536]{1,0:T(8,128)(2,1)S(1)}, u32[]{:S(2)}, u32[]{:S(2)}) collective-permute-start(bf16[64,1536]{1,0:T(8,128)(2,1)S(1)} %pass_on.10), channel_id=1, source_target_pairs={{0,4},{4,0},{8,12},{12,8},{1,5},{5,1},{9,13},{13,9},{2,6},{6,2},{1... | collective-permute-start | bytes 589832 | tf_op jit(solution)/shard_map/ppermute | solution.py:353
  32.0 2.7 %expand.2.refs_1_.refs_2_ = f32[256,1536]{1,0:T(8,128)S(1)} custom-call(bf16[768,6144]{1,0:T(8,128)(2,1)S(1)} %load.3.after_ref.refs_0_, bf16[768,6144]{1,0:T(8,128)(2,1)S(1)} %get-tuple-element.27.refs_1_, bf16[64,1536]{1,0:T(8,128)(2,1)S(1)} %norm.1.after_ref.refs_2_, bf16[64,1536]{1,0:T(8,128)(2,1)S(1)} %collective-permute-done.3.refs_3_, ...), custom_call_target="tpu_custom_call" | custom-call | flops 2415919104 | bytes 1572864 | tf_op jit(solution)/shard_map/expand/pallas_call | solution.py:216
  34.6 1.7 %collective-permute-done.13.refs_0_ = bf16[64,1536]{1,0:T(8,128)(2,1)S(1)} collective-permute-done((bf16[64,1536]{1,0:T(8,128)(2,1)S(1)}, bf16[64,1536]{1,0:T(8,128)(2,1)S(1)}, u32[]{:S(2)}, u32[]{:S(2)}) %collective-permute-start.13) | collective-permute-done | bytes 196640 | tf_op jit(solution)/shard_map/ppermute | solution.py:353
  36.3 1.2 %collective-permute-done.12.refs_0_ = bf16[64,1536]{1,0:T(8,128)(2,1)S(1)} collective-permute-done((bf16[64,1536]{1,0:T(8,128)(2,1)S(1)}, bf16[64,1536]{1,0:T(8,128)(2,1)S(1)}, u32[]{:S(2)}, u32[]{:S(2)}) %collective-permute-start.12) | collective-permute-done | bytes 196640 | tf_op jit(solution)/shard_map/ppermute | solution.py:353
  37.8 1.2 %collective-permute-done.15.refs_9_ = bf16[64,1536]{1,0:T(8,128)(2,1)S(1)} collective-permute-done((bf16[64,1536]{1,0:T(8,128)(2,1)S(1)}, bf16[64,1536]{1,0:T(8,128)(2,1)S(1)}, u32[]{:S(2)}, u32[]{:S(2)}) %collective-permute-start.15) | collective-permute-done | bytes 196640 | tf_op jit(solution)/shard_map/ppermute | solution.py:353
  39.0 3.1 %expand.3.hidden_ref.refs_0_ = bf16[256,1536]{1,0:T(8,128)(2,1)S(1)} custom-call(bf16[768,6144]{1,0:T(8,128)(2,1)S(1)} %load.3.after_ref.refs_0_, bf16[768,6144]{1,0:T(8,128)(2,1)S(1)} %get-tuple-element.27.refs_1_, f32[256,1536]{1,0:T(8,128)S(1)} %expand.2.refs_1_.refs_2_, bf16[1536]{0:T(1024)(128)(2,1)S(1)} %copy-done.2, ...), custom_call_target="tpu_custom_call" | custom-call | flops 2415919104 | bytes 1572864 | tf_op jit(solution)/shard_map/expand/pallas_call | solution.py:216
  42.1 0.8 %reduce.8 = (bf16[64,1536]{1,0:T(8,128)(2,1)S(1)}, bf16[64,1536]{1,0:T(8,128)(2,1)S(1)}) custom-call(bf16[256,1536]{1,0:T(8,128)(2,1)S(1)} %expand.3.hidden_ref.refs_0_, bf16[768,6144]{1,0:T(8,128)(2,1)S(1)} %load.5.refs_1_.refs_0_, bf16[768,6144]{1,0:T(8,128)(2,1)S(1)} %get-tuple-element.28.refs_2_.refs_1_), custom_call_target="tpu_custom_call" | custom-call | flops 603979776 | bytes 393216 | tf_op jit(solution)/shard_map/reduce/pallas_call | solution.py:259
  42.9 0.2 collective-permute-start.18
  43.1 0.4 collective-permute-start.19
  43.5 0.8 %reduce.10 = (bf16[64,1536]{1,0:T(8,128)(2,1)S(1)}, bf16[64,1536]{1,0:T(8,128)(2,1)S(1)}) custom-call(bf16[256,1536]{1,0:T(8,128)(2,1)S(1)} %expand.3.hidden_ref.refs_0_, bf16[768,6144]{1,0:T(8,128)(2,1)S(1)} %load.5.refs_1_.refs_0_, bf16[768,6144]{1,0:T(8,128)(2,1)S(1)} %get-tuple-element.28.refs_2_.refs_1_), custom_call_target="tpu_custom_call" | custom-call | flops 603979776 | bytes 393216 | tf_op jit(solution)/shard_map/reduce/pallas_call | solution.py:259
  44.3 0.2 collective-permute-start.20
  44.5 0.4 collective-permute-start.21
  44.9 0.8 %reduce.9 = (bf16[64,1536]{1,0:T(8,128)(2,1)S(1)}, bf16[64,1536]{1,0:T(8,128)(2,1)S(1)}) custom-call(bf16[256,1536]{1,0:T(8,128)(2,1)S(1)} %expand.3.hidden_ref.refs_0_, bf16[768,6144]{1,0:T(8,128)(2,1)S(1)} %load.5.refs_1_.refs_0_, bf16[768,6144]{1,0:T(8,128)(2,1)S(1)} %get-tuple-element.28.refs_2_.refs_1_, ...), custom_call_target="tpu_custom_call" | custom-call | flops 603979776 | bytes 393216 | tf_op jit(solution)/shard_map/reduce/pallas_call | solution.py:259
  45.8 0.3 collective-permute-done.21.refs_5_.refs_3_
  46.1 0.8 %reduce.13 = (bf16[64,1536]{1,0:T(8,128)(2,1)S(1)}, bf16[64,1536]{1,0:T(8,128)(2,1)S(1)}) custom-call(bf16[256,1536]{1,0:T(8,128)(2,1)S(1)} %pass_on.13.hidden_ref, bf16[768,6144]{1,0:T(8,128)(2,1)S(1)} %load.5.refs_1_.refs_0_, bf16[768,6144]{1,0:T(8,128)(2,1)S(1)} %get-tuple-element.28.refs_2_.refs_1_), custom_call_target="tpu_custom_call" | custom-call | flops 603979776 | bytes 393216 | tf_op jit(solution)/shard_map/reduce/pallas_call | solution.py:259
  46.9 0.3 collective-permute-start.24
  47.2 0.3 collective-permute-start.25
  47.5 0.6 collective-permute-start.26
  48.1 0.8 %reduce.15 = (f32[64,1536]{1,0:T(8,128)S(1)}, bf16[64,1536]{1,0:T(8,128)(2,1)S(1)}) custom-call(bf16[256,1536]{1,0:T(8,128)(2,1)S(1)} %pass_on.13.hidden_ref, bf16[768,6144]{1,0:T(8,128)(2,1)S(1)} %load.5.refs_1_.refs_0_, bf16[768,6144]{1,0:T(8,128)(2,1)S(1)} %get-tuple-element.28.refs_2_.refs_1_, ...), custom_call_target="tpu_custom_call" | custom-call | flops 603979776 | bytes 393216 | tf_op jit(solution)/shard_map/reduce/pallas_call | solution.py:259
  48.9 1.1 %collective-permute-start.31 = (bf16[64,1536]{1,0:T(8,128)(2,1)S(1)}, bf16[64,1536]{1,0:T(8,128)(2,1)S(1)}, u32[]{:S(2)}, u32[]{:S(2)}) collective-permute-start(bf16[64,1536]{1,0:T(8,128)(2,1)S(1)} %get-tuple-element.44), channel_id=1, source_target_pairs={{0,4},{4,0},{8,12},{12,8},{1,5},{5,1},{9,13},{13,9},{2,6},{6,2},{1... | collective-permute-start | bytes 589832 | tf_op jit(solution)/shard_map/ppermute | solution.py:353
  50.0 0.8 %reduce.11 = (bf16[64,1536]{1,0:T(8,128)(2,1)S(1)}, bf16[64,1536]{1,0:T(8,128)(2,1)S(1)}) custom-call(bf16[256,1536]{1,0:T(8,128)(2,1)S(1)} %pass_on.13.hidden_ref, bf16[768,6144]{1,0:T(8,128)(2,1)S(1)} %load.5.refs_1_.refs_0_, bf16[768,6144]{1,0:T(8,128)(2,1)S(1)} %get-tuple-element.28.refs_2_.refs_1_), custom_call_target="tpu_custom_call" | custom-call | flops 603979776 | bytes 393216 | tf_op jit(solution)/shard_map/reduce/pallas_call | solution.py:259
  50.9 0.5 collective-permute-start.23
  51.4 0.8 %reduce.14 = (f32[64,1536]{1,0:T(8,128)S(1)}, f32[64,1536]{1,0:T(8,128)S(1)}) custom-call(bf16[256,1536]{1,0:T(8,128)(2,1)S(1)} %pass_on.13.hidden_ref, bf16[768,6144]{1,0:T(8,128)(2,1)S(1)} %load.5.refs_1_.refs_0_, bf16[768,6144]{1,0:T(8,128)(2,1)S(1)} %get-tuple-element.28.refs_2_.refs_1_, bf16[64,1536]{1,0:T(8,128)(2,1)S(1)} %collective-permute-done.24.refs_2_, ...), custom_call_target="tpu_custom_call" | custom-call | flops 603979776 | bytes 393216 | tf_op jit(solution)/shard_map/reduce/pallas_call | solution.py:259
  52.2 2.3 %collective-permute-done.26.refs_1_ = bf16[64,1536]{1,0:T(8,128)(2,1)S(1)} collective-permute-done((bf16[64,1536]{1,0:T(8,128)(2,1)S(1)}, bf16[64,1536]{1,0:T(8,128)(2,1)S(1)}, u32[]{:S(2)}, u32[]{:S(2)}) %collective-permute-start.26) | collective-permute-done | bytes 196640 | tf_op jit(solution)/shard_map/ppermute | solution.py:353
  54.5 1.1 %collective-permute-start.28 = (bf16[64,1536]{1,0:T(8,128)(2,1)S(1)}, bf16[64,1536]{1,0:T(8,128)(2,1)S(1)}, u32[]{:S(2)}, u32[]{:S(2)}) collective-permute-start(bf16[64,1536]{1,0:T(8,128)(2,1)S(1)} %add.3), channel_id=1, source_target_pairs={{0,4},{4,0},{8,12},{12,8},{1,5},{5,1},{9,13},{13,9},{2,6},{6,2},{1... | collective-permute-start | bytes 589832 | tf_op jit(solution)/shard_map/ppermute | solution.py:353
  55.6 0.6 collective-permute-start.27
  56.3 1.4 %collective-permute-start.32 = (bf16[64,1536]{1,0:T(8,128)(2,1)S(1)}, bf16[64,1536]{1,0:T(8,128)(2,1)S(1)}, u32[]{:S(2)}, u32[]{:S(2)}) collective-permute-start(bf16[64,1536]{1,0:T(8,128)(2,1)S(1)} %pass_on.15), channel_id=1, source_target_pairs={{0,2},{1,3},{2,0},{3,1},{4,6},{5,7},{6,4},{7,5},{8,10},{9,11},{10,... | collective-permute-start | bytes 589832 | tf_op jit(solution)/shard_map/ppermute | solution.py:353
  57.8 0.8 %reduce.12 = (f32[64,1536]{1,0:T(8,128)S(1)}, bf16[64,1536]{1,0:T(8,128)(2,1)S(1)}) custom-call(bf16[256,1536]{1,0:T(8,128)(2,1)S(1)} %pass_on.13.hidden_ref, bf16[768,6144]{1,0:T(8,128)(2,1)S(1)} %load.5.refs_1_.refs_0_, bf16[768,6144]{1,0:T(8,128)(2,1)S(1)} %get-tuple-element.28.refs_2_.refs_1_, bf16[64,1536]{1,0:T(8,128)(2,1)S(1)} %collective-permute-done.22.refs_2_, ...), custom_call_target="tpu_custom_call" | custom-call | flops 603979776 | bytes 393216 | tf_op jit(solution)/shard_map/reduce/pallas_call | solution.py:259
  58.6 1.1 %collective-permute-start.30 = (bf16[64,1536]{1,0:T(8,128)(2,1)S(1)}, bf16[64,1536]{1,0:T(8,128)(2,1)S(1)}, u32[]{:S(2)}, u32[]{:S(2)}) collective-permute-start(bf16[64,1536]{1,0:T(8,128)(2,1)S(1)} %get-tuple-element.42), channel_id=1, source_target_pairs={{0,4},{4,0},{8,12},{12,8},{1,5},{5,1},{9,13},{13,9},{2,6},{6,2},{1... | collective-permute-start | bytes 589832 | tf_op jit(solution)/shard_map/ppermute | solution.py:353
  59.7 2.1 %collective-permute-done.28.refs_2_ = bf16[64,1536]{1,0:T(8,128)(2,1)S(1)} collective-permute-done((bf16[64,1536]{1,0:T(8,128)(2,1)S(1)}, bf16[64,1536]{1,0:T(8,128)(2,1)S(1)}, u32[]{:S(2)}, u32[]{:S(2)}) %collective-permute-start.28) | collective-permute-done | bytes 196640 | tf_op jit(solution)/shard_map/ppermute | solution.py:353
  61.7 1.7 %collective-permute-done.27.refs_1_ = bf16[64,1536]{1,0:T(8,128)(2,1)S(1)} collective-permute-done((bf16[64,1536]{1,0:T(8,128)(2,1)S(1)}, bf16[64,1536]{1,0:T(8,128)(2,1)S(1)}, u32[]{:S(2)}, u32[]{:S(2)}) %collective-permute-start.27) | collective-permute-done | bytes 196640 | tf_op jit(solution)/shard_map/ppermute | solution.py:353
  63.5 1.8 %collective-permute-start.29 = (bf16[64,1536]{1,0:T(8,128)(2,1)S(1)}, bf16[64,1536]{1,0:T(8,128)(2,1)S(1)}, u32[]{:S(2)}, u32[]{:S(2)}) collective-permute-start(bf16[64,1536]{1,0:T(8,128)(2,1)S(1)} %add.4), channel_id=1, source_target_pairs={{0,12},{4,8},{8,4},{12,0},{1,13},{5,9},{9,5},{13,1},{2,14},{6,10},... | collective-permute-start | bytes 589832 | tf_op jit(solution)/shard_map/ppermute | solution.py:353
  65.3 3.1 %copy.28.patches_ref = f32[2,256,1536]{2,1,0:T(8,128)} custom-call(f32[2,256,1536]{2,1,0:T(8,128)} %patches_ref.3, f32[64,1536]{1,0:T(8,128)S(1)} %get-tuple-element.36.after_ref.own_ref), custom_call_target="tpu_custom_call" | custom-call | bytes 6291456 | tf_op jit(solution)/shard_map/copy/pallas_call | solution.py:120
  68.4 2.7 %collective-permute-done.29.refs_0_ = bf16[64,1536]{1,0:T(8,128)(2,1)S(1)} collective-permute-done((bf16[64,1536]{1,0:T(8,128)(2,1)S(1)}, bf16[64,1536]{1,0:T(8,128)(2,1)S(1)}, u32[]{:S(2)}, u32[]{:S(2)}) %collective-permute-start.29) | collective-permute-done | bytes 196640 | tf_op jit(solution)/shard_map/ppermute | solution.py:353
  71.2 2.1 %scatter.1 = f32[2,256,1536]{2,1,0:T(8,128)} custom-call(s32[2]{0:T(128)} %counts_ref.1, s32[2,256]{1,0:T(2,128)} %ranking_ref.1, f32[64,1536]{1,0:T(8,128)S(1)} %get-tuple-element.25.rows_ref, f32[1536]{0:T(1024)S(1)} %copy-done.1, f32[2,256,1536]{2,1,0:T(8,128)} %copy.28.patches_ref, ...), custom_call_target="tpu_custom_call", output_to_operand_aliasing={{}: (4, {})} | custom-call | tf_op jit(solution)/shard_map/scatter/pallas_call | solution.py:455
  (53 shorter events, 1.1 us)
Async XLA Ops:
  2.3 7.0 %copy-start = (f32[1536]{0:T(1024)S(1)}, f32[1536]{0:T(1024)}, u32[]{:S(2)}) copy-start(f32[1536]{0:T(1024)} %gain_ref.1) | copy-start | bytes 18436
  2.3 7.0 %collective-permute-start = (f32[64,128]{1,0:T(8,128)S(1)}, f32[64,128]{1,0:T(8,128)S(1)}, u32[]{:S(2)}, u32[]{:S(2)}) collective-permute-start(f32[64,128]{1,0:T(8,128)S(1)} %get-tuple-element.26.after_ref.refs_0_), channel_id=1, source_target_pairs={{0,3},{1,2},{2,1},{3,0},{4,7},{5,6},{6,5},{7,4},{8,11},{9,10},{10,... | collective-permute-start | bytes 98312 | tf_op jit(solution)/shard_map/ppermute | solution.py:353
  4.8 4.5 %collective-permute-start.1 = (f32[64,128]{1,0:T(8,128)S(1)}, f32[64,128]{1,0:T(8,128)S(1)}, u32[]{:S(2)}, u32[]{:S(2)}) collective-permute-start(f32[64,128]{1,0:T(8,128)S(1)} %get-tuple-element.26.after_ref.refs_0_), channel_id=1, source_target_pairs={{0,2},{1,3},{2,0},{3,1},{4,6},{5,7},{6,4},{7,5},{8,10},{9,11},{10,... | collective-permute-start | bytes 98312 | tf_op jit(solution)/shard_map/ppermute | solution.py:353
  5.4 3.9 %collective-permute-start.2 = (f32[64,128]{1,0:T(8,128)S(1)}, f32[64,128]{1,0:T(8,128)S(1)}, u32[]{:S(2)}, u32[]{:S(2)}) collective-permute-start(f32[64,128]{1,0:T(8,128)S(1)} %get-tuple-element.26.after_ref.refs_0_), channel_id=1, source_target_pairs={{0,1},{1,0},{2,3},{3,2},{4,5},{5,4},{6,7},{7,6},{8,9},{9,8},{10,11... | collective-permute-start | bytes 98312 | tf_op jit(solution)/shard_map/ppermute | solution.py:353
  9.5 11.9 %collective-permute-start.4 = (bf16[64,1536]{1,0:T(8,128)(2,1)S(1)}, bf16[64,1536]{1,0:T(8,128)(2,1)S(1)}, u32[]{:S(2)}, u32[]{:S(2)}) collective-permute-start(bf16[64,1536]{1,0:T(8,128)(2,1)S(1)} %norm.1.after_ref.refs_2_), channel_id=1, source_target_pairs={{0,12},{4,8},{8,4},{12,0},{1,13},{5,9},{9,5},{13,1},{2,14},{6,10},... | collective-permute-start | bytes 589832 | tf_op jit(solution)/shard_map/ppermute | solution.py:353
  13.4 14.4 %collective-permute-start.6 = (bf16[64,1536]{1,0:T(8,128)(2,1)S(1)}, bf16[64,1536]{1,0:T(8,128)(2,1)S(1)}, u32[]{:S(2)}, u32[]{:S(2)}) collective-permute-start(bf16[64,1536]{1,0:T(8,128)(2,1)S(1)} %norm.1.after_ref.refs_2_), channel_id=1, source_target_pairs={{0,2},{1,3},{2,0},{3,1},{4,6},{5,7},{6,4},{7,5},{8,10},{9,11},{10,... | collective-permute-start | bytes 589832 | tf_op jit(solution)/shard_map/ppermute | solution.py:353
  14.9 13.5 %collective-permute-start.3 = (bf16[64,1536]{1,0:T(8,128)(2,1)S(1)}, bf16[64,1536]{1,0:T(8,128)(2,1)S(1)}, u32[]{:S(2)}, u32[]{:S(2)}) collective-permute-start(bf16[64,1536]{1,0:T(8,128)(2,1)S(1)} %norm.1.after_ref.refs_2_), channel_id=1, source_target_pairs={{0,4},{4,0},{8,12},{12,8},{1,5},{5,1},{9,13},{13,9},{2,6},{6,2},{1... | collective-permute-start | bytes 589832 | tf_op jit(solution)/shard_map/ppermute | solution.py:353
  21.4 7.1 %collective-permute-start.7 = (bf16[64,1536]{1,0:T(8,128)(2,1)S(1)}, bf16[64,1536]{1,0:T(8,128)(2,1)S(1)}, u32[]{:S(2)}, u32[]{:S(2)}) collective-permute-start(bf16[64,1536]{1,0:T(8,128)(2,1)S(1)} %pass_on.8.after_ref.refs_5_), channel_id=1, source_target_pairs={{0,2},{1,3},{2,0},{3,1},{4,6},{5,7},{6,4},{7,5},{8,10},{9,11},{10,... | collective-permute-start | bytes 589832 | tf_op jit(solution)/shard_map/ppermute | solution.py:353
  22.0 6.5 %collective-permute-start.5 = (bf16[64,1536]{1,0:T(8,128)(2,1)S(1)}, bf16[64,1536]{1,0:T(8,128)(2,1)S(1)}, u32[]{:S(2)}, u32[]{:S(2)}) collective-permute-start(bf16[64,1536]{1,0:T(8,128)(2,1)S(1)} %pass_on.8.after_ref.refs_5_), channel_id=1, source_target_pairs={{0,4},{4,0},{8,12},{12,8},{1,5},{5,1},{9,13},{13,9},{2,6},{6,2},{1... | collective-permute-start | bytes 589832 | tf_op jit(solution)/shard_map/ppermute | solution.py:353
  24.0 5.1 %collective-permute-start.8 = (bf16[64,1536]{1,0:T(8,128)(2,1)S(1)}, bf16[64,1536]{1,0:T(8,128)(2,1)S(1)}, u32[]{:S(2)}, u32[]{:S(2)}) collective-permute-start(bf16[64,1536]{1,0:T(8,128)(2,1)S(1)} %norm.1.after_ref.refs_2_), channel_id=1, source_target_pairs={{0,1},{1,0},{2,3},{3,2},{4,5},{5,4},{6,7},{7,6},{8,9},{9,8},{10,11... | collective-permute-start | bytes 589832 | tf_op jit(solution)/shard_map/ppermute | solution.py:353
  27.8 2.9 %collective-permute-start.11 = (bf16[64,1536]{1,0:T(8,128)(2,1)S(1)}, bf16[64,1536]{1,0:T(8,128)(2,1)S(1)}, u32[]{:S(2)}, u32[]{:S(2)}) collective-permute-start(bf16[64,1536]{1,0:T(8,128)(2,1)S(1)} %pass_on.8.after_ref.refs_5_), channel_id=1, source_target_pairs={{0,1},{1,0},{2,3},{3,2},{4,5},{5,4},{6,7},{7,6},{8,9},{9,8},{10,11... | collective-permute-start | bytes 589832 | tf_op jit(solution)/shard_map/ppermute | solution.py:353
  28.4 3.5 %collective-permute-start.9 = (bf16[64,1536]{1,0:T(8,128)(2,1)S(1)}, bf16[64,1536]{1,0:T(8,128)(2,1)S(1)}, u32[]{:S(2)}, u32[]{:S(2)}) collective-permute-start(bf16[64,1536]{1,0:T(8,128)(2,1)S(1)} %collective-permute-done.3.refs_3_), channel_id=1, source_target_pairs={{0,1},{1,0},{2,3},{3,2},{4,5},{5,4},{6,7},{7,6},{8,9},{9,8},{10,11... | collective-permute-start | bytes 589832 | tf_op jit(solution)/shard_map/ppermute | solution.py:353
  28.5 3.5 %collective-permute-start.10 = (bf16[64,1536]{1,0:T(8,128)(2,1)S(1)}, bf16[64,1536]{1,0:T(8,128)(2,1)S(1)}, u32[]{:S(2)}, u32[]{:S(2)}) collective-permute-start(bf16[64,1536]{1,0:T(8,128)(2,1)S(1)} %pass_on.9.refs_4_.refs_1_), channel_id=1, source_target_pairs={{0,1},{1,0},{2,3},{3,2},{4,5},{5,4},{6,7},{7,6},{8,9},{9,8},{10,11... | collective-permute-start | bytes 589832 | tf_op jit(solution)/shard_map/ppermute | solution.py:353
  28.9 8.6 %collective-permute-start.14 = (bf16[64,1536]{1,0:T(8,128)(2,1)S(1)}, bf16[64,1536]{1,0:T(8,128)(2,1)S(1)}, u32[]{:S(2)}, u32[]{:S(2)}) collective-permute-start(bf16[64,1536]{1,0:T(8,128)(2,1)S(1)} %collective-permute-done.6.refs_2_.refs_4_), channel_id=1, source_target_pairs={{0,1},{1,0},{2,3},{3,2},{4,5},{5,4},{6,7},{7,6},{8,9},{9,8},{10,11... | collective-permute-start | bytes 589832 | tf_op jit(solution)/shard_map/ppermute | solution.py:353
  29.1 9.9 %copy-start.2 = (bf16[1536]{0:T(1024)(128)(2,1)S(1)}, bf16[1536]{0:T(1024)(128)(2,1)}, u32[]{:S(2)}) copy-start(bf16[1536]{0:T(1024)(128)(2,1)} %refs_3_.1) | copy-start | bytes 9220
  29.1 7.2 %collective-permute-start.13 = (bf16[64,1536]{1,0:T(8,128)(2,1)S(1)}, bf16[64,1536]{1,0:T(8,128)(2,1)S(1)}, u32[]{:S(2)}, u32[]{:S(2)}) collective-permute-start(bf16[64,1536]{1,0:T(8,128)(2,1)S(1)} %pass_on.9.refs_4_.refs_1_), channel_id=1, source_target_pairs={{0,2},{1,3},{2,0},{3,1},{4,6},{5,7},{6,4},{7,5},{8,10},{9,11},{10,... | collective-permute-start | bytes 589832 | tf_op jit(solution)/shard_map/ppermute | solution.py:353
  30.7 6.9 %collective-permute-start.12 = (bf16[64,1536]{1,0:T(8,128)(2,1)S(1)}, bf16[64,1536]{1,0:T(8,128)(2,1)S(1)}, u32[]{:S(2)}, u32[]{:S(2)}) collective-permute-start(bf16[64,1536]{1,0:T(8,128)(2,1)S(1)} %pass_on.10), channel_id=1, source_target_pairs={{0,4},{4,0},{8,12},{12,8},{1,5},{5,1},{9,13},{13,9},{2,6},{6,2},{1... | collective-permute-start | bytes 589832 | tf_op jit(solution)/shard_map/ppermute | solution.py:353
  31.9 5.6 %collective-permute-start.17 = (bf16[64,1536]{1,0:T(8,128)(2,1)S(1)}, bf16[64,1536]{1,0:T(8,128)(2,1)S(1)}, u32[]{:S(2)}, u32[]{:S(2)}) collective-permute-start(bf16[64,1536]{1,0:T(8,128)(2,1)S(1)} %collective-permute-done.7.refs_3_.refs_7_), channel_id=1, source_target_pairs={{0,1},{1,0},{2,3},{3,2},{4,5},{5,4},{6,7},{7,6},{8,9},{9,8},{10,11... | collective-permute-start | bytes 589832 | tf_op jit(solution)/shard_map/ppermute | solution.py:353
  36.3 1.4 %collective-permute-start.16 = (bf16[64,1536]{1,0:T(8,128)(2,1)S(1)}, bf16[64,1536]{1,0:T(8,128)(2,1)S(1)}, u32[]{:S(2)}, u32[]{:S(2)}) collective-permute-start(bf16[64,1536]{1,0:T(8,128)(2,1)S(1)} %pass_on.12.refs_6_), channel_id=1, source_target_pairs={{0,1},{1,0},{2,3},{3,2},{4,5},{5,4},{6,7},{7,6},{8,9},{9,8},{10,11... | collective-permute-start | bytes 589832 | tf_op jit(solution)/shard_map/ppermute | solution.py:353
  37.6 1.4 %collective-permute-start.15 = (bf16[64,1536]{1,0:T(8,128)(2,1)S(1)}, bf16[64,1536]{1,0:T(8,128)(2,1)S(1)}, u32[]{:S(2)}, u32[]{:S(2)}) collective-permute-start(bf16[64,1536]{1,0:T(8,128)(2,1)S(1)} %pass_on.11.refs_5_), channel_id=1, source_target_pairs={{0,1},{1,0},{2,3},{3,2},{4,5},{5,4},{6,7},{7,6},{8,9},{9,8},{10,11... | collective-permute-start | bytes 589832 | tf_op jit(solution)/shard_map/ppermute | solution.py:353
  42.9 1.9 %collective-permute-start.18 = (bf16[64,1536]{1,0:T(8,128)(2,1)S(1)}, bf16[64,1536]{1,0:T(8,128)(2,1)S(1)}, u32[]{:S(2)}, u32[]{:S(2)}) collective-permute-start(bf16[64,1536]{1,0:T(8,128)(2,1)S(1)} %get-tuple-element.29), channel_id=1, source_target_pairs={{0,1},{1,0},{2,3},{3,2},{4,5},{5,4},{6,7},{7,6},{8,9},{9,8},{10,11... | collective-permute-start | bytes 589832 | tf_op jit(solution)/shard_map/ppermute | solution.py:353
  43.1 1.7 %collective-permute-start.19 = (bf16[64,1536]{1,0:T(8,128)(2,1)S(1)}, bf16[64,1536]{1,0:T(8,128)(2,1)S(1)}, u32[]{:S(2)}, u32[]{:S(2)}) collective-permute-start(bf16[64,1536]{1,0:T(8,128)(2,1)S(1)} %get-tuple-element.30), channel_id=1, source_target_pairs={{0,1},{1,0},{2,3},{3,2},{4,5},{5,4},{6,7},{7,6},{8,9},{9,8},{10,11... | collective-permute-start | bytes 589832 | tf_op jit(solution)/shard_map/ppermute | solution.py:353
  44.3 1.5 %collective-permute-start.20 = (bf16[64,1536]{1,0:T(8,128)(2,1)S(1)}, bf16[64,1536]{1,0:T(8,128)(2,1)S(1)}, u32[]{:S(2)}, u32[]{:S(2)}) collective-permute-start(bf16[64,1536]{1,0:T(8,128)(2,1)S(1)} %get-tuple-element.32), channel_id=1, source_target_pairs={{0,1},{1,0},{2,3},{3,2},{4,5},{5,4},{6,7},{7,6},{8,9},{9,8},{10,11... | collective-permute-start | bytes 589832 | tf_op jit(solution)/shard_map/ppermute | solution.py:353
  44.5 1.6 %collective-permute-start.21 = (bf16[64,1536]{1,0:T(8,128)(2,1)S(1)}, bf16[64,1536]{1,0:T(8,128)(2,1)S(1)}, u32[]{:S(2)}, u32[]{:S(2)}) collective-permute-start(bf16[64,1536]{1,0:T(8,128)(2,1)S(1)} %get-tuple-element.33), channel_id=1, source_target_pairs={{0,1},{1,0},{2,3},{3,2},{4,5},{5,4},{6,7},{7,6},{8,9},{9,8},{10,11... | collective-permute-start | bytes 589832 | tf_op jit(solution)/shard_map/ppermute | solution.py:353
  46.9 4.0 %collective-permute-start.24 = (bf16[64,1536]{1,0:T(8,128)(2,1)S(1)}, bf16[64,1536]{1,0:T(8,128)(2,1)S(1)}, u32[]{:S(2)}, u32[]{:S(2)}) collective-permute-start(bf16[64,1536]{1,0:T(8,128)(2,1)S(1)} %get-tuple-element.37), channel_id=1, source_target_pairs={{0,1},{1,0},{2,3},{3,2},{4,5},{5,4},{6,7},{7,6},{8,9},{9,8},{10,11... | collective-permute-start | bytes 589832 | tf_op jit(solution)/shard_map/ppermute | solution.py:353
  47.2 4.2 %collective-permute-start.25 = (bf16[64,1536]{1,0:T(8,128)(2,1)S(1)}, bf16[64,1536]{1,0:T(8,128)(2,1)S(1)}, u32[]{:S(2)}, u32[]{:S(2)}) collective-permute-start(bf16[64,1536]{1,0:T(8,128)(2,1)S(1)} %get-tuple-element.38), channel_id=1, source_target_pairs={{0,1},{1,0},{2,3},{3,2},{4,5},{5,4},{6,7},{7,6},{8,9},{9,8},{10,11... | collective-permute-start | bytes 589832 | tf_op jit(solution)/shard_map/ppermute | solution.py:353
  47.5 7.0 %collective-permute-start.26 = (bf16[64,1536]{1,0:T(8,128)(2,1)S(1)}, bf16[64,1536]{1,0:T(8,128)(2,1)S(1)}, u32[]{:S(2)}, u32[]{:S(2)}) collective-permute-start(bf16[64,1536]{1,0:T(8,128)(2,1)S(1)} %get-tuple-element.31.refs_1_), channel_id=1, source_target_pairs={{0,2},{1,3},{2,0},{3,1},{4,6},{5,7},{6,4},{7,5},{8,10},{9,11},{10,... | collective-permute-start | bytes 589832 | tf_op jit(solution)/shard_map/ppermute | solution.py:353
  48.9 7.4 %collective-permute-start.31 = (bf16[64,1536]{1,0:T(8,128)(2,1)S(1)}, bf16[64,1536]{1,0:T(8,128)(2,1)S(1)}, u32[]{:S(2)}, u32[]{:S(2)}) collective-permute-start(bf16[64,1536]{1,0:T(8,128)(2,1)S(1)} %get-tuple-element.44), channel_id=1, source_target_pairs={{0,4},{4,0},{8,12},{12,8},{1,5},{5,1},{9,13},{13,9},{2,6},{6,2},{1... | collective-permute-start | bytes 589832 | tf_op jit(solution)/shard_map/ppermute | solution.py:353
  50.8 7.0 %collective-permute-start.22 = (bf16[64,1536]{1,0:T(8,128)(2,1)S(1)}, bf16[64,1536]{1,0:T(8,128)(2,1)S(1)}, u32[]{:S(2)}, u32[]{:S(2)}) collective-permute-start(bf16[64,1536]{1,0:T(8,128)(2,1)S(1)} %get-tuple-element.34), channel_id=1, source_target_pairs={{0,1},{1,0},{2,3},{3,2},{4,5},{5,4},{6,7},{7,6},{8,9},{9,8},{10,11... | collective-permute-start | bytes 589832 | tf_op jit(solution)/shard_map/ppermute | solution.py:353
  50.9 6.9 %collective-permute-start.23 = (bf16[64,1536]{1,0:T(8,128)(2,1)S(1)}, bf16[64,1536]{1,0:T(8,128)(2,1)S(1)}, u32[]{:S(2)}, u32[]{:S(2)}) collective-permute-start(bf16[64,1536]{1,0:T(8,128)(2,1)S(1)} %get-tuple-element.35), channel_id=1, source_target_pairs={{0,1},{1,0},{2,3},{3,2},{4,5},{5,4},{6,7},{7,6},{8,9},{9,8},{10,11... | collective-permute-start | bytes 589832 | tf_op jit(solution)/shard_map/ppermute | solution.py:353
  54.5 7.2 %collective-permute-start.28 = (bf16[64,1536]{1,0:T(8,128)(2,1)S(1)}, bf16[64,1536]{1,0:T(8,128)(2,1)S(1)}, u32[]{:S(2)}, u32[]{:S(2)}) collective-permute-start(bf16[64,1536]{1,0:T(8,128)(2,1)S(1)} %add.3), channel_id=1, source_target_pairs={{0,4},{4,0},{8,12},{12,8},{1,5},{5,1},{9,13},{13,9},{2,6},{6,2},{1... | collective-permute-start | bytes 589832 | tf_op jit(solution)/shard_map/ppermute | solution.py:353
  55.6 7.8 %collective-permute-start.27 = (bf16[64,1536]{1,0:T(8,128)(2,1)S(1)}, bf16[64,1536]{1,0:T(8,128)(2,1)S(1)}, u32[]{:S(2)}, u32[]{:S(2)}) collective-permute-start(bf16[64,1536]{1,0:T(8,128)(2,1)S(1)} %pass_on.14), channel_id=1, source_target_pairs={{0,2},{1,3},{2,0},{3,1},{4,6},{5,7},{6,4},{7,5},{8,10},{9,11},{10,... | collective-permute-start | bytes 589832 | tf_op jit(solution)/shard_map/ppermute | solution.py:353
  56.3 14.8 %copy-start.1 = (f32[1536]{0:T(1024)S(1)}, f32[1536]{0:T(1024)}, u32[]{:S(2)}) copy-start(f32[1536]{0:T(1024)} %bias_ref.1) | copy-start | bytes 18436
  56.3 12.1 %collective-permute-start.32 = (bf16[64,1536]{1,0:T(8,128)(2,1)S(1)}, bf16[64,1536]{1,0:T(8,128)(2,1)S(1)}, u32[]{:S(2)}, u32[]{:S(2)}) collective-permute-start(bf16[64,1536]{1,0:T(8,128)(2,1)S(1)} %pass_on.15), channel_id=1, source_target_pairs={{0,2},{1,3},{2,0},{3,1},{4,6},{5,7},{6,4},{7,5},{8,10},{9,11},{10,... | collective-permute-start | bytes 589832 | tf_op jit(solution)/shard_map/ppermute | solution.py:353
  58.6 9.8 %collective-permute-start.30 = (bf16[64,1536]{1,0:T(8,128)(2,1)S(1)}, bf16[64,1536]{1,0:T(8,128)(2,1)S(1)}, u32[]{:S(2)}, u32[]{:S(2)}) collective-permute-start(bf16[64,1536]{1,0:T(8,128)(2,1)S(1)} %get-tuple-element.42), channel_id=1, source_target_pairs={{0,4},{4,0},{8,12},{12,8},{1,5},{5,1},{9,13},{13,9},{2,6},{6,2},{1... | collective-permute-start | bytes 589832 | tf_op jit(solution)/shard_map/ppermute | solution.py:353
  63.5 7.6 %collective-permute-start.29 = (bf16[64,1536]{1,0:T(8,128)(2,1)S(1)}, bf16[64,1536]{1,0:T(8,128)(2,1)S(1)}, u32[]{:S(2)}, u32[]{:S(2)}) collective-permute-start(bf16[64,1536]{1,0:T(8,128)(2,1)S(1)} %add.4), channel_id=1, source_target_pairs={{0,12},{4,8},{8,4},{12,0},{1,13},{5,9},{9,5},{13,1},{2,14},{6,10},... | collective-permute-start | bytes 589832 | tf_op jit(solution)/shard_map/ppermute | solution.py:353

commit v5 on v4

--- a/solution.py
+++ b/solution.py
@@ -419,9 +419,13 @@
         if y:
             for z in (1, half):
                 mine[z] = pass_on(mine[z], [running])
-        inputs = mine + [hop(b, "tensor", 1) for b in mine]
+        other = [hop(b, "tensor", 1) for b in mine]
         bias = expand_bias if y == last else None
-        running = expand(expand_weights, 2 * y, running, bias, inputs, groups)
+        if y:
+            running = expand(expand_weights, 2 * y, running, None, mine, groups)
+            running = expand(expand_weights, 2 * y + 1, running, bias, other, groups)
+        else:
+            running = expand(expand_weights, 0, running, bias, mine + other, groups)
 
     terms = {}
     parents = {p[:-1] for p in by_length}

time: 73.5 us -> 72.8 us (level)
  waiting for transfers between devices: 13.6 us -> 12.2 us
    ppermute x33, waiting for transfers between devices: 13.6 us -> 12.2 us  [hop(): lax.ppermute(array, axis, [(i, i ^ mask) for i in range(sizes[axis])])]
    pallas_call x2 -> x3, Pallas kernels: 5.75 us -> 5.97 us  [expand(): pl.pallas_call(functools.partial(expand_kernel, first, chunks, groups, la...]
  transfers between devices with their start and end apart: 33 -> 33, of which waited for: 10 -> 8; matrix products, arithmetic and copies ran while one was open for 0% -> 0% of each run, Pallas kernels for 34% -> 37%
where the time goes in v5:
time: 72.8 us; the launch traced here: 72.5 us
  Pallas kernels  34.7 us (48%)
  starting transfers between devices  25.4 us (35%)
  waiting for transfers between devices  12.2 us (17%)
    ppermute x33, starting transfers between devices, hop(): lax.ppermute(array, axis, [(i, i ^ mask) for i in range(sizes[axis])])  25.4 us
    pallas_call x3, Pallas kernels, load(): pl.pallas_call(functools.partial(load_kernel, tuple((part for _, part in...  14.1 us
    ppermute x33, waiting for transfers between devices, hop(): lax.ppermute(array, axis, [(i, i ^ mask) for i in range(sizes[axis])])  12.2 us
    pallas_call x8, Pallas kernels, reduce(): pl.pallas_call(functools.partial(reduce_kernel, groups, offsets[0], offse...  6.83 us
    pallas_call x3, Pallas kernels, expand(): pl.pallas_call(functools.partial(expand_kernel, first, chunks, groups, la...  5.97 us
    pallas_call x1, Pallas kernels, copy(): pl.pallas_call(copy_kernel, in_specs=[outside, pl.BlockSpec(memory_space=...  3.1 us
    pallas_call x1, Pallas kernels, body(): pl.pallas_call(gather_kernel, in_specs=[outside] * 3, out_specs=[whole, w...  2.27 us
    pallas_call x1, Pallas kernels, body(): pl.pallas_call(scatter_kernel, in_specs=[scalars, scalars, whole, whole,...  2.1 us
  transfers between devices with their start and end apart: 33, of which 8 were waited for; matrix products, arithmetic and copies ran while one was open for 0% of the time, Pallas kernels for 37%

profile of v5, /device:TPU:0, one launch (start us, length us, event | category | flops | bytes accessed | tf_op | source)
XLA Modules:
  0.0 72.5 jit_solution(12617645178090773919)
XLA Ops:
  0.0 2.3 %gather.1 = (f32[64,1536]{1,0:T(8,128)S(1)}, f32[64,128]{1,0:T(8,128)S(1)}) custom-call(s32[2]{0:T(128)} %counts_ref.1, s32[2,256]{1,0:T(2,128)} %ranking_ref.1, f32[2,256,1536]{2,1,0:T(8,128)} %patches_ref.3), custom_call_target="tpu_custom_call" | custom-call | tf_op jit(solution)/shard_map/gather/pallas_call | solution.py:355
  2.3 2.5 %collective-permute-start = (f32[64,128]{1,0:T(8,128)S(1)}, f32[64,128]{1,0:T(8,128)S(1)}, u32[]{:S(2)}, u32[]{:S(2)}) collective-permute-start(f32[64,128]{1,0:T(8,128)S(1)} %get-tuple-element.26.after_ref.refs_0_), channel_id=1, source_target_pairs={{0,3},{1,2},{2,1},{3,0},{4,7},{5,6},{6,5},{7,4},{8,11},{9,10},{10,... | collective-permute-start | bytes 98312 | tf_op jit(solution)/shard_map/ppermute | solution.py:353
  4.8 0.6 collective-permute-start.1
  5.4 3.8 %load.3.after_ref.refs_0_ = bf16[768,6144]{1,0:T(8,128)(2,1)S(1)} custom-call(f32[64,128]{1,0:T(8,128)S(1)} %get-tuple-element.26.after_ref.refs_0_, bf16[1536,6144]{1,0:T(8,128)(2,1)} %refs_0_.4), custom_call_target="tpu_custom_call" | custom-call | bytes 18874368 | tf_op jit(solution)/shard_map/load/pallas_call | solution.py:88
  9.3 0.2 norm.1.after_ref.refs_2_
  9.5 3.9 %collective-permute-start.4 = (bf16[64,1536]{1,0:T(8,128)(2,1)S(1)}, bf16[64,1536]{1,0:T(8,128)(2,1)S(1)}, u32[]{:S(2)}, u32[]{:S(2)}) collective-permute-start(bf16[64,1536]{1,0:T(8,128)(2,1)S(1)} %norm.1.after_ref.refs_2_), channel_id=1, source_target_pairs={{0,12},{4,8},{8,4},{12,0},{1,13},{5,9},{9,5},{13,1},{2,14},{6,10},... | collective-permute-start | bytes 589832 | tf_op jit(solution)/shard_map/ppermute | solution.py:353
  13.4 1.5 %collective-permute-start.6 = (bf16[64,1536]{1,0:T(8,128)(2,1)S(1)}, bf16[64,1536]{1,0:T(8,128)(2,1)S(1)}, u32[]{:S(2)}, u32[]{:S(2)}) collective-permute-start(bf16[64,1536]{1,0:T(8,128)(2,1)S(1)} %norm.1.after_ref.refs_2_), channel_id=1, source_target_pairs={{0,2},{1,3},{2,0},{3,1},{4,6},{5,7},{6,4},{7,5},{8,10},{9,11},{10,... | collective-permute-start | bytes 589832 | tf_op jit(solution)/shard_map/ppermute | solution.py:353
  14.9 6.5 %load.4 = (bf16[768,6144]{1,0:T(8,128)(2,1)S(1)}, bf16[768,6144]{1,0:T(8,128)(2,1)S(1)}) custom-call(bf16[64,1536]{1,0:T(8,128)(2,1)S(1)} %norm.1.after_ref.refs_2_, bf16[1536,6144]{1,0:T(8,128)(2,1)} %refs_0_.4, bf16[1536,6144]{1,0:T(8,128)(2,1)} %refs_0_.5), custom_call_target="tpu_custom_call" | custom-call | bytes 37748736 | tf_op jit(solution)/shard_map/load/pallas_call | solution.py:88
  21.4 0.6 collective-permute-start.7
  22.0 2.0 %collective-permute-start.5 = (bf16[64,1536]{1,0:T(8,128)(2,1)S(1)}, bf16[64,1536]{1,0:T(8,128)(2,1)S(1)}, u32[]{:S(2)}, u32[]{:S(2)}) collective-permute-start(bf16[64,1536]{1,0:T(8,128)(2,1)S(1)} %pass_on.8.after_ref.refs_5_), channel_id=1, source_target_pairs={{0,4},{4,0},{8,12},{12,8},{1,5},{5,1},{9,13},{13,9},{2,6},{6,2},{1... | collective-permute-start | bytes 589832 | tf_op jit(solution)/shard_map/ppermute | solution.py:353
  24.0 3.8 %load.5.refs_1_.refs_0_ = bf16[768,6144]{1,0:T(8,128)(2,1)S(1)} custom-call(bf16[64,1536]{1,0:T(8,128)(2,1)S(1)} %pass_on.8.after_ref.refs_5_, bf16[1536,6144]{1,0:T(8,128)(2,1)} %refs_0_.5), custom_call_target="tpu_custom_call" | custom-call | bytes 18874368 | tf_op jit(solution)/shard_map/load/pallas_call | solution.py:88
  27.8 0.6 collective-permute-start.11
  28.5 0.4 collective-permute-start.10
  28.9 0.2 collective-permute-start.14
  29.1 1.5 %collective-permute-start.13 = (bf16[64,1536]{1,0:T(8,128)(2,1)S(1)}, bf16[64,1536]{1,0:T(8,128)(2,1)S(1)}, u32[]{:S(2)}, u32[]{:S(2)}) collective-permute-start(bf16[64,1536]{1,0:T(8,128)(2,1)S(1)} %pass_on.9.refs_4_.refs_1_), channel_id=1, source_target_pairs={{0,2},{1,3},{2,0},{3,1},{4,6},{5,7},{6,4},{7,5},{8,10},{9,11},{10,... | collective-permute-start | bytes 589832 | tf_op jit(solution)/shard_map/ppermute | solution.py:353
  30.7 1.3 %collective-permute-start.12 = (bf16[64,1536]{1,0:T(8,128)(2,1)S(1)}, bf16[64,1536]{1,0:T(8,128)(2,1)S(1)}, u32[]{:S(2)}, u32[]{:S(2)}) collective-permute-start(bf16[64,1536]{1,0:T(8,128)(2,1)S(1)} %pass_on.10), channel_id=1, source_target_pairs={{0,4},{4,0},{8,12},{12,8},{1,5},{5,1},{9,13},{13,9},{2,6},{6,2},{1... | collective-permute-start | bytes 589832 | tf_op jit(solution)/shard_map/ppermute | solution.py:353
  32.0 2.6 %expand.3.refs_1_.refs_2_ = f32[256,1536]{1,0:T(8,128)S(1)} custom-call(bf16[768,6144]{1,0:T(8,128)(2,1)S(1)} %load.3.after_ref.refs_0_, bf16[768,6144]{1,0:T(8,128)(2,1)S(1)} %get-tuple-element.27.refs_1_, bf16[64,1536]{1,0:T(8,128)(2,1)S(1)} %norm.1.after_ref.refs_2_, bf16[64,1536]{1,0:T(8,128)(2,1)S(1)} %collective-permute-done.3.refs_3_, ...), custom_call_target="tpu_custom_call" | custom-call | flops 2415919104 | bytes 1572864 | tf_op jit(solution)/shard_map/expand/pallas_call | solution.py:216
  34.6 1.7 %collective-permute-done.13.refs_0_ = bf16[64,1536]{1,0:T(8,128)(2,1)S(1)} collective-permute-done((bf16[64,1536]{1,0:T(8,128)(2,1)S(1)}, bf16[64,1536]{1,0:T(8,128)(2,1)S(1)}, u32[]{:S(2)}, u32[]{:S(2)}) %collective-permute-start.13) | collective-permute-done | bytes 196640 | tf_op jit(solution)/shard_map/ppermute | solution.py:353
  36.3 1.2 %collective-permute-done.12.refs_0_ = bf16[64,1536]{1,0:T(8,128)(2,1)S(1)} collective-permute-done((bf16[64,1536]{1,0:T(8,128)(2,1)S(1)}, bf16[64,1536]{1,0:T(8,128)(2,1)S(1)}, u32[]{:S(2)}, u32[]{:S(2)}) %collective-permute-start.12) | collective-permute-done | bytes 196640 | tf_op jit(solution)/shard_map/ppermute | solution.py:353
  37.6 1.4 %expand.4.refs_2_ = f32[256,1536]{1,0:T(8,128)S(1)} custom-call(bf16[768,6144]{1,0:T(8,128)(2,1)S(1)} %load.3.after_ref.refs_0_, bf16[768,6144]{1,0:T(8,128)(2,1)S(1)} %get-tuple-element.27.refs_1_, f32[256,1536]{1,0:T(8,128)S(1)} %expand.3.refs_1_.refs_2_, bf16[64,1536]{1,0:T(8,128)(2,1)S(1)} %collective-permute-done.6.refs_2_.refs_3_, ...), custom_call_target="tpu_custom_call" | custom-call | flops 1207959552 | bytes 786432 | tf_op jit(solution)/shard_map/expand/pallas_call | solution.py:216
  39.1 1.9 %expand.5.hidden_ref.refs_0_ = bf16[256,1536]{1,0:T(8,128)(2,1)S(1)} custom-call(bf16[768,6144]{1,0:T(8,128)(2,1)S(1)} %load.3.after_ref.refs_0_, bf16[768,6144]{1,0:T(8,128)(2,1)S(1)} %get-tuple-element.27.refs_1_, f32[256,1536]{1,0:T(8,128)S(1)} %expand.4.refs_2_, bf16[1536]{0:T(1024)(128)(2,1)S(1)} %copy-done.2, ...), custom_call_target="tpu_custom_call" | custom-call | flops 1207959552 | bytes 786432 | tf_op jit(solution)/shard_map/expand/pallas_call | solution.py:216
  41.0 0.9 %reduce.8 = (bf16[64,1536]{1,0:T(8,128)(2,1)S(1)}, bf16[64,1536]{1,0:T(8,128)(2,1)S(1)}) custom-call(bf16[256,1536]{1,0:T(8,128)(2,1)S(1)} %expand.5.hidden_ref.refs_0_, bf16[768,6144]{1,0:T(8,128)(2,1)S(1)} %load.5.refs_1_.refs_0_, bf16[768,6144]{1,0:T(8,128)(2,1)S(1)} %get-tuple-element.28.refs_2_.refs_1_), custom_call_target="tpu_custom_call" | custom-call | flops 603979776 | bytes 393216 | tf_op jit(solution)/shard_map/reduce/pallas_call | solution.py:259
  41.8 0.6 collective-permute-start.18
  42.5 0.8 %reduce.10 = (bf16[64,1536]{1,0:T(8,128)(2,1)S(1)}, bf16[64,1536]{1,0:T(8,128)(2,1)S(1)}) custom-call(bf16[256,1536]{1,0:T(8,128)(2,1)S(1)} %expand.5.hidden_ref.refs_0_, bf16[768,6144]{1,0:T(8,128)(2,1)S(1)} %load.5.refs_1_.refs_0_, bf16[768,6144]{1,0:T(8,128)(2,1)S(1)} %get-tuple-element.28.refs_2_.refs_1_), custom_call_target="tpu_custom_call" | custom-call | flops 603979776 | bytes 393216 | tf_op jit(solution)/shard_map/reduce/pallas_call | solution.py:259
  43.3 0.5 collective-permute-start.20
  43.9 0.9 %reduce.9 = (bf16[64,1536]{1,0:T(8,128)(2,1)S(1)}, bf16[64,1536]{1,0:T(8,128)(2,1)S(1)}) custom-call(bf16[256,1536]{1,0:T(8,128)(2,1)S(1)} %expand.5.hidden_ref.refs_0_, bf16[768,6144]{1,0:T(8,128)(2,1)S(1)} %load.5.refs_1_.refs_0_, bf16[768,6144]{1,0:T(8,128)(2,1)S(1)} %get-tuple-element.28.refs_2_.refs_1_, ...), custom_call_target="tpu_custom_call" | custom-call | flops 603979776 | bytes 393216 | tf_op jit(solution)/shard_map/reduce/pallas_call | solution.py:259
  44.9 0.4 collective-permute-done.21.refs_5_.refs_3_
  45.3 0.8 %reduce.13 = (bf16[64,1536]{1,0:T(8,128)(2,1)S(1)}, bf16[64,1536]{1,0:T(8,128)(2,1)S(1)}) custom-call(bf16[256,1536]{1,0:T(8,128)(2,1)S(1)} %pass_on.13.hidden_ref, bf16[768,6144]{1,0:T(8,128)(2,1)S(1)} %load.5.refs_1_.refs_0_, bf16[768,6144]{1,0:T(8,128)(2,1)S(1)} %get-tuple-element.28.refs_2_.refs_1_), custom_call_target="tpu_custom_call" | custom-call | flops 603979776 | bytes 393216 | tf_op jit(solution)/shard_map/reduce/pallas_call | solution.py:259
  46.1 0.4 collective-permute-start.24
  46.5 0.2 collective-permute-start.25
  46.7 0.6 collective-permute-start.26
  47.3 0.9 %reduce.15 = (f32[64,1536]{1,0:T(8,128)S(1)}, bf16[64,1536]{1,0:T(8,128)(2,1)S(1)}) custom-call(bf16[256,1536]{1,0:T(8,128)(2,1)S(1)} %pass_on.13.hidden_ref, bf16[768,6144]{1,0:T(8,128)(2,1)S(1)} %load.5.refs_1_.refs_0_, bf16[768,6144]{1,0:T(8,128)(2,1)S(1)} %get-tuple-element.28.refs_2_.refs_1_, ...), custom_call_target="tpu_custom_call" | custom-call | flops 603979776 | bytes 393216 | tf_op jit(solution)/shard_map/reduce/pallas_call | solution.py:259
  48.2 1.1 %collective-permute-start.31 = (bf16[64,1536]{1,0:T(8,128)(2,1)S(1)}, bf16[64,1536]{1,0:T(8,128)(2,1)S(1)}, u32[]{:S(2)}, u32[]{:S(2)}) collective-permute-start(bf16[64,1536]{1,0:T(8,128)(2,1)S(1)} %get-tuple-element.44), channel_id=1, source_target_pairs={{0,4},{4,0},{8,12},{12,8},{1,5},{5,1},{9,13},{13,9},{2,6},{6,2},{1... | collective-permute-start | bytes 589832 | tf_op jit(solution)/shard_map/ppermute | solution.py:353
  49.3 0.8 %reduce.11 = (bf16[64,1536]{1,0:T(8,128)(2,1)S(1)}, bf16[64,1536]{1,0:T(8,128)(2,1)S(1)}) custom-call(bf16[256,1536]{1,0:T(8,128)(2,1)S(1)} %pass_on.13.hidden_ref, bf16[768,6144]{1,0:T(8,128)(2,1)S(1)} %load.5.refs_1_.refs_0_, bf16[768,6144]{1,0:T(8,128)(2,1)S(1)} %get-tuple-element.28.refs_2_.refs_1_), custom_call_target="tpu_custom_call" | custom-call | flops 603979776 | bytes 393216 | tf_op jit(solution)/shard_map/reduce/pallas_call | solution.py:259
  50.2 0.5 collective-permute-start.23
  50.7 0.9 %reduce.14 = (f32[64,1536]{1,0:T(8,128)S(1)}, f32[64,1536]{1,0:T(8,128)S(1)}) custom-call(bf16[256,1536]{1,0:T(8,128)(2,1)S(1)} %pass_on.13.hidden_ref, bf16[768,6144]{1,0:T(8,128)(2,1)S(1)} %load.5.refs_1_.refs_0_, bf16[768,6144]{1,0:T(8,128)(2,1)S(1)} %get-tuple-element.28.refs_2_.refs_1_, bf16[64,1536]{1,0:T(8,128)(2,1)S(1)} %collective-permute-done.24.refs_2_, ...), custom_call_target="tpu_custom_call" | custom-call | flops 603979776 | bytes 393216 | tf_op jit(solution)/shard_map/reduce/pallas_call | solution.py:259
  51.6 2.2 %collective-permute-done.26.refs_1_ = bf16[64,1536]{1,0:T(8,128)(2,1)S(1)} collective-permute-done((bf16[64,1536]{1,0:T(8,128)(2,1)S(1)}, bf16[64,1536]{1,0:T(8,128)(2,1)S(1)}, u32[]{:S(2)}, u32[]{:S(2)}) %collective-permute-start.26) | collective-permute-done | bytes 196640 | tf_op jit(solution)/shard_map/ppermute | solution.py:353
  53.8 1.0 %collective-permute-start.28 = (bf16[64,1536]{1,0:T(8,128)(2,1)S(1)}, bf16[64,1536]{1,0:T(8,128)(2,1)S(1)}, u32[]{:S(2)}, u32[]{:S(2)}) collective-permute-start(bf16[64,1536]{1,0:T(8,128)(2,1)S(1)} %add.3), channel_id=1, source_target_pairs={{0,4},{4,0},{8,12},{12,8},{1,5},{5,1},{9,13},{13,9},{2,6},{6,2},{1... | collective-permute-start | bytes 589832 | tf_op jit(solution)/shard_map/ppermute | solution.py:353
  54.9 0.6 collective-permute-start.27
  55.6 1.5 %collective-permute-start.32 = (bf16[64,1536]{1,0:T(8,128)(2,1)S(1)}, bf16[64,1536]{1,0:T(8,128)(2,1)S(1)}, u32[]{:S(2)}, u32[]{:S(2)}) collective-permute-start(bf16[64,1536]{1,0:T(8,128)(2,1)S(1)} %pass_on.15), channel_id=1, source_target_pairs={{0,2},{1,3},{2,0},{3,1},{4,6},{5,7},{6,4},{7,5},{8,10},{9,11},{10,... | collective-permute-start | bytes 589832 | tf_op jit(solution)/shard_map/ppermute | solution.py:353
  57.1 0.9 %reduce.12 = (f32[64,1536]{1,0:T(8,128)S(1)}, bf16[64,1536]{1,0:T(8,128)(2,1)S(1)}) custom-call(bf16[256,1536]{1,0:T(8,128)(2,1)S(1)} %pass_on.13.hidden_ref, bf16[768,6144]{1,0:T(8,128)(2,1)S(1)} %load.5.refs_1_.refs_0_, bf16[768,6144]{1,0:T(8,128)(2,1)S(1)} %get-tuple-element.28.refs_2_.refs_1_, bf16[64,1536]{1,0:T(8,128)(2,1)S(1)} %collective-permute-done.22.refs_2_, ...), custom_call_target="tpu_custom_call" | custom-call | flops 603979776 | bytes 393216 | tf_op jit(solution)/shard_map/reduce/pallas_call | solution.py:259
  57.9 1.1 %collective-permute-start.30 = (bf16[64,1536]{1,0:T(8,128)(2,1)S(1)}, bf16[64,1536]{1,0:T(8,128)(2,1)S(1)}, u32[]{:S(2)}, u32[]{:S(2)}) collective-permute-start(bf16[64,1536]{1,0:T(8,128)(2,1)S(1)} %get-tuple-element.42), channel_id=1, source_target_pairs={{0,4},{4,0},{8,12},{12,8},{1,5},{5,1},{9,13},{13,9},{2,6},{6,2},{1... | collective-permute-start | bytes 589832 | tf_op jit(solution)/shard_map/ppermute | solution.py:353
  59.0 2.1 %collective-permute-done.28.refs_2_ = bf16[64,1536]{1,0:T(8,128)(2,1)S(1)} collective-permute-done((bf16[64,1536]{1,0:T(8,128)(2,1)S(1)}, bf16[64,1536]{1,0:T(8,128)(2,1)S(1)}, u32[]{:S(2)}, u32[]{:S(2)}) %collective-permute-start.28) | collective-permute-done | bytes 196640 | tf_op jit(solution)/shard_map/ppermute | solution.py:353
  61.1 1.6 %collective-permute-done.27.refs_1_ = bf16[64,1536]{1,0:T(8,128)(2,1)S(1)} collective-permute-done((bf16[64,1536]{1,0:T(8,128)(2,1)S(1)}, bf16[64,1536]{1,0:T(8,128)(2,1)S(1)}, u32[]{:S(2)}, u32[]{:S(2)}) %collective-permute-start.27) | collective-permute-done | bytes 196640 | tf_op jit(solution)/shard_map/ppermute | solution.py:353
  62.8 1.8 %collective-permute-start.29 = (bf16[64,1536]{1,0:T(8,128)(2,1)S(1)}, bf16[64,1536]{1,0:T(8,128)(2,1)S(1)}, u32[]{:S(2)}, u32[]{:S(2)}) collective-permute-start(bf16[64,1536]{1,0:T(8,128)(2,1)S(1)} %add.4), channel_id=1, source_target_pairs={{0,12},{4,8},{8,4},{12,0},{1,13},{5,9},{9,5},{13,1},{2,14},{6,10},... | collective-permute-start | bytes 589832 | tf_op jit(solution)/shard_map/ppermute | solution.py:353
  64.6 3.1 %copy.28.patches_ref = f32[2,256,1536]{2,1,0:T(8,128)} custom-call(f32[2,256,1536]{2,1,0:T(8,128)} %patches_ref.3, f32[64,1536]{1,0:T(8,128)S(1)} %get-tuple-element.36.after_ref.own_ref), custom_call_target="tpu_custom_call" | custom-call | bytes 6291456 | tf_op jit(solution)/shard_map/copy/pallas_call | solution.py:120
  67.7 2.7 %collective-permute-done.29.refs_0_ = bf16[64,1536]{1,0:T(8,128)(2,1)S(1)} collective-permute-done((bf16[64,1536]{1,0:T(8,128)(2,1)S(1)}, bf16[64,1536]{1,0:T(8,128)(2,1)S(1)}, u32[]{:S(2)}, u32[]{:S(2)}) %collective-permute-start.29) | collective-permute-done | bytes 196640 | tf_op jit(solution)/shard_map/ppermute | solution.py:353
  70.4 2.1 %scatter.1 = f32[2,256,1536]{2,1,0:T(8,128)} custom-call(s32[2]{0:T(128)} %counts_ref.1, s32[2,256]{1,0:T(2,128)} %ranking_ref.1, f32[64,1536]{1,0:T(8,128)S(1)} %get-tuple-element.25.rows_ref, f32[1536]{0:T(1024)S(1)} %copy-done.1, f32[2,256,1536]{2,1,0:T(8,128)} %copy.28.patches_ref, ...), custom_call_target="tpu_custom_call", output_to_operand_aliasing={{}: (4, {})} | custom-call | tf_op jit(solution)/shard_map/scatter/pallas_call | solution.py:459
  (54 shorter events, 0.7 us)
Async XLA Ops:
  2.3 7.0 %copy-start = (f32[1536]{0:T(1024)S(1)}, f32[1536]{0:T(1024)}, u32[]{:S(2)}) copy-start(f32[1536]{0:T(1024)} %gain_ref.1) | copy-start | bytes 18436
  2.3 7.0 %collective-permute-start = (f32[64,128]{1,0:T(8,128)S(1)}, f32[64,128]{1,0:T(8,128)S(1)}, u32[]{:S(2)}, u32[]{:S(2)}) collective-permute-start(f32[64,128]{1,0:T(8,128)S(1)} %get-tuple-element.26.after_ref.refs_0_), channel_id=1, source_target_pairs={{0,3},{1,2},{2,1},{3,0},{4,7},{5,6},{6,5},{7,4},{8,11},{9,10},{10,... | collective-permute-start | bytes 98312 | tf_op jit(solution)/shard_map/ppermute | solution.py:353
  4.8 4.5 %collective-permute-start.1 = (f32[64,128]{1,0:T(8,128)S(1)}, f32[64,128]{1,0:T(8,128)S(1)}, u32[]{:S(2)}, u32[]{:S(2)}) collective-permute-start(f32[64,128]{1,0:T(8,128)S(1)} %get-tuple-element.26.after_ref.refs_0_), channel_id=1, source_target_pairs={{0,2},{1,3},{2,0},{3,1},{4,6},{5,7},{6,4},{7,5},{8,10},{9,11},{10,... | collective-permute-start | bytes 98312 | tf_op jit(solution)/shard_map/ppermute | solution.py:353
  5.4 3.9 %collective-permute-start.2 = (f32[64,128]{1,0:T(8,128)S(1)}, f32[64,128]{1,0:T(8,128)S(1)}, u32[]{:S(2)}, u32[]{:S(2)}) collective-permute-start(f32[64,128]{1,0:T(8,128)S(1)} %get-tuple-element.26.after_ref.refs_0_), channel_id=1, source_target_pairs={{0,1},{1,0},{2,3},{3,2},{4,5},{5,4},{6,7},{7,6},{8,9},{9,8},{10,11... | collective-permute-start | bytes 98312 | tf_op jit(solution)/shard_map/ppermute | solution.py:353
  9.5 11.9 %collective-permute-start.4 = (bf16[64,1536]{1,0:T(8,128)(2,1)S(1)}, bf16[64,1536]{1,0:T(8,128)(2,1)S(1)}, u32[]{:S(2)}, u32[]{:S(2)}) collective-permute-start(bf16[64,1536]{1,0:T(8,128)(2,1)S(1)} %norm.1.after_ref.refs_2_), channel_id=1, source_target_pairs={{0,12},{4,8},{8,4},{12,0},{1,13},{5,9},{9,5},{13,1},{2,14},{6,10},... | collective-permute-start | bytes 589832 | tf_op jit(solution)/shard_map/ppermute | solution.py:353
  13.4 14.4 %collective-permute-start.6 = (bf16[64,1536]{1,0:T(8,128)(2,1)S(1)}, bf16[64,1536]{1,0:T(8,128)(2,1)S(1)}, u32[]{:S(2)}, u32[]{:S(2)}) collective-permute-start(bf16[64,1536]{1,0:T(8,128)(2,1)S(1)} %norm.1.after_ref.refs_2_), channel_id=1, source_target_pairs={{0,2},{1,3},{2,0},{3,1},{4,6},{5,7},{6,4},{7,5},{8,10},{9,11},{10,... | collective-permute-start | bytes 589832 | tf_op jit(solution)/shard_map/ppermute | solution.py:353
  14.9 13.5 %collective-permute-start.3 = (bf16[64,1536]{1,0:T(8,128)(2,1)S(1)}, bf16[64,1536]{1,0:T(8,128)(2,1)S(1)}, u32[]{:S(2)}, u32[]{:S(2)}) collective-permute-start(bf16[64,1536]{1,0:T(8,128)(2,1)S(1)} %norm.1.after_ref.refs_2_), channel_id=1, source_target_pairs={{0,4},{4,0},{8,12},{12,8},{1,5},{5,1},{9,13},{13,9},{2,6},{6,2},{1... | collective-permute-start | bytes 589832 | tf_op jit(solution)/shard_map/ppermute | solution.py:353
  21.4 7.1 %collective-permute-start.7 = (bf16[64,1536]{1,0:T(8,128)(2,1)S(1)}, bf16[64,1536]{1,0:T(8,128)(2,1)S(1)}, u32[]{:S(2)}, u32[]{:S(2)}) collective-permute-start(bf16[64,1536]{1,0:T(8,128)(2,1)S(1)} %pass_on.8.after_ref.refs_5_), channel_id=1, source_target_pairs={{0,2},{1,3},{2,0},{3,1},{4,6},{5,7},{6,4},{7,5},{8,10},{9,11},{10,... | collective-permute-start | bytes 589832 | tf_op jit(solution)/shard_map/ppermute | solution.py:353
  22.0 6.5 %collective-permute-start.5 = (bf16[64,1536]{1,0:T(8,128)(2,1)S(1)}, bf16[64,1536]{1,0:T(8,128)(2,1)S(1)}, u32[]{:S(2)}, u32[]{:S(2)}) collective-permute-start(bf16[64,1536]{1,0:T(8,128)(2,1)S(1)} %pass_on.8.after_ref.refs_5_), channel_id=1, source_target_pairs={{0,4},{4,0},{8,12},{12,8},{1,5},{5,1},{9,13},{13,9},{2,6},{6,2},{1... | collective-permute-start | bytes 589832 | tf_op jit(solution)/shard_map/ppermute | solution.py:353
  24.0 5.1 %collective-permute-start.8 = (bf16[64,1536]{1,0:T(8,128)(2,1)S(1)}, bf16[64,1536]{1,0:T(8,128)(2,1)S(1)}, u32[]{:S(2)}, u32[]{:S(2)}) collective-permute-start(bf16[64,1536]{1,0:T(8,128)(2,1)S(1)} %norm.1.after_ref.refs_2_), channel_id=1, source_target_pairs={{0,1},{1,0},{2,3},{3,2},{4,5},{5,4},{6,7},{7,6},{8,9},{9,8},{10,11... | collective-permute-start | bytes 589832 | tf_op jit(solution)/shard_map/ppermute | solution.py:353
  27.8 2.9 %collective-permute-start.11 = (bf16[64,1536]{1,0:T(8,128)(2,1)S(1)}, bf16[64,1536]{1,0:T(8,128)(2,1)S(1)}, u32[]{:S(2)}, u32[]{:S(2)}) collective-permute-start(bf16[64,1536]{1,0:T(8,128)(2,1)S(1)} %pass_on.8.after_ref.refs_5_), channel_id=1, source_target_pairs={{0,1},{1,0},{2,3},{3,2},{4,5},{5,4},{6,7},{7,6},{8,9},{9,8},{10,11... | collective-permute-start | bytes 589832 | tf_op jit(solution)/shard_map/ppermute | solution.py:353
  28.4 3.5 %collective-permute-start.9 = (bf16[64,1536]{1,0:T(8,128)(2,1)S(1)}, bf16[64,1536]{1,0:T(8,128)(2,1)S(1)}, u32[]{:S(2)}, u32[]{:S(2)}) collective-permute-start(bf16[64,1536]{1,0:T(8,128)(2,1)S(1)} %collective-permute-done.3.refs_3_), channel_id=1, source_target_pairs={{0,1},{1,0},{2,3},{3,2},{4,5},{5,4},{6,7},{7,6},{8,9},{9,8},{10,11... | collective-permute-start | bytes 589832 | tf_op jit(solution)/shard_map/ppermute | solution.py:353
  28.5 3.5 %collective-permute-start.10 = (bf16[64,1536]{1,0:T(8,128)(2,1)S(1)}, bf16[64,1536]{1,0:T(8,128)(2,1)S(1)}, u32[]{:S(2)}, u32[]{:S(2)}) collective-permute-start(bf16[64,1536]{1,0:T(8,128)(2,1)S(1)} %pass_on.9.refs_4_.refs_1_), channel_id=1, source_target_pairs={{0,1},{1,0},{2,3},{3,2},{4,5},{5,4},{6,7},{7,6},{8,9},{9,8},{10,11... | collective-permute-start | bytes 589832 | tf_op jit(solution)/shard_map/ppermute | solution.py:353
  28.9 10.1 %collective-permute-start.14 = (bf16[64,1536]{1,0:T(8,128)(2,1)S(1)}, bf16[64,1536]{1,0:T(8,128)(2,1)S(1)}, u32[]{:S(2)}, u32[]{:S(2)}) collective-permute-start(bf16[64,1536]{1,0:T(8,128)(2,1)S(1)} %collective-permute-done.6.refs_2_.refs_3_), channel_id=1, source_target_pairs={{0,1},{1,0},{2,3},{3,2},{4,5},{5,4},{6,7},{7,6},{8,9},{9,8},{10,11... | collective-permute-start | bytes 589832 | tf_op jit(solution)/shard_map/ppermute | solution.py:353
  29.1 7.2 %collective-permute-start.13 = (bf16[64,1536]{1,0:T(8,128)(2,1)S(1)}, bf16[64,1536]{1,0:T(8,128)(2,1)S(1)}, u32[]{:S(2)}, u32[]{:S(2)}) collective-permute-start(bf16[64,1536]{1,0:T(8,128)(2,1)S(1)} %pass_on.9.refs_4_.refs_1_), channel_id=1, source_target_pairs={{0,2},{1,3},{2,0},{3,1},{4,6},{5,7},{6,4},{7,5},{8,10},{9,11},{10,... | collective-permute-start | bytes 589832 | tf_op jit(solution)/shard_map/ppermute | solution.py:353
  30.7 6.9 %collective-permute-start.12 = (bf16[64,1536]{1,0:T(8,128)(2,1)S(1)}, bf16[64,1536]{1,0:T(8,128)(2,1)S(1)}, u32[]{:S(2)}, u32[]{:S(2)}) collective-permute-start(bf16[64,1536]{1,0:T(8,128)(2,1)S(1)} %pass_on.10), channel_id=1, source_target_pairs={{0,4},{4,0},{8,12},{12,8},{1,5},{5,1},{9,13},{13,9},{2,6},{6,2},{1... | collective-permute-start | bytes 589832 | tf_op jit(solution)/shard_map/ppermute | solution.py:353
  31.9 7.1 %collective-permute-start.17 = (bf16[64,1536]{1,0:T(8,128)(2,1)S(1)}, bf16[64,1536]{1,0:T(8,128)(2,1)S(1)}, u32[]{:S(2)}, u32[]{:S(2)}) collective-permute-start(bf16[64,1536]{1,0:T(8,128)(2,1)S(1)} %collective-permute-done.7.refs_3_.refs_6_), channel_id=1, source_target_pairs={{0,1},{1,0},{2,3},{3,2},{4,5},{5,4},{6,7},{7,6},{8,9},{9,8},{10,11... | collective-permute-start | bytes 589832 | tf_op jit(solution)/shard_map/ppermute | solution.py:353
  36.3 2.7 %collective-permute-start.16 = (bf16[64,1536]{1,0:T(8,128)(2,1)S(1)}, bf16[64,1536]{1,0:T(8,128)(2,1)S(1)}, u32[]{:S(2)}, u32[]{:S(2)}) collective-permute-start(bf16[64,1536]{1,0:T(8,128)(2,1)S(1)} %pass_on.12.refs_5_), channel_id=1, source_target_pairs={{0,1},{1,0},{2,3},{3,2},{4,5},{5,4},{6,7},{7,6},{8,9},{9,8},{10,11... | collective-permute-start | bytes 589832 | tf_op jit(solution)/shard_map/ppermute | solution.py:353
  37.6 1.5 %copy-start.2 = (bf16[1536]{0:T(1024)(128)(2,1)S(1)}, bf16[1536]{0:T(1024)(128)(2,1)}, u32[]{:S(2)}) copy-start(bf16[1536]{0:T(1024)(128)(2,1)} %refs_3_.1) | copy-start | bytes 9220
  37.6 1.5 %collective-permute-start.15 = (bf16[64,1536]{1,0:T(8,128)(2,1)S(1)}, bf16[64,1536]{1,0:T(8,128)(2,1)S(1)}, u32[]{:S(2)}, u32[]{:S(2)}) collective-permute-start(bf16[64,1536]{1,0:T(8,128)(2,1)S(1)} %pass_on.11.refs_4_), channel_id=1, source_target_pairs={{0,1},{1,0},{2,3},{3,2},{4,5},{5,4},{6,7},{7,6},{8,9},{9,8},{10,11... | collective-permute-start | bytes 589832 | tf_op jit(solution)/shard_map/ppermute | solution.py:353
  41.8 2.1 %collective-permute-start.18 = (bf16[64,1536]{1,0:T(8,128)(2,1)S(1)}, bf16[64,1536]{1,0:T(8,128)(2,1)S(1)}, u32[]{:S(2)}, u32[]{:S(2)}) collective-permute-start(bf16[64,1536]{1,0:T(8,128)(2,1)S(1)} %get-tuple-element.29), channel_id=1, source_target_pairs={{0,1},{1,0},{2,3},{3,2},{4,5},{5,4},{6,7},{7,6},{8,9},{9,8},{10,11... | collective-permute-start | bytes 589832 | tf_op jit(solution)/shard_map/ppermute | solution.py:353
  42.4 1.5 %collective-permute-start.19 = (bf16[64,1536]{1,0:T(8,128)(2,1)S(1)}, bf16[64,1536]{1,0:T(8,128)(2,1)S(1)}, u32[]{:S(2)}, u32[]{:S(2)}) collective-permute-start(bf16[64,1536]{1,0:T(8,128)(2,1)S(1)} %get-tuple-element.30), channel_id=1, source_target_pairs={{0,1},{1,0},{2,3},{3,2},{4,5},{5,4},{6,7},{7,6},{8,9},{9,8},{10,11... | collective-permute-start | bytes 589832 | tf_op jit(solution)/shard_map/ppermute | solution.py:353
  43.3 1.6 %collective-permute-start.20 = (bf16[64,1536]{1,0:T(8,128)(2,1)S(1)}, bf16[64,1536]{1,0:T(8,128)(2,1)S(1)}, u32[]{:S(2)}, u32[]{:S(2)}) collective-permute-start(bf16[64,1536]{1,0:T(8,128)(2,1)S(1)} %get-tuple-element.32), channel_id=1, source_target_pairs={{0,1},{1,0},{2,3},{3,2},{4,5},{5,4},{6,7},{7,6},{8,9},{9,8},{10,11... | collective-permute-start | bytes 589832 | tf_op jit(solution)/shard_map/ppermute | solution.py:353
  43.8 1.4 %collective-permute-start.21 = (bf16[64,1536]{1,0:T(8,128)(2,1)S(1)}, bf16[64,1536]{1,0:T(8,128)(2,1)S(1)}, u32[]{:S(2)}, u32[]{:S(2)}) collective-permute-start(bf16[64,1536]{1,0:T(8,128)(2,1)S(1)} %get-tuple-element.33), channel_id=1, source_target_pairs={{0,1},{1,0},{2,3},{3,2},{4,5},{5,4},{6,7},{7,6},{8,9},{9,8},{10,11... | collective-permute-start | bytes 589832 | tf_op jit(solution)/shard_map/ppermute | solution.py:353
  46.1 4.1 %collective-permute-start.24 = (bf16[64,1536]{1,0:T(8,128)(2,1)S(1)}, bf16[64,1536]{1,0:T(8,128)(2,1)S(1)}, u32[]{:S(2)}, u32[]{:S(2)}) collective-permute-start(bf16[64,1536]{1,0:T(8,128)(2,1)S(1)} %get-tuple-element.37), channel_id=1, source_target_pairs={{0,1},{1,0},{2,3},{3,2},{4,5},{5,4},{6,7},{7,6},{8,9},{9,8},{10,11... | collective-permute-start | bytes 589832 | tf_op jit(solution)/shard_map/ppermute | solution.py:353
  46.5 4.2 %collective-permute-start.25 = (bf16[64,1536]{1,0:T(8,128)(2,1)S(1)}, bf16[64,1536]{1,0:T(8,128)(2,1)S(1)}, u32[]{:S(2)}, u32[]{:S(2)}) collective-permute-start(bf16[64,1536]{1,0:T(8,128)(2,1)S(1)} %get-tuple-element.38), channel_id=1, source_target_pairs={{0,1},{1,0},{2,3},{3,2},{4,5},{5,4},{6,7},{7,6},{8,9},{9,8},{10,11... | collective-permute-start | bytes 589832 | tf_op jit(solution)/shard_map/ppermute | solution.py:353
  46.7 7.1 %collective-permute-start.26 = (bf16[64,1536]{1,0:T(8,128)(2,1)S(1)}, bf16[64,1536]{1,0:T(8,128)(2,1)S(1)}, u32[]{:S(2)}, u32[]{:S(2)}) collective-permute-start(bf16[64,1536]{1,0:T(8,128)(2,1)S(1)} %get-tuple-element.31.refs_1_), channel_id=1, source_target_pairs={{0,2},{1,3},{2,0},{3,1},{4,6},{5,7},{6,4},{7,5},{8,10},{9,11},{10,... | collective-permute-start | bytes 589832 | tf_op jit(solution)/shard_map/ppermute | solution.py:353
  48.2 7.4 %collective-permute-start.31 = (bf16[64,1536]{1,0:T(8,128)(2,1)S(1)}, bf16[64,1536]{1,0:T(8,128)(2,1)S(1)}, u32[]{:S(2)}, u32[]{:S(2)}) collective-permute-start(bf16[64,1536]{1,0:T(8,128)(2,1)S(1)} %get-tuple-element.44), channel_id=1, source_target_pairs={{0,4},{4,0},{8,12},{12,8},{1,5},{5,1},{9,13},{13,9},{2,6},{6,2},{1... | collective-permute-start | bytes 589832 | tf_op jit(solution)/shard_map/ppermute | solution.py:353
  50.1 6.9 %collective-permute-start.22 = (bf16[64,1536]{1,0:T(8,128)(2,1)S(1)}, bf16[64,1536]{1,0:T(8,128)(2,1)S(1)}, u32[]{:S(2)}, u32[]{:S(2)}) collective-permute-start(bf16[64,1536]{1,0:T(8,128)(2,1)S(1)} %get-tuple-element.34), channel_id=1, source_target_pairs={{0,1},{1,0},{2,3},{3,2},{4,5},{5,4},{6,7},{7,6},{8,9},{9,8},{10,11... | collective-permute-start | bytes 589832 | tf_op jit(solution)/shard_map/ppermute | solution.py:353
  50.2 6.8 %collective-permute-start.23 = (bf16[64,1536]{1,0:T(8,128)(2,1)S(1)}, bf16[64,1536]{1,0:T(8,128)(2,1)S(1)}, u32[]{:S(2)}, u32[]{:S(2)}) collective-permute-start(bf16[64,1536]{1,0:T(8,128)(2,1)S(1)} %get-tuple-element.35), channel_id=1, source_target_pairs={{0,1},{1,0},{2,3},{3,2},{4,5},{5,4},{6,7},{7,6},{8,9},{9,8},{10,11... | collective-permute-start | bytes 589832 | tf_op jit(solution)/shard_map/ppermute | solution.py:353
  53.8 7.3 %collective-permute-start.28 = (bf16[64,1536]{1,0:T(8,128)(2,1)S(1)}, bf16[64,1536]{1,0:T(8,128)(2,1)S(1)}, u32[]{:S(2)}, u32[]{:S(2)}) collective-permute-start(bf16[64,1536]{1,0:T(8,128)(2,1)S(1)} %add.3), channel_id=1, source_target_pairs={{0,4},{4,0},{8,12},{12,8},{1,5},{5,1},{9,13},{13,9},{2,6},{6,2},{1... | collective-permute-start | bytes 589832 | tf_op jit(solution)/shard_map/ppermute | solution.py:353
  54.9 7.8 %collective-permute-start.27 = (bf16[64,1536]{1,0:T(8,128)(2,1)S(1)}, bf16[64,1536]{1,0:T(8,128)(2,1)S(1)}, u32[]{:S(2)}, u32[]{:S(2)}) collective-permute-start(bf16[64,1536]{1,0:T(8,128)(2,1)S(1)} %pass_on.14), channel_id=1, source_target_pairs={{0,2},{1,3},{2,0},{3,1},{4,6},{5,7},{6,4},{7,5},{8,10},{9,11},{10,... | collective-permute-start | bytes 589832 | tf_op jit(solution)/shard_map/ppermute | solution.py:353
  55.6 14.9 %copy-start.1 = (f32[1536]{0:T(1024)S(1)}, f32[1536]{0:T(1024)}, u32[]{:S(2)}) copy-start(f32[1536]{0:T(1024)} %bias_ref.1) | copy-start | bytes 18436
  55.6 12.1 %collective-permute-start.32 = (bf16[64,1536]{1,0:T(8,128)(2,1)S(1)}, bf16[64,1536]{1,0:T(8,128)(2,1)S(1)}, u32[]{:S(2)}, u32[]{:S(2)}) collective-permute-start(bf16[64,1536]{1,0:T(8,128)(2,1)S(1)} %pass_on.15), channel_id=1, source_target_pairs={{0,2},{1,3},{2,0},{3,1},{4,6},{5,7},{6,4},{7,5},{8,10},{9,11},{10,... | collective-permute-start | bytes 589832 | tf_op jit(solution)/shard_map/ppermute | solution.py:353
  57.9 9.8 %collective-permute-start.30 = (bf16[64,1536]{1,0:T(8,128)(2,1)S(1)}, bf16[64,1536]{1,0:T(8,128)(2,1)S(1)}, u32[]{:S(2)}, u32[]{:S(2)}) collective-permute-start(bf16[64,1536]{1,0:T(8,128)(2,1)S(1)} %get-tuple-element.42), channel_id=1, source_target_pairs={{0,4},{4,0},{8,12},{12,8},{1,5},{5,1},{9,13},{13,9},{2,6},{6,2},{1... | collective-permute-start | bytes 589832 | tf_op jit(solution)/shard_map/ppermute | solution.py:353
  62.8 7.6 %collective-permute-start.29 = (bf16[64,1536]{1,0:T(8,128)(2,1)S(1)}, bf16[64,1536]{1,0:T(8,128)(2,1)S(1)}, u32[]{:S(2)}, u32[]{:S(2)}) collective-permute-start(bf16[64,1536]{1,0:T(8,128)(2,1)S(1)} %add.4), channel_id=1, source_target_pairs={{0,12},{4,8},{8,4},{12,0},{1,13},{5,9},{9,5},{13,1},{2,14},{6,10},... | collective-permute-start | bytes 589832 | tf_op jit(solution)/shard_map/ppermute | solution.py:353
